TPU v7x, 128 devices: a whole 4x4x4 slice. The times are simulated.
128 devices in a mesh: sfc: 128 (over z, x, y, core).
Axes of the slice: x: 4, y: 4, z: 4, core: 2. Of those that a mesh axis runs over, the one named last changes fastest.
Arguments:
- tracers: float32 [8192, 16, 512], P('sfc'), may hold values from 0 to 2
- velocity: float32 [8192, 16, 128], P('sfc'), may hold values from -4 to 4
- jacobian: float32 [8192, 16], P('sfc'), may hold values from 0.5 to 2
- elem_nodes: int32 [8192, 16], P('sfc'), may hold values from 0 to 624, as said below
Outputs:
- tracers_out: float32 [8192, 16, 512], P('sfc')
Inputs may be any that keep to these rules, and one draw needn't show every extreme that they name: `elem_nodes`: the 64 elements of each block of 64 consecutive rows are those of a square of the element grid, listed in some order: the element at column ex and row ey of the square has, at GLL point 4 j + i, the local node (3 ey + j) * 25 + 3 ex + i.
All inputs are finite; a program needn't handle non-finite values.
Results may differ from a plain program's by a relative error of at most 0.0003.
Values sent between devices are 32-bit elements; how exact they have to be, the bound alone decides.
No kernel may reach another device: no remote copies, remote signals or barrier semaphores. Data moves between devices by JAX's collectives and lax.ppermute only.
A program may use at most 128 MiB of HBM per device.

v0:
```python
import jax
import jax.numpy as jnp
import numpy as np
from jax import lax
from jax.sharding import PartitionSpec as P

TT = 8
PX = 8
Q = 8


HIGHEST = lax.Precision.HIGHEST
STEP_SIZE = 0.04
DIFFUSION = 0.0001


def from_behind(block, axis, distance):
    devices = range(lax.axis_size(axis))
    route = [((i - distance) % len(devices), i) for i in devices]
    return lax.ppermute(block, axis, route)


def padded(value, sides, width):
    for axis, dim in sides:
        peers, length = (lax.axis_size(axis), value.shape[dim])
        up = [(i, (i + 1) % peers) for i in range(peers)]
        down = [(j, i) for i, j in up]
        last = lax.slice_in_dim(value, length - width, length, axis=dim)
        initial = lax.slice_in_dim(value, 0, width, axis=dim)
        before = lax.ppermute(last, axis, up)
        after = lax.ppermute(initial, axis, down)
        value = jnp.concatenate([before, value, after], axis=dim)
    return value


def gll_tables():
    points = np.array([-1.0, -np.sqrt(0.2), np.sqrt(0.2), 1.0])
    weights = np.array([1.0, 5.0, 5.0, 1.0]) / 6.0
    barycentric = np.array(
        [
            1.0
            / np.prod(
                [points[target] - points[partner] for partner in range(4) if partner != target]
            )
            for target in range(4)
        ]
    )
    deriv = np.zeros((4, 4))
    for row_index in range(4):
        for col_index in range(4):
            if row_index != col_index:
                deriv[row_index, col_index] = (
                    barycentric[col_index]
                    / barycentric[row_index]
                    / (points[row_index] - points[col_index])
                )
        deriv[row_index, row_index] = -np.sum(deriv[row_index])
    return (
        jnp.asarray(deriv, jnp.float32),
        jnp.asarray(np.outer(weights, weights).reshape(16), jnp.float32),
    )


def along_xi(deriv, field):
    shaped = field.reshape(field.shape[0], 4, 4, field.shape[2])
    return jnp.einsum("ai,ejiw->ejaw", deriv, shaped, precision=HIGHEST).reshape(field.shape)


def along_eta(deriv, field):
    shaped = field.reshape(field.shape[0], 4, 4, field.shape[2])
    return jnp.einsum("aj,ejiw->eaiw", deriv, shaped, precision=HIGHEST).reshape(field.shape)


def tendency(deriv, field, wind_xi, wind_eta, metric):
    return (
        -(along_xi(deriv, metric * wind_xi * field) + along_eta(deriv, metric * wind_eta * field))
        / metric
    )


def laplace(deriv, field, metric):
    return (
        along_xi(deriv, metric * along_xi(deriv, field))
        + along_eta(deriv, metric * along_eta(deriv, field))
    ) / metric


def limit(values, mass):
    weight = mass[:, :, None]
    element_mean = jnp.sum(weight * values, axis=1, keepdims=True) / jnp.sum(
        weight, axis=1, keepdims=True
    )
    lowest = jnp.min(values, axis=1, keepdims=True)
    positive = jnp.maximum(element_mean, 0.0)
    negative = lowest < 0.0
    denominator = jnp.where(negative, positive - lowest, 1.0)
    scaling = jnp.where(negative, positive / denominator, 1.0)
    return element_mean + scaling * (values - element_mean)


def send_corner(values, offset):
    return from_behind(values, "sfc", offset)


def add_corners(sums, result, side):
    last = side - 1
    result = result.at[0, 0].add(send_corner(sums[last, last], PX + 1))
    result = result.at[0, last].add(send_corner(sums[last, 0], PX - 1))
    result = result.at[last, 0].add(send_corner(sums[0, last], -PX + 1))
    return result.at[last, last].add(send_corner(sums[0, 0], -PX - 1))


def combine_shared(sums, side):
    edges = jnp.stack([sums[:, 0], sums[:, side - 1]])
    beside_all = padded(edges, (("sfc", 0),), 1)
    columns = sums.at[:, 0].add(beside_all[0]).at[:, side - 1].add(beside_all[3])
    from_north = from_behind(sums[0], "sfc", -PX)
    from_south = from_behind(sums[side - 1], "sfc", PX)
    result = columns.at[side - 1].add(from_north).at[0].add(from_south)
    result = add_corners(sums, result, side)
    return result


def per_device(tracers, velocity, jacobian, elem_nodes):
    deriv, node_weights = gll_tables()
    side = 3 * TT + 1
    width = tracers.shape[2]
    mass = jacobian * node_weights
    flat_nodes = elem_nodes.reshape(-1)
    local_mass = jax.ops.segment_sum(
        mass.reshape(-1, 1), flat_nodes, num_segments=side * side
    ).reshape(side, side, 1)
    mass_sums = combine_shared(local_mass, side)

    def average(field):
        sums = jax.ops.segment_sum(
            (mass[:, :, None] * field).reshape(-1, width), flat_nodes, num_segments=side * side
        )
        combined = combine_shared(sums.reshape(side, side, width), side) / mass_sums
        return combined.reshape(side * side, width)[flat_nodes].reshape(field.shape)

    levels = velocity.shape[2] // 2
    wind_xi = jnp.tile(velocity[:, :, :levels], (1, 1, Q))
    wind_eta = jnp.tile(velocity[:, :, levels:], (1, 1, Q))
    metric = jacobian[:, :, None]
    section_one = average(
        limit(tracers + STEP_SIZE * tendency(deriv, tracers, wind_xi, wind_eta, metric), mass)
    )
    section_two = average(
        limit(
            0.75 * tracers
            + 0.25
            * (section_one + STEP_SIZE * tendency(deriv, section_one, wind_xi, wind_eta, metric)),
            mass,
        )
    )
    section_three = average(
        limit(
            tracers / 3.0
            + 2.0
            / 3.0
            * (section_two + STEP_SIZE * tendency(deriv, section_two, wind_xi, wind_eta, metric)),
            mass,
        )
    )
    lap_one = average(laplace(deriv, section_three, metric))
    lap_two = average(laplace(deriv, lap_one, metric))
    return section_three - DIFFUSION * lap_two


def solution(mesh):
    in_specs = (P("sfc", None, None), P("sfc", None, None), P("sfc", None), P("sfc", None))
    out_specs = P("sfc", None, None)
    return jax.shard_map(
        per_device, mesh=mesh, in_specs=in_specs, out_specs=out_specs, check_vma=False
    )
```

profile of v0, /device:TPU:0, one launch (start us, length us, event | category | flops | bytes accessed | tf_op | source)
XLA Modules:
  0.0 504.2 jit_solution(13864215175022826652)
XLA Ops:
  1.8 7.6 %scatter_custom_fusion.1 = f32[625]{0:T(1024)S(1)} fusion(s32[1024]{0:T(1024)S(1)} %reshape.1858, f32[1024]{0:T(1024)S(1)} %reshape.1844, f32[]{:T(128)} %constant.1059.clone.1), kind=kCustom, calls=%fused_computation.167 | custom fusion | flops 1024 | bytes 2504 | tf_op jit(solution)/shard_map/scatter-add | solution.py:130
  30.3 5.0 tile.27
  52.9 6.9 %fusion.8 = (f32[64,16,512]{2,1,0:T(8,128)}, f32[64,16,512]{2,1,0:T(8,128)}) fusion(f32[64,16,512]{2,1,0:T(8,128)S(1)} %copy-done, f32[64,16,512]{2,0,1:T(8,128)} %reshape.1891, f32[64,16]{1,0:T(8,128)S(1)} %copy.120, f32[64,16,512]{2,0,1:T(8,128)} %reshape.1892), kind=kLoop, calls=%fused_computation.28 | loop fusion | flops 2097152 | bytes 10489856 | tf_op jit(solution)/shard_map/mul | solution.py:76
  65.5 5.8 %fusion.25 = f32[64,4,512,4]{2,3,1,0:T(4,128)S(1)} fusion(f32[4,4,1,1]{1,0,3,2:T(4,128)S(1)} %copy-done.6, f32[64,4,4,512]{3,2,1,0:T(4,128)} %reshape.1719), kind=kOutput, calls=%fused_computation.45 | convolution fusion | flops 25165824 | bytes 4194368 | tf_op jit(solution)/shard_map/aj,ejiw->eaiw/dot_general | solution.py:71
  71.4 5.8 %fusion.6 = f32[64,4,4,512]{3,2,1,0:T(4,128)} fusion(f32[64,4,512,4]{2,3,1,0:T(4,128)S(1)} %fusion.25, f32[64,4,4,512]{3,2,1,0:T(4,128)S(1)} %copy-done.3, f32[4,4,1,1]{1,0,3,2:T(4,128)S(1)} %copy-done.6), kind=kOutput, calls=%fused_computation.24 | convolution fusion | flops 26214400 | bytes 6291520 | tf_op jit(solution)/shard_map/ai,ejiw->ejaw/dot_general | solution.py:66
  84.6 7.5 %scatter_custom_fusion = f32[625,512]{1,0:T(8,128)S(1)} fusion(s32[1024]{0:T(1024)S(1)} %reshape.1858, f32[1024,512]{1,0:T(8,128)} %bitcast.222, f32[]{:T(128)} %constant.1059.clone.1), kind=kCustom, calls=%fused_computation.86 | custom fusion | flops 524288 | bytes 1280512 | tf_op jit(solution)/shard_map/scatter-add | solution.py:136
  100.3 7.7 %collective-permute-done.8 = f32[1,25,1]{1,2,0:T(1,128)S(1)} collective-permute-done((f32[1,25,1]{1,2,0:T(1,128)}, f32[1,25,1]{1,2,0:T(1,128)S(1)}, u32[]{:S(2)}, u32[]{:S(2)}) %collective-permute-start.8) | collective-permute-done | bytes 132 | tf_op jit(solution)/shard_map/ppermute | solution.py:30
  110.1 7.2 %collective-permute-done.12 = f32[1]{0:T(128)} collective-permute-done((f32[1]{0:T(128)}, f32[1]{0:T(128)}, u32[]{:S(2)}, u32[]{:S(2)}) %collective-permute-start.12) | collective-permute-done | bytes 36 | tf_op jit(solution)/shard_map/ppermute | solution.py:20
  118.0 5.4 %collective-permute-start.2 = (f32[25,512]{1,0:T(8,128)}, f32[25,512]{1,0:T(8,128)S(1)}, u32[]{:S(2)}, u32[]{:S(2)}) collective-permute-start(f32[25,512]{1,0:T(8,128)} %get-tuple-element.653), channel_id=1, source_target_pairs={{8,0},{9,1},{10,2},{11,3},{12,4},{13,5},{14,6},{15,7},{16,8},{17,9... | collective-permute-start | bytes 153608 | tf_op jit(solution)/shard_map/ppermute | solution.py:20
  148.5 5.6 %collective-permute-done.4 = f32[512]{0:T(512)S(1)} collective-permute-done((f32[512]{0:T(512)S(1)}, f32[512]{0:T(512)S(1)}, u32[]{:S(2)}, u32[]{:S(2)}) %collective-permute-start.4) | collective-permute-done | bytes 2080 | tf_op jit(solution)/shard_map/ppermute | solution.py:20
  185.8 6.2 %fusion.5 = f32[64,4,4,512]{3,2,1,0:T(4,128)} fusion(f32[64,4,512,4]{2,3,1,0:T(4,128)S(1)} %fusion.21, f32[4,4,1,1]{1,0,3,2:T(4,128)S(1)} %copy-done.6, f32[64,4,4,512]{3,0,2,1:T(8,128)S(1)} %get-tuple-element.612), kind=kOutput, calls=%fused_computation.22 | convolution fusion | flops 26214400 | bytes 6291520 | tf_op jit(solution)/shard_map/ai,ejiw->ejaw/dot_general | solution.py:66
  200.2 7.8 %scatter_custom_fusion.2 = f32[625,512]{1,0:T(8,128)S(1)} fusion(s32[1024]{0:T(1024)} %copy-done.14, f32[1024,512]{1,0:T(8,128)} %bitcast.223, f32[]{:T(128)} %constant.1059.clone.1), kind=kCustom, calls=%fused_computation.84 | custom fusion | flops 524288 | bytes 1280512 | tf_op jit(solution)/shard_map/scatter-add | solution.py:136
  233.3 5.4 %collective-permute-done.20 = f32[512]{0:T(512)S(1)} collective-permute-done((f32[512]{0:T(512)S(1)}, f32[512]{0:T(512)S(1)}, u32[]{:S(2)}, u32[]{:S(2)}) %collective-permute-start.20) | collective-permute-done | bytes 2080 | tf_op jit(solution)/shard_map/ppermute | solution.py:20
  270.6 6.2 %fusion.4 = f32[64,4,4,512]{3,2,1,0:T(4,128)} fusion(f32[64,4,512,4]{2,3,1,0:T(4,128)S(1)} %fusion.17, f32[4,4,1,1]{1,0,3,2:T(4,128)S(1)} %copy-done.6, f32[64,4,4,512]{3,0,2,1:T(8,128)S(1)} %get-tuple-element.610), kind=kOutput, calls=%fused_computation.20 | convolution fusion | flops 26214400 | bytes 6291520 | tf_op jit(solution)/shard_map/ai,ejiw->ejaw/dot_general | solution.py:66
  285.0 8.0 %scatter_custom_fusion.3 = f32[625,512]{1,0:T(8,128)S(1)} fusion(s32[1024]{0:T(1024)} %copy-done.14, f32[1024,512]{1,0:T(8,128)} %bitcast.221, f32[]{:T(128)} %constant.1059.clone.1), kind=kCustom, calls=%fused_computation.82 | custom fusion | flops 524288 | bytes 1280512 | tf_op jit(solution)/shard_map/scatter-add | solution.py:136
  309.3 8.7 %collective-permute-done.28 = f32[512]{0:T(512)S(1)} collective-permute-done((f32[512]{0:T(512)S(1)}, f32[512]{0:T(512)S(1)}, u32[]{:S(2)}, u32[]{:S(2)}) %collective-permute-start.28) | collective-permute-done | bytes 2080 | tf_op jit(solution)/shard_map/ppermute | solution.py:20
  329.9 5.8 %fusion.15 = f32[64,4,512,4]{2,3,1,0:T(4,128)S(1)} fusion(f32[4,4,1,1]{1,0,3,2:T(4,128)S(1)} %copy-done.6, f32[64,4,4,512]{3,2,1,0:T(4,128)} %reshape_reshape.8), kind=kOutput, calls=%fused_computation.35 | convolution fusion | flops 25165824 | bytes 4194368 | tf_op jit(solution)/shard_map/aj,ejiw->eaiw/dot_general | solution.py:71
  345.3 6.3 %bitcast_add_fusion.1 = f32[64,4,4,512]{3,2,1,0:T(4,128)} fusion(f32[64,4,512,4]{2,3,1,0:T(4,128)S(1)} %fusion.13, f32[4,4,1,1]{1,0,3,2:T(4,128)S(1)} %copy-done.6, f32[64,4,512,4]{2,3,1,0:T(4,128)S(1)} %fusion.79, f32[64,4,4]{2,1,0:T(4,128)S(1)} %copy-done.4), kind=kOutput, calls=%fused_computation.15 | convolution fusion | flops 26214400 | bytes 6295616 | tf_op jit(solution)/shard_map/ai,ejiw->ejaw/dot_general | solution.py:66
  354.5 8.2 %scatter_custom_fusion.4 = f32[625,512]{1,0:T(8,128)S(1)} fusion(s32[1024]{0:T(1024)} %copy-done.14, f32[1024,512]{1,0:T(8,128)} %add.475, f32[1024]{0:T(1024)S(1)} %copy-done.10, f32[1024]{0:T(1024)S(1)} %copy-done.9, f32[]{:T(128)} %constant.1059.clone.1), kind=kCustom, calls=%fused_computation.52 | custom fusion | flops 1572864 | bytes 3385856 | tf_op jit(solution)/shard_map/scatter-add | solution.py:136
  388.1 5.4 %collective-permute-done.36 = f32[512]{0:T(512)S(1)} collective-permute-done((f32[512]{0:T(512)S(1)}, f32[512]{0:T(512)S(1)}, u32[]{:S(2)}, u32[]{:S(2)}) %collective-permute-start.36) | collective-permute-done | bytes 2080 | tf_op jit(solution)/shard_map/ppermute | solution.py:20
  416.9 5.8 %fusion.11 = f32[64,4,512,4]{2,3,1,0:T(4,128)S(1)} fusion(f32[4,4,1,1]{1,0,3,2:T(4,128)S(1)} %copy-done.6, f32[64,4,4,512]{3,2,1,0:T(4,128)} %reshape_reshape.9), kind=kOutput, calls=%fused_computation.31 | convolution fusion | flops 25165824 | bytes 4194368 | tf_op jit(solution)/shard_map/aj,ejiw->eaiw/dot_general | solution.py:71
  432.3 6.2 %bitcast_add_fusion = f32[64,4,4,512]{3,2,1,0:T(4,128)} fusion(f32[64,4,512,4]{2,3,1,0:T(4,128)S(1)} %fusion.9, f32[4,4,1,1]{1,0,3,2:T(4,128)S(1)} %copy-done.6, f32[64,4,512,4]{2,3,1,0:T(4,128)S(1)} %fusion.80, f32[64,4,4]{2,1,0:T(4,128)S(1)} %copy-done.5), kind=kOutput, calls=%fused_computation.11 | convolution fusion | flops 26214400 | bytes 6295616 | tf_op jit(solution)/shard_map/ai,ejiw->ejaw/dot_general | solution.py:66
  441.5 8.2 %scatter_custom_fusion.5 = f32[625,512]{1,0:T(8,128)S(1)} fusion(s32[1024]{0:T(1024)} %copy-done.14, f32[1024,512]{1,0:T(8,128)} %add.485, f32[1024]{0:T(1024)S(1)} %copy-done.10, f32[1024]{0:T(1024)S(1)} %copy-done.9, f32[]{:T(128)} %constant.1059.clone.1), kind=kCustom, calls=%fused_computation.48 | custom fusion | flops 1572864 | bytes 3385856 | tf_op jit(solution)/shard_map/scatter-add | solution.py:136
  475.1 5.4 %collective-permute-done.44 = f32[512]{0:T(512)S(1)} collective-permute-done((f32[512]{0:T(512)S(1)}, f32[512]{0:T(512)S(1)}, u32[]{:S(2)}, u32[]{:S(2)}) %collective-permute-start.44) | collective-permute-done | bytes 2080 | tf_op jit(solution)/shard_map/ppermute | solution.py:20
  (297 shorter events, 339.7 us)
Async XLA Ops:
  10.1 99.2 %collective-permute-start.11 = (f32[25,1]{0,1:T(1,128)}, f32[25,1]{0,1:T(1,128)}, u32[]{:S(2)}, u32[]{:S(2)}) collective-permute-start(f32[25,1]{0,1:T(1,128)} %get-tuple-element.662), channel_id=1, source_target_pairs={{120,0},{121,1},{122,2},{123,3},{124,4},{125,5},{126,6},{127,7},{0... | collective-permute-start | bytes 308 | tf_op jit(solution)/shard_map/ppermute | solution.py:20
  11.7 96.8 %collective-permute-start.10 = (f32[25,1]{0,1:T(1,128)}, f32[25,1]{0,1:T(1,128)}, u32[]{:S(2)}, u32[]{:S(2)}) collective-permute-start(f32[25,1]{0,1:T(1,128)} %get-tuple-element.663), channel_id=1, source_target_pairs={{8,0},{9,1},{10,2},{11,3},{12,4},{13,5},{14,6},{15,7},{16,8},{17,9... | collective-permute-start | bytes 308 | tf_op jit(solution)/shard_map/ppermute | solution.py:20
  17.2 114.8 %collective-permute-start.15 = (f32[1]{0:T(128)}, f32[1]{0:T(128)}, u32[]{:S(2)}, u32[]{:S(2)}) collective-permute-start(f32[1]{0:T(128)} %bitcast.38), channel_id=1, source_target_pairs={{9,0},{10,1},{11,2},{12,3},{13,4},{14,5},{15,6},{16,7},{17,8},{18,... | collective-permute-start | bytes 20 | tf_op jit(solution)/shard_map/ppermute | solution.py:20
  20.8 109.2 %collective-permute-start.14 = (f32[1]{0:T(128)}, f32[1]{0:T(128)}, u32[]{:S(2)}, u32[]{:S(2)}) collective-permute-start(f32[1]{0:T(128)} %bitcast.35), channel_id=1, source_target_pairs={{7,0},{8,1},{9,2},{10,3},{11,4},{12,5},{13,6},{14,7},{15,8},{16,9}... | collective-permute-start | bytes 20 | tf_op jit(solution)/shard_map/ppermute | solution.py:20
  21.5 78.1 %collective-permute-start.9 = (f32[1,25,1]{1,2,0:T(1,128)}, f32[1,25,1]{1,2,0:T(1,128)}, u32[]{:S(2)}, u32[]{:S(2)}) collective-permute-start(f32[1,25,1]{1,2,0:T(1,128)} %bitcast.119), channel_id=1, source_target_pairs={{1,0},{2,1},{3,2},{4,3},{5,4},{6,5},{7,6},{8,7},{9,8},{10,9},{11,1... | collective-permute-start | bytes 308 | tf_op jit(solution)/shard_map/ppermute | solution.py:31
  109.3 24.2 %collective-permute-start = (f32[1,25,512]{2,0,1:T(1,128)S(1)}, f32[1,25,512]{2,0,1:T(1,128)S(1)}, u32[]{:S(2)}, u32[]{:S(2)}) collective-permute-start(f32[1,25,512]{2,0,1:T(1,128)S(1)} %get-tuple-element.643), channel_id=1, source_target_pairs={{0,1},{1,2},{2,3},{3,4},{4,5},{5,6},{6,7},{7,8},{8,9},{9,10},{10,1... | collective-permute-start | bytes 153608 | tf_op jit(solution)/shard_map/ppermute | solution.py:30
  117.3 29.8 %collective-permute-start.3 = (f32[25,512]{1,0:T(8,128)S(1)}, f32[25,512]{1,0:T(8,128)S(1)}, u32[]{:S(2)}, u32[]{:S(2)}) collective-permute-start(f32[25,512]{1,0:T(8,128)S(1)} %get-tuple-element.652), channel_id=1, source_target_pairs={{120,0},{121,1},{122,2},{123,3},{124,4},{125,5},{126,6},{127,7},{0... | collective-permute-start | bytes 153608 | tf_op jit(solution)/shard_map/ppermute | solution.py:20
  118.0 27.4 %collective-permute-start.2 = (f32[25,512]{1,0:T(8,128)}, f32[25,512]{1,0:T(8,128)S(1)}, u32[]{:S(2)}, u32[]{:S(2)}) collective-permute-start(f32[25,512]{1,0:T(8,128)} %get-tuple-element.653), channel_id=1, source_target_pairs={{8,0},{9,1},{10,2},{11,3},{12,4},{13,5},{14,6},{15,7},{16,8},{17,9... | collective-permute-start | bytes 153608 | tf_op jit(solution)/shard_map/ppermute | solution.py:20
  130.0 30.9 %collective-permute-start.6 = (f32[512]{0:T(512)S(1)}, f32[512]{0:T(512)S(1)}, u32[]{:S(2)}, u32[]{:S(2)}) collective-permute-start(f32[512]{0:T(512)S(1)} %bitcast.252), channel_id=1, source_target_pairs={{7,0},{8,1},{9,2},{10,3},{11,4},{12,5},{13,6},{14,7},{15,8},{16,9}... | collective-permute-start | bytes 6152 | tf_op jit(solution)/shard_map/ppermute | solution.py:20
  132.0 30.9 %collective-permute-start.7 = (f32[512]{0:T(512)S(1)}, f32[512]{0:T(512)S(1)}, u32[]{:S(2)}, u32[]{:S(2)}) collective-permute-start(f32[512]{0:T(512)S(1)} %bitcast.251), channel_id=1, source_target_pairs={{9,0},{10,1},{11,2},{12,3},{13,4},{14,5},{15,6},{16,7},{17,8},{18,... | collective-permute-start | bytes 6152 | tf_op jit(solution)/shard_map/ppermute | solution.py:20
  139.2 16.3 %collective-permute-start.5 = (f32[512]{0:T(512)S(1)}, f32[512]{0:T(512)S(1)}, u32[]{:S(2)}, u32[]{:S(2)}) collective-permute-start(f32[512]{0:T(512)S(1)} %bitcast.253), channel_id=1, source_target_pairs={{121,0},{122,1},{123,2},{124,3},{125,4},{126,5},{127,6},{0,7},{1,8... | collective-permute-start | bytes 6152 | tf_op jit(solution)/shard_map/ppermute | solution.py:20
  212.0 19.9 %collective-permute-start.19 = (f32[25,512]{1,0:T(8,128)S(1)}, f32[25,512]{1,0:T(8,128)S(1)}, u32[]{:S(2)}, u32[]{:S(2)}) collective-permute-start(f32[25,512]{1,0:T(8,128)S(1)} %get-tuple-element.650), channel_id=1, source_target_pairs={{120,0},{121,1},{122,2},{123,3},{124,4},{125,5},{126,6},{127,7},{0... | collective-permute-start | bytes 153608 | tf_op jit(solution)/shard_map/ppermute | solution.py:20
  213.5 16.5 %collective-permute-start.18 = (f32[25,512]{1,0:T(8,128)}, f32[25,512]{1,0:T(8,128)S(1)}, u32[]{:S(2)}, u32[]{:S(2)}) collective-permute-start(f32[25,512]{1,0:T(8,128)} %get-tuple-element.651), channel_id=1, source_target_pairs={{8,0},{9,1},{10,2},{11,3},{12,4},{13,5},{14,6},{15,7},{16,8},{17,9... | collective-permute-start | bytes 153608 | tf_op jit(solution)/shard_map/ppermute | solution.py:20
  217.4 28.1 %collective-permute-start.22 = (f32[512]{0:T(512)S(1)}, f32[512]{0:T(512)S(1)}, u32[]{:S(2)}, u32[]{:S(2)}) collective-permute-start(f32[512]{0:T(512)S(1)} %bitcast.260), channel_id=1, source_target_pairs={{7,0},{8,1},{9,2},{10,3},{11,4},{12,5},{13,6},{14,7},{15,8},{16,9}... | collective-permute-start | bytes 6152 | tf_op jit(solution)/shard_map/ppermute | solution.py:20
  217.4 30.1 %collective-permute-start.23 = (f32[512]{0:T(512)S(1)}, f32[512]{0:T(512)S(1)}, u32[]{:S(2)}, u32[]{:S(2)}) collective-permute-start(f32[512]{0:T(512)S(1)} %bitcast.256), channel_id=1, source_target_pairs={{9,0},{10,1},{11,2},{12,3},{13,4},{14,5},{15,6},{16,7},{17,8},{18,... | collective-permute-start | bytes 6152 | tf_op jit(solution)/shard_map/ppermute | solution.py:20
  298.8 22.5 %collective-permute-start.30 = (f32[512]{0:T(512)S(1)}, f32[512]{0:T(512)S(1)}, u32[]{:S(2)}, u32[]{:S(2)}) collective-permute-start(f32[512]{0:T(512)S(1)} %bitcast.261), channel_id=1, source_target_pairs={{7,0},{8,1},{9,2},{10,3},{11,4},{12,5},{13,6},{14,7},{15,8},{16,9}... | collective-permute-start | bytes 6152 | tf_op jit(solution)/shard_map/ppermute | solution.py:20
  298.8 22.6 %collective-permute-start.31 = (f32[512]{0:T(512)S(1)}, f32[512]{0:T(512)S(1)}, u32[]{:S(2)}, u32[]{:S(2)}) collective-permute-start(f32[512]{0:T(512)S(1)} %bitcast.257), channel_id=1, source_target_pairs={{9,0},{10,1},{11,2},{12,3},{13,4},{14,5},{15,6},{16,7},{17,8},{18,... | collective-permute-start | bytes 6152 | tf_op jit(solution)/shard_map/ppermute | solution.py:20
  366.7 19.9 %collective-permute-start.35 = (f32[25,512]{1,0:T(8,128)S(1)}, f32[25,512]{1,0:T(8,128)S(1)}, u32[]{:S(2)}, u32[]{:S(2)}) collective-permute-start(f32[25,512]{1,0:T(8,128)S(1)} %get-tuple-element.646), channel_id=1, source_target_pairs={{120,0},{121,1},{122,2},{123,3},{124,4},{125,5},{126,6},{127,7},{0... | collective-permute-start | bytes 153608 | tf_op jit(solution)/shard_map/ppermute | solution.py:20
  372.1 28.1 %collective-permute-start.38 = (f32[512]{0:T(512)S(1)}, f32[512]{0:T(512)S(1)}, u32[]{:S(2)}, u32[]{:S(2)}) collective-permute-start(f32[512]{0:T(512)S(1)} %bitcast.262), channel_id=1, source_target_pairs={{7,0},{8,1},{9,2},{10,3},{11,4},{12,5},{13,6},{14,7},{15,8},{16,9}... | collective-permute-start | bytes 6152 | tf_op jit(solution)/shard_map/ppermute | solution.py:20
  372.1 30.1 %collective-permute-start.39 = (f32[512]{0:T(512)S(1)}, f32[512]{0:T(512)S(1)}, u32[]{:S(2)}, u32[]{:S(2)}) collective-permute-start(f32[512]{0:T(512)S(1)} %bitcast.258), channel_id=1, source_target_pairs={{9,0},{10,1},{11,2},{12,3},{13,4},{14,5},{15,6},{16,7},{17,8},{18,... | collective-permute-start | bytes 6152 | tf_op jit(solution)/shard_map/ppermute | solution.py:20
  453.7 19.9 %collective-permute-start.43 = (f32[25,512]{1,0:T(8,128)S(1)}, f32[25,512]{1,0:T(8,128)S(1)}, u32[]{:S(2)}, u32[]{:S(2)}) collective-permute-start(f32[25,512]{1,0:T(8,128)S(1)} %get-tuple-element.644), channel_id=1, source_target_pairs={{120,0},{121,1},{122,2},{123,3},{124,4},{125,5},{126,6},{127,7},{0... | collective-permute-start | bytes 153608 | tf_op jit(solution)/shard_map/ppermute | solution.py:20
  455.5 16.3 %collective-permute-start.42 = (f32[25,512]{1,0:T(8,128)}, f32[25,512]{1,0:T(8,128)S(1)}, u32[]{:S(2)}, u32[]{:S(2)}) collective-permute-start(f32[25,512]{1,0:T(8,128)} %get-tuple-element.645), channel_id=1, source_target_pairs={{8,0},{9,1},{10,2},{11,3},{12,4},{13,5},{14,6},{15,7},{16,8},{17,9... | collective-permute-start | bytes 153608 | tf_op jit(solution)/shard_map/ppermute | solution.py:20
  459.1 28.1 %collective-permute-start.46 = (f32[512]{0:T(512)S(1)}, f32[512]{0:T(512)S(1)}, u32[]{:S(2)}, u32[]{:S(2)}) collective-permute-start(f32[512]{0:T(512)S(1)} %bitcast.259), channel_id=1, source_target_pairs={{7,0},{8,1},{9,2},{10,3},{11,4},{12,5},{13,6},{14,7},{15,8},{16,9}... | collective-permute-start | bytes 6152 | tf_op jit(solution)/shard_map/ppermute | solution.py:20
  459.1 30.1 %collective-permute-start.47 = (f32[512]{0:T(512)S(1)}, f32[512]{0:T(512)S(1)}, u32[]{:S(2)}, u32[]{:S(2)}) collective-permute-start(f32[512]{0:T(512)S(1)} %bitcast.255), channel_id=1, source_target_pairs={{9,0},{10,1},{11,2},{12,3},{13,4},{14,5},{15,6},{16,7},{17,8},{18,... | collective-permute-start | bytes 6152 | tf_op jit(solution)/shard_map/ppermute | solution.py:20
  (39 other events, 486.2 us)
where the time goes:
time: 512 us; the launch traced here: 504 us
  local copies, waits for them, and re-layouts  161 us (31%)
  other arithmetic  142 us (28%)
  starting transfers between devices  74.3 us (15%)
  matrix products  73.5 us (14%)
  waiting for transfers between devices  47.1 us (9%)
  between operations  6.16 us (1%)
    ppermute x36, starting transfers between devices, from_behind(): return lax.ppermute(block, axis, route)  66.7 us
    scatter-add x5, other arithmetic, average(): jax.ops.segment_sum((mass[:, :, None] * field).reshape(-1, width), flat_n...  39.8 us
    dot_general x7, matrix products, along_xi(): jnp.einsum('ai,ejiw->ejaw', deriv, shaped, precision=HIGHEST)  38.3 us
    ppermute x36, waiting for transfers between devices, from_behind(): return lax.ppermute(block, axis, route)  37.8 us
    dot_general x7, matrix products, along_eta(): jnp.einsum('aj,ejiw->eaiw', deriv, shaped, precision=HIGHEST)  35.2 us
    gather x5, local copies, waits for them, and re-layouts, average(): return combined.reshape(side * side, width)[flat_nodes].reshape(field.shape)  23 us
    scatter-add x12, local copies, waits for them, and re-layouts, combine_shared(): sums.at[:, 0].add(beside_all[0]).at[:, side - 1].add(beside_all[3])  18.1 us
    mul x3, other arithmetic, tendency(): metric * wind_xi * field  15.3 us
  transfers between devices with their start and end apart: 48, of which 9 were waited for; matrix products, arithmetic and copies ran while one was open for 32% of the time, Pallas kernels for 0%

commit v1 on v0

v1 whole, which is shorter than its diff:
```python
import functools
import jax
import jax.numpy as jnp
import numpy as np
from jax import lax
from jax.experimental import pallas as pl
from jax.experimental.pallas import tpu as pltpu
from jax.sharding import PartitionSpec as P

TT = 8
PX = 8
STEP_SIZE = 0.04
DIFFUSION = 0.0001
F32 = jnp.float32
VMEM_LIMIT = 48 * 1024 * 1024


def gll_derivative():
    points = np.array([-1.0, -np.sqrt(0.2), np.sqrt(0.2), 1.0])
    bary = np.array(
        [1.0 / np.prod([points[t] - points[p] for p in range(4) if p != t]) for t in range(4)]
    )
    deriv = np.zeros((4, 4))
    for a in range(4):
        for i in range(4):
            if a != i:
                deriv[a, i] = bary[i] / bary[a] / (points[a] - points[i])
        deriv[a, a] = -np.sum(deriv[a])
    return deriv


D = gll_derivative()
ODD_00, ODD_01 = (float(0.5 * (D[0, 0] - D[0, 3])), float(0.5 * (D[0, 1] - D[0, 2])))
ODD_10, ODD_11 = (float(0.5 * (D[1, 0] - D[1, 3])), float(0.5 * (D[1, 1] - D[1, 2])))
EVEN_0, EVEN_1 = (float(0.5 * (D[0, 0] + D[0, 3])), float(0.5 * (D[1, 0] + D[1, 3])))


def line(g0, g1, g2, g3):
    o0, o1 = (g0 - g3, g1 - g2)
    ev = (g0 + g3) - (g1 + g2)
    a = ODD_00 * o0 + ODD_01 * o1
    c = ODD_10 * o0 + ODD_11 * o1
    b = EVEN_0 * ev
    e = EVEN_1 * ev
    return a + b, c + e, c - e, a - b


def roll(x, shift):
    return pltpu.roll(x, shift % 8, 0)


def sublane():
    return lax.broadcasted_iota(jnp.int32, (8, 128), 0)


def row8(ref, y):
    return jnp.broadcast_to(ref[pl.ds(y, 1), :], (8, 128))


def tendency_step(f, u, v, rj):
    dx = [None] * 16
    for j in range(4):
        dx[4 * j : 4 * j + 4] = line(*[u(4 * j + i) * f[4 * j + i] for i in range(4)])
    out = [None] * 16
    for i in range(4):
        de = line(*[v(4 * j + i) * f[4 * j + i] for j in range(4)])
        for j in range(4):
            n = 4 * j + i
            out[n] = f[n] - rj(n) * (dx[n] + de[j])
    return out


def weighted(values):
    corner = (values[0] + values[3]) + (values[12] + values[15])
    edge = ((values[1] + values[2]) + (values[4] + values[7])) + (
        (values[8] + values[11]) + (values[13] + values[14])
    )
    inner = (values[5] + values[6]) + (values[9] + values[10])
    return corner + 5.0 * edge + 25.0 * inner


def limited(g, jac, rden):
    mean = weighted([jac[n] * g[n] for n in range(16)]) * rden
    lows = list(g)
    while len(lows) > 1:
        lows = [jnp.minimum(lows[k], lows[k + 1]) for k in range(0, len(lows), 2)]
    low = lows[0]
    positive = jnp.maximum(mean, 0.0)
    negative = low < 0.0
    denominator = jnp.where(negative, positive - low, 1.0)
    scaling = jnp.where(negative, positive / denominator, 1.0)
    return [jac[n] * (mean + scaling * (g[n] - mean)) for n in range(16)]


def add_nodes(sums, edge, ey, c, sub):
    for j in range(4):
        c0, c1, c2, c3 = c[4 * j : 4 * j + 4]
        c0 = c0 + jnp.where(sub == 0, 0.0, roll(c3, 1))
        last = c3[7:8, :]
        y = 3 * ey + j
        if j == 0:
            c0, c1, c2 = (c0 + sums[y, 0], c1 + sums[y, 1], c2 + sums[y, 2])
            last = last + edge[pl.ds(y, 1), :]
        sums[y, 0] = c0
        sums[y, 1] = c1
        sums[y, 2] = c2
        edge[pl.ds(y, 1), :] = last


def clear_first(sums, edge):
    for ii in range(3):
        sums[0, ii] = jnp.zeros((8, 128), F32)
    edge[0:1, :] = jnp.zeros((1, 128), F32)


def thin_messages(sums, edge, west, north, south):
    def copy(y, _):
        west[pl.ds(y, 1), :] = sums[y, 0, 0:1, :]
        return 0

    lax.fori_loop(0, 25, copy, 0, unroll=5)
    for out, y in ((north, 0), (south, 24)):
        for ii in range(3):
            out[8 * ii : 8 * ii + 8, :] = sums[y, ii]
        out[24:32, :] = row8(edge, y)


def spot(nodes, e):
    corner = nodes[e, 0]
    ey = corner // 75
    return ey * 8 + (corner - 75 * ey) // 3


def first_kernel(
    nodes, x, vel, jin, sums, west, east, north, south, t0, u_ref, v_ref, rj_ref, j_ref, rd_ref, gathered, jc
):
    step = pl.program_id(0)
    sub = sublane()
    lane = lax.broadcasted_iota(jnp.int32, (8, 128), 1)

    def gather(src):
        def body(e, _):
            gathered[spot(nodes, e)] = src[e]
            return 0

        lax.fori_loop(0, 64, body, 0, unroll=8)

    @pl.when(step == 0)
    def _():
        gather(vel)
        jc[...] = jnp.zeros_like(jc)

        def jbody(e, _):
            jc[pl.ds(spot(nodes, e), 1), 0:16] = jin[pl.ds(e, 1), :]
            return 0

        lax.fori_loop(0, 64, jbody, 0, unroll=8)
        flat = gathered.reshape(1024, 128)

        def coef(ey, _):
            comp = jc[pl.ds(pl.multiple_of(8 * ey, 8), 8), :]
            js = []
            for n in range(16):
                jv = jnp.broadcast_to(comp[:, n : n + 1], (8, 128))
                w = flat[pl.ds(ey * 128 + n, 8, stride=16), :]
                wr = pltpu.roll(w, 64, 1)
                dj = STEP_SIZE * jv
                u_ref[n, ey] = dj * jnp.where(lane < 64, w, wr)
                v_ref[n, ey] = dj * jnp.where(lane < 64, wr, w)
                j_ref[n, ey] = jv
                rj_ref[n, ey] = 1.0 / jv
                js.append(jv)
            rd_ref[ey] = 1.0 / weighted(js)
            return 0

        lax.fori_loop(0, 8, coef, 0)

    gather(x)
    flat = gathered.reshape(1024, 128)
    clear_first(sums, east)

    def rows(ey, _):
        f = [flat[pl.ds(ey * 128 + n, 8, stride=16), :] for n in range(16)]
        for n in range(16):
            t0[n, ey] = f[n]
        g = tendency_step(
            f, lambda n: u_ref[n, ey], lambda n: v_ref[n, ey], lambda n: rj_ref[n, ey]
        )
        c = limited(g, [j_ref[n, ey] for n in range(16)], rd_ref[ey])
        add_nodes(sums, east, ey, c, sub)
        return 0

    lax.fori_loop(0, 8, rows, 0)
    thin_messages(sums, east, west, north, south)
    for out in (west, east):
        for half in range(2):
            out[32 + 8 * half : 40 + 8 * half, :] = jc[
                pl.ds(pl.multiple_of(8 * (4 * half + step), 8), 8), :
            ]


def geometry_kernel(own, from_e, from_w, from_n, from_s, j_ref, inv):
    sub = sublane()

    def tile(ref, base, t):
        return ref[base : base + 8, 128 * t : 128 * t + 128]

    pending = None
    for r in range(-3, 11):
        if r < 0:
            t = r + 4
            a, b = (tile(from_n, 32, t), tile(from_n, 40, t))
        elif r > 7:
            t = r - 8
            a, b = (tile(from_s, 32, t), tile(from_s, 40, t))
        else:
            base, t = (32 + 8 * (r // 4), r % 4)
            a = tile(own, base, t)
            b = jnp.where(sub < 4, tile(from_e, base, t), tile(from_w, base, t))
        kept = None
        for j in range(4):
            ca = [jnp.broadcast_to(a[:, 4 * j + i : 4 * j + i + 1], (8, 128)) for i in range(4)]
            cb = [jnp.broadcast_to(b[:, 4 * j + i : 4 * j + i + 1], (8, 128)) for i in range(4)]
            if -2 <= r <= 9:
                for i in range(4):
                    j_ref[4 * j + i, r + 2, 0:8] = ca[i]
                    j_ref[4 * j + i, r + 2, 8:16] = cb[i]
            ra, rb = (roll(ca[3], 1), roll(cb[3], 1))
            row = [
                ca[0] + jnp.where(sub == 0, rb, ra),
                cb[0] + jnp.where(sub == 0, ra, rb),
                ca[1],
                cb[1],
                ca[2],
                cb[2],
            ]
            if j == 3:
                kept = row
                continue
            if j == 0 and pending is not None:
                row = [p + q for p, q in zip(row, pending)]
            y = 3 * r + j + 6
            if 0 <= y <= 36:
                for ii in range(3):
                    inv[y, ii, 0:8] = 1.0 / row[2 * ii]
                    inv[y, ii, 8:16] = 1.0 / row[2 * ii + 1]
        pending = kept


def node_values(sums, edge, from_e, from_w, from_n, from_s, inv, whole, side, sub):
    def body(y, _):
        whole[y, 0] = (sums[y, 0] + jnp.where(sub == 0, row8(from_w, y), 0.0)) * inv[y + 6, 0, 0:8]
        whole[y, 1] = sums[y, 1] * inv[y + 6, 1, 0:8]
        whole[y, 2] = sums[y, 2] * inv[y + 6, 2, 0:8]
        side[pl.ds(y, 1), :] = (edge[pl.ds(y, 1), :] + from_e[pl.ds(y, 1), :]) * inv[y + 6, 0, 8:9]
        return 0

    lax.fori_loop(0, 25, body, 0, unroll=5)
    for y, msg in ((0, from_n), (24, from_s)):
        for ii in range(3):
            whole[y, ii] = whole[y, ii] + msg[8 * ii : 8 * ii + 8, :] * inv[y + 6, ii, 0:8]
        side[y : y + 1, :] = side[y : y + 1, :] + msg[24:25, :] * inv[y + 6, 0, 8:9]


def element_values(whole, side, ey, sub):
    f = []
    for j in range(4):
        y = 3 * ey + j
        p0 = whole[y, 0]
        f += [p0, whole[y, 1], whole[y, 2], jnp.where(sub == 7, row8(side, y), roll(p0, 7))]
    return f


def stage_kernel(
    keep, take, wide, sums, edge, from_e, from_w, from_n, from_s, inv, t0, u_ref, v_ref, rj_ref, j_ref, rd_ref,
    out, west, east, third, fourth, whole, side,
):
    sub = sublane()
    node_values(sums, edge, from_e, from_w, from_n, from_s, inv, whole, side, sub)
    column = fourth if wide else east
    clear_first(out, column)

    def rows(ey, _):
        f = element_values(whole, side, ey, sub)
        h = tendency_step(
            f, lambda n: u_ref[n, ey], lambda n: v_ref[n, ey], lambda n: rj_ref[n, ey]
        )
        g = [keep * t0[n, ey] + take * h[n] for n in range(16)]
        c = limited(g, [j_ref[n, ey] for n in range(16)], rd_ref[ey])
        add_nodes(out, column, ey, c, sub)
        return 0

    lax.fori_loop(0, 8, rows, 0)
    if not wide:
        thin_messages(out, column, west, third, fourth)
        return

    def pack(y, _):
        p0, p1, p2 = (out[y, 0], out[y, 1], out[y, 2])
        west[y] = jnp.where(sub < 3, p0, jnp.where(sub < 5, roll(p1, 3), roll(p2, 5)))
        east[y] = jnp.where(
            sub >= 6,
            p0,
            jnp.where(sub >= 4, roll(p1, -2), jnp.where(sub >= 2, roll(p2, -4), row8(column, y))),
        )
        return 0

    lax.fori_loop(0, 25, pack, 0, unroll=5)


def joined_row(sums, edge, from_e, from_w, y, sub):
    me, mw = (from_e[y], from_w[y])
    a0 = sums[y, 0] + jnp.where(sub == 0, mw, 0.0)
    b0 = jnp.where(sub == 0, row8(edge, y) + me, jnp.where(sub < 4, me, mw))
    b1 = jnp.where(sub < 4, roll(me, -3), roll(mw, 2))
    b2 = jnp.where(sub < 4, roll(me, -5), roll(mw, 4))
    return a0, sums[y, 1], sums[y, 2], b0, b1, b2


def rows_kernel(sums, edge, from_e, from_w, north, south):
    sub = sublane()
    for out, first in ((north, 0), (south, 18)):
        for k in range(7):
            a0, a1, a2, b0, b1, b2 = joined_row(sums, edge, from_e, from_w, first + k, sub)
            out[k, 0:8] = a0
            out[k, 8:16] = a1
            out[k, 16:24] = a2
            out[k, 24:32] = b0
            out[k, 32:40] = jnp.where((sub < 2) | (sub >= 6), b1, roll(b2, 4))


def laplace_rows(src, j_ref, inv, dst, first, last, sub):
    for ii in range(3):
        dst[3 * first, ii] = jnp.zeros((16, 128), F32)

    def core(f, jac):
        out = [None] * 16
        for j in range(4):
            d = line(*f[4 * j : 4 * j + 4])
            out[4 * j : 4 * j + 4] = line(*[jac(4 * j + i) * d[i] for i in range(4)])
        for i in range(4):
            d = line(*f[i::4])
            d = line(*[jac(4 * j + i) * d[j] for j in range(4)])
            for j in range(4):
                out[4 * j + i] = out[4 * j + i] + d[j]
        return out

    def rows(r, _):
        fa, fb = ([], [])
        for j in range(4):
            y = 3 * r + j
            pa, pb = (src[y, 0, 0:8], src[y, 0, 8:16])
            ra, rb = (roll(pa, 7), roll(pb, 7))
            fa += [pa, src[y, 1, 0:8], src[y, 2, 0:8], jnp.where(sub == 7, rb, ra)]
            fb += [pb, src[y, 1, 8:16], src[y, 2, 8:16], jnp.where(sub == 7, ra, rb)]
        ca = core(fa, lambda n: j_ref[n, r, 0:8])
        cb = core(fb, lambda n: j_ref[n, r, 8:16])
        for j in range(4):
            y = 3 * r + j
            ra, rb = (roll(ca[4 * j + 3], 1), roll(cb[4 * j + 3], 1))
            row = [
                (ca[4 * j] + jnp.where(sub == 0, rb, ra), cb[4 * j] + jnp.where(sub == 0, ra, rb)),
                (ca[4 * j + 1], cb[4 * j + 1]),
                (ca[4 * j + 2], cb[4 * j + 2]),
            ]
            for ii in range(3):
                a, b = row[ii]
                if j == 0:
                    a, b = (a + dst[y, ii, 0:8], b + dst[y, ii, 8:16])
                if j < 3:
                    a, b = (a * inv[y, ii, 0:8], b * inv[y, ii, 8:16])
                dst[y, ii, 0:8] = a
                dst[y, ii, 8:16] = b
        return 0

    lax.fori_loop(first, last, rows, 0)


def last_kernel(
    nodes, sums, edge, from_e, from_w, from_n, from_s, j_ref, inv, out, field, one, two, spread
):
    sub = sublane()

    def own(y, _):
        a0, a1, a2, b0, b1, b2 = joined_row(sums, edge, from_e, from_w, y, sub)
        for ii, (a, b) in enumerate(((a0, b0), (a1, b1), (a2, b2))):
            field[y + 6, ii, 0:8] = a * inv[y + 6, ii, 0:8]
            field[y + 6, ii, 8:16] = b * inv[y + 6, ii, 8:16]
        return 0

    lax.fori_loop(0, 25, own, 0, unroll=5)
    for msg, first, shared in ((from_n, 0, 6), (from_s, 30, 0)):
        for k in range(7):
            y = first + k
            c = msg[k, 32:40]
            parts = [msg[k, 0:8], msg[k, 24:32], msg[k, 8:16], c, msg[k, 16:24], roll(c, 4)]
            for ii in range(3):
                a, b = (parts[2 * ii] * inv[y, ii, 0:8], parts[2 * ii + 1] * inv[y, ii, 8:16])
                if k == shared:
                    a, b = (a + field[y, ii, 0:8], b + field[y, ii, 8:16])
                field[y, ii, 0:8] = a
                field[y, ii, 8:16] = b
    laplace_rows(field, j_ref, inv, one, 0, 12, sub)
    laplace_rows(one, j_ref, inv, two, 1, 11, sub)
    flat = spread.reshape(1024, 128)

    def finish(ey, _):
        for j in range(4):
            y = 3 * ey + j + 6
            p0 = field[y, 0, 0:8] - DIFFUSION * two[y, 0, 0:8]
            q0 = field[y, 0, 8:16] - DIFFUSION * two[y, 0, 8:16]
            vals = [
                p0,
                field[y, 1, 0:8] - DIFFUSION * two[y, 1, 0:8],
                field[y, 2, 0:8] - DIFFUSION * two[y, 2, 0:8],
                jnp.where(sub == 7, roll(q0, 7), roll(p0, 7)),
            ]
            for i in range(4):
                flat[pl.ds(ey * 128 + 4 * j + i, 8, stride=16), :] = vals[i]
        return 0

    lax.fori_loop(0, 8, finish, 0)

    def scatter(e, _):
        out[e] = spread[spot(nodes, e)]
        return 0

    lax.fori_loop(0, 64, scatter, 0, unroll=8)


def sds(*shape):
    return jax.ShapeDtypeStruct(shape, F32)


def tiled(*shape):
    zeros = (0,) * (len(shape) - 1)
    return pl.BlockSpec(shape, lambda t: zeros + (t,))


def fixed(*shape):
    zeros = (0,) * len(shape)
    return pl.BlockSpec(shape, lambda t: zeros)


PARAMS = pltpu.CompilerParams(vmem_limit_bytes=VMEM_LIMIT, dimension_semantics=("arbitrary",))
SMEM = pl.BlockSpec(memory_space=pltpu.SMEM)


def shifted(value, distance):
    size = lax.axis_size("sfc")
    return lax.ppermute(value, "sfc", [((i - distance) % size, i) for i in range(size)])


def per_device(tracers, velocity, jacobian, elem_nodes):
    coef = [sds(16, 8, 8, 128)] * 4 + [sds(8, 8, 128)]
    coef_specs = [fixed(16, 8, 8, 128)] * 4 + [fixed(8, 8, 128)]
    sums_spec = tiled(27, 3, 8, 128)
    first = pl.pallas_call(
        first_kernel,
        grid=(4,),
        in_specs=[SMEM, tiled(64, 16, 128), fixed(64, 16, 128), fixed(64, 16)],
        out_specs=[sums_spec, tiled(48, 128), tiled(48, 128), tiled(32, 128), tiled(32, 128), tiled(16, 8, 8, 128)]
        + coef_specs,
        out_shape=[sds(27, 3, 8, 512), sds(48, 512), sds(48, 512), sds(32, 512), sds(32, 512), sds(16, 8, 8, 512)]
        + coef,
        scratch_shapes=[pltpu.VMEM((64, 16, 128), F32), pltpu.VMEM((64, 128), F32)],
        compiler_params=PARAMS,
        name="section_one_sums",
    )
    sums, west, east, north, south, t0, *coefs = first(elem_nodes, tracers, velocity, jacobian)

    row = lax.broadcasted_iota(jnp.int32, (32, 1), 0)

    def corrected(own, from_w, from_e, y):
        return own + jnp.where(row == 0, from_w[y : y + 1], 0.0) + jnp.where(row >= 24, from_e[y : y + 1], 0.0)

    from_e, from_w = (shifted(west, -1), shifted(east, 1))
    low = lax.broadcasted_iota(jnp.int32, (8, 1), 0) < 4
    beside = [jnp.where(low, from_e[k : k + 8], from_w[k : k + 8]) for k in (32, 40)]
    msg_n = jnp.concatenate([corrected(north, from_w, from_e, 0), west[32:40], beside[0]])
    msg_s = jnp.concatenate([corrected(south, from_w, from_e, 24), west[40:48], beside[1]])
    from_s, from_n = (shifted(msg_n, -PX), shifted(msg_s, PX))

    whole = pl.BlockSpec(memory_space=pltpu.VMEM)
    jac, inv = pl.pallas_call(
        geometry_kernel,
        in_specs=[whole] * 5,
        out_specs=[whole] * 2,
        out_shape=[sds(16, 12, 16, 128), sds(37, 3, 16, 128)],
        compiler_params=pltpu.CompilerParams(vmem_limit_bytes=VMEM_LIMIT),
        name="geometry",
    )(west, from_e, from_w, from_n, from_s)
    jac_spec, inv_spec = (fixed(16, 12, 16, 128), fixed(37, 3, 16, 128))

    def stage(keep, take, wide, sums, edge, from_e, from_w, from_n, from_s, rows):
        if wide:
            outs = [sds(25, 8, 512), sds(25, 8, 512), sds(8, 512), sds(32, 512)]
            specs = [tiled(25, 8, 128), tiled(25, 8, 128), tiled(8, 128), tiled(32, 128)]
        else:
            outs = [sds(32, 512)] * 4
            specs = [tiled(32, 128)] * 4
        return pl.pallas_call(
            functools.partial(stage_kernel, keep, take, wide),
            grid=(4,),
            in_specs=[sums_spec]
            + [tiled(rows, 128)] * 5
            + [inv_spec, tiled(16, 8, 8, 128)]
            + coef_specs,
            out_specs=[sums_spec] + specs,
            out_shape=[sds(27, 3, 8, 512)] + outs,
            scratch_shapes=[pltpu.VMEM((27, 3, 8, 128), F32), pltpu.VMEM((32, 128), F32)],
            compiler_params=PARAMS,
            name="section_three_sums" if wide else "section_two_sums",
        )(sums, edge, from_e, from_w, from_n, from_s, inv, t0, *coefs)

    sums, west, east, north, south = stage(
        0.75, 0.25, False, sums, east, from_e, from_w, from_n, from_s, 48
    )
    from_e, from_w = (shifted(west, -1), shifted(east, 1))
    msg_n = corrected(north, from_w, from_e, 0)
    msg_s = corrected(south, from_w, from_e, 24)
    from_s, from_n = (shifted(msg_n, -PX), shifted(msg_s, PX))

    sums, west, east, _, edge = stage(
        1.0 / 3.0, 2.0 / 3.0, True, sums, east, from_e, from_w, from_n, from_s, 32
    )
    from_e, from_w = (shifted(west, -1), shifted(east, 1))
    message = tiled(25, 8, 128)
    band = tiled(7, 40, 128)
    msg_n, msg_s = pl.pallas_call(
        rows_kernel,
        grid=(4,),
        in_specs=[sums_spec, tiled(32, 128), message, message],
        out_specs=[band, band],
        out_shape=[sds(7, 40, 512)] * 2,
        compiler_params=PARAMS,
        name="row_bands",
    )(sums, edge, from_e, from_w)
    from_s, from_n = (shifted(msg_n, -PX), shifted(msg_s, PX))
    return pl.pallas_call(
        last_kernel,
        grid=(4,),
        in_specs=[SMEM, sums_spec, tiled(32, 128), message, message, band, band, jac_spec, inv_spec],
        out_specs=tiled(64, 16, 128),
        out_shape=sds(64, 16, 512),
        scratch_shapes=[pltpu.VMEM((37, 3, 16, 128), F32)] * 3 + [pltpu.VMEM((64, 16, 128), F32)],
        compiler_params=PARAMS,
        name="biharmonic",
    )(elem_nodes, sums, edge, from_e, from_w, from_n, from_s, jac, inv)


def solution(mesh):
    in_specs = (P("sfc", None, None), P("sfc", None, None), P("sfc", None), P("sfc", None))
    out_specs = P("sfc", None, None)
    return jax.shard_map(
        per_device, mesh=mesh, in_specs=in_specs, out_specs=out_specs, check_vma=False
    )
```

time: 512 us -> 118 us (0.23); the launches traced: 504 us -> 118 us
  local copies, waits for them, and re-layouts: 161 us -> 3.7 us
  other arithmetic: 142 us -> 0.29 us
  matrix products: 73.5 us -> 0 us
  starting transfers between devices: 74.3 us -> 27.8 us
  Pallas kernels: 0 us -> 39.7 us
  between operations: 6.16 us -> 0.11 us
    dot_general x14 -> x0, matrix products: 73.5 us -> none  [the longest x7 38.3 us: along_xi(): jnp.einsum('ai,ejiw->ejaw', deriv, shaped, precision=HIGHEST)]
    scatter-add x16 -> x0, other arithmetic: 59.3 us -> none  [the longest x5 39.8 us: average(): jax.ops.segment_sum((mass[:, :, None] * field).reshape(-1, width), flat_n...]
    scatter-add x38 -> x0, local copies, waits for them, and re-layouts: 48 us -> none  [the longest x12 18.1 us: combine_shared(): sums.at[:, 0].add(beside_all[0]).at[:, side - 1].add(beside_all[3])]
    ppermute x48 -> x12, starting transfers between devices: 74.3 us -> 27.8 us  [shifted(): lax.ppermute(value, 'sfc', [((i - distance) % size, i) for i in range(siz...]
    pallas_call x0 -> x6, Pallas kernels: none -> 39.7 us  [the longest x1 16.6 us: per_device(): pl.pallas_call(last_kernel, grid=(4,), in_specs=[SMEM, sums_spec, tiled(3...]
    another operation x21 -> x0, local copies, waits for them, and re-layouts: 37.5 us -> none  [the longest x3 12 us: per_device(): wind_eta = jnp.tile(velocity[:, :, levels:], (1, 1, Q))]
    reshape x16 -> x0, local copies, waits for them, and re-layouts: 26.2 us -> none  [the longest x7 14.8 us: average(): return combined.reshape(side * side, width)[flat_nodes].reshape(field.shape)]
    mul x8 -> x0, other arithmetic: 23 us -> none  [the longest x3 15.3 us: tendency(): metric * wind_xi * field]
  transfers between devices with their start and end apart: 48 -> 12, of which waited for: 9 -> 9; matrix products, arithmetic and copies ran while one was open for 32% -> 0% of each run, Pallas kernels for 0% -> 0%
where the time goes in v1:
time: 118 us
  waiting for transfers between devices  46.2 us (39%)
  Pallas kernels  39.7 us (34%)
  starting transfers between devices  27.8 us (24%)
  local copies, waits for them, and re-layouts  3.7 us (3%)
    ppermute x12, waiting for transfers between devices, shifted(): lax.ppermute(value, 'sfc', [((i - distance) % size, i) for i in range(siz...  46.2 us
    ppermute x12, starting transfers between devices, shifted(): lax.ppermute(value, 'sfc', [((i - distance) % size, i) for i in range(siz...  27.8 us
    pallas_call x1, Pallas kernels, per_device(): pl.pallas_call(last_kernel, grid=(4,), in_specs=[SMEM, sums_spec, tiled(3...  16.6 us
    pallas_call x1, Pallas kernels, per_device(): first(elem_nodes, tracers, velocity, jacobian)  11.4 us
    pallas_call x2, Pallas kernels, stage(): pl.pallas_call(functools.partial(stage_kernel, keep, take, wide), grid=(4...  10.4 us
    unnamed x8, local copies, waits for them, and re-layouts  3.68 us
  transfers between devices with their start and end apart: 12, of which 9 were waited for; matrix products, arithmetic and copies ran while one was open for 0% of the time, Pallas kernels for 0%

profile of v1, /device:TPU:0, one launch (start us, length us, event | category | flops | bytes accessed | tf_op | source)
XLA Modules:
  0.0 117.8 jit_solution(13922614288094362714)
XLA Ops:
  0.0 0.8 copy.7.nodes
  0.8 0.8 copy.6.jin
  1.6 1.0 copy-done.2
  2.6 11.4 %section_one_sums.1 = (f32[27,3,8,512]{3,2,1,0:T(8,128)S(1)}, f32[48,512]{1,0:T(8,128)S(1)}, f32[48,512]{1,0:T(8,128)S(1)}, f32[32,512]{1,0:T(8,128)S(1)}, f32[3...) custom-call(s32[64,16]{1,0:T(8,128)S(1)} %copy.7.nodes, ...), custom_call_target="tpu_custom_call" | custom-call | tf_op jit(solution)/shard_map/section_one_sums/pallas_call | solution.py:470
  14.0 8.2 %collective-permute-start = (f32[48,512]{1,0:T(8,128)S(1)}, f32[48,512]{1,0:T(8,128)S(1)}, u32[]{:S(2)}, u32[]{:S(2)}) collective-permute-start(f32[48,512]{1,0:T(8,128)S(1)} %get-tuple-element.31.own), channel_id=1, source_target_pairs={{1,0},{2,1},{3,2},{4,3},{5,4},{6,5},{7,6},{8,7},{9,8},{10,9},{11,1... | collective-permute-start | bytes 294920 | tf_op jit(solution)/shard_map/ppermute | solution.py:451
  22.2 2.3 %collective-permute-done.1.from_w = f32[48,512]{1,0:T(8,128)S(1)} collective-permute-done((f32[48,512]{1,0:T(8,128)S(1)}, f32[48,512]{1,0:T(8,128)S(1)}, u32[]{:S(2)}, u32[]{:S(2)}) %collective-permute-start.1) | collective-permute-done | bytes 98336 | tf_op jit(solution)/shard_map/ppermute | solution.py:451
  24.8 5.4 %collective-permute-start.3 = (f32[48,512]{1,0:T(8,128)S(1)}, f32[48,512]{1,0:T(8,128)S(1)}, u32[]{:S(2)}, u32[]{:S(2)}) collective-permute-start(f32[48,512]{1,0:T(8,128)S(1)} %pad_maximum_fusion.1), channel_id=1, source_target_pairs={{8,0},{9,1},{10,2},{11,3},{12,4},{13,5},{14,6},{15,7},{16,8},{17,9... | collective-permute-start | bytes 294920 | tf_op jit(solution)/shard_map/ppermute | solution.py:451
  30.2 2.5 %collective-permute-done.2.from_n = f32[48,512]{1,0:T(8,128)S(1)} collective-permute-done((f32[48,512]{1,0:T(8,128)S(1)}, f32[48,512]{1,0:T(8,128)S(1)}, u32[]{:S(2)}, u32[]{:S(2)}) %collective-permute-start.2) | collective-permute-done | bytes 98336 | tf_op jit(solution)/shard_map/ppermute | solution.py:451
  32.7 0.8 geometry.1
  33.5 4.8 %section_two_sums.1 = (f32[27,3,8,512]{3,2,1,0:T(8,128)S(1)}, f32[32,512]{1,0:T(8,128)S(1)}, f32[32,512]{1,0:T(8,128)S(1)}, f32[32,512]{1,0:T(8,128)S(1)}, f32[32,512]{1,0:T(8,128)S(1)}) custom-call(f32[27,3,8,512]{3,2,1,0:T(8,128)} %copy-done.1, f32[48,512]{1,0:T(8,128)S(1)} %get-tuple-element.30.edge, f32[48,512]{1,0:T(8,128)S(1)} %collective-permute-done.from_e, ...), custom_call_target="tpu_custom_call" | custom-call | tf_op jit(solution)/shard_map/section_two_sums/pallas_call | solution.py:502
  38.3 1.1 copy-done
  39.4 6.1 %collective-permute-start.4 = (f32[32,512]{1,0:T(8,128)S(1)}, f32[32,512]{1,0:T(8,128)S(1)}, u32[]{:S(2)}, u32[]{:S(2)}) collective-permute-start(f32[32,512]{1,0:T(8,128)S(1)} %get-tuple-element.43), channel_id=1, source_target_pairs={{1,0},{2,1},{3,2},{4,3},{5,4},{6,5},{7,6},{8,7},{9,8},{10,9},{11,1... | collective-permute-start | bytes 196616 | tf_op jit(solution)/shard_map/ppermute | solution.py:451
  45.5 1.9 %collective-permute-done.4.from_e = f32[32,512]{1,0:T(8,128)S(1)} collective-permute-done((f32[32,512]{1,0:T(8,128)S(1)}, f32[32,512]{1,0:T(8,128)S(1)}, u32[]{:S(2)}, u32[]{:S(2)}) %collective-permute-start.4) | collective-permute-done | bytes 65568 | tf_op jit(solution)/shard_map/ppermute | solution.py:451
  47.4 7.8 %collective-permute-done.5.from_w = f32[32,512]{1,0:T(8,128)S(1)} collective-permute-done((f32[32,512]{1,0:T(8,128)S(1)}, f32[32,512]{1,0:T(8,128)S(1)}, u32[]{:S(2)}, u32[]{:S(2)}) %collective-permute-start.5) | collective-permute-done | bytes 65568 | tf_op jit(solution)/shard_map/ppermute | solution.py:451
  55.4 2.0 %collective-permute-start.6 = (f32[32,512]{1,0:T(8,128)S(1)}, f32[32,512]{1,0:T(8,128)S(1)}, u32[]{:S(2)}, u32[]{:S(2)}) collective-permute-start(f32[32,512]{1,0:T(8,128)S(1)} %get-tuple-element.66), channel_id=1, source_target_pairs={{120,0},{121,1},{122,2},{123,3},{124,4},{125,5},{126,6},{127,7},{0... | collective-permute-start | bytes 196616 | tf_op jit(solution)/shard_map/ppermute | solution.py:451
  57.5 2.2 %collective-permute-done.7.from_s = f32[32,512]{1,0:T(8,128)S(1)} collective-permute-done((f32[32,512]{1,0:T(8,128)S(1)}, f32[32,512]{1,0:T(8,128)S(1)}, u32[]{:S(2)}, u32[]{:S(2)}) %collective-permute-start.7) | collective-permute-done | bytes 65568 | tf_op jit(solution)/shard_map/ppermute | solution.py:451
  59.7 3.4 %collective-permute-done.6.from_n = f32[32,512]{1,0:T(8,128)S(1)} collective-permute-done((f32[32,512]{1,0:T(8,128)S(1)}, f32[32,512]{1,0:T(8,128)S(1)}, u32[]{:S(2)}, u32[]{:S(2)}) %collective-permute-start.6) | collective-permute-done | bytes 65568 | tf_op jit(solution)/shard_map/ppermute | solution.py:451
  63.1 5.5 %section_three_sums.1 = (f32[27,3,8,512]{3,2,1,0:T(8,128)S(1)}, f32[25,8,512]{2,1,0:T(8,128)S(1)}, f32[25,8,512]{2,1,0:T(8,128)S(1)}, f32[8,512]{1,0:T(8,128)}, f32[32,512]{1,0:T(8,128)S(1)}) custom-call(f32[27,3,8,512]{3,2,1,0:T(8,128)} %copy-done, f32[32,512]{1,0:T(8,128)S(1)} %get-tuple-element.42.edge, f32[32,512]{1,0:T(8,128)S(1)} %collective-permute-done.4.from_e, ...), custom_call_target="tpu_custom_call" | custom-call | tf_op jit(solution)/shard_map/section_three_sums/pallas_call | solution.py:502
  69.1 5.0 %collective-permute-done.8.from_e = f32[25,8,512]{2,1,0:T(8,128)S(1)} collective-permute-done((f32[25,8,512]{2,1,0:T(8,128)S(1)}, f32[25,8,512]{2,1,0:T(8,128)S(1)}, u32[]{:S(2)}, u32[]{:S(2)}) %collective-permute-start.8) | collective-permute-done | bytes 409632 | tf_op jit(solution)/shard_map/ppermute | solution.py:451
  74.1 13.4 %collective-permute-done.9.from_w = f32[25,8,512]{2,1,0:T(8,128)S(1)} collective-permute-done((f32[25,8,512]{2,1,0:T(8,128)S(1)}, f32[25,8,512]{2,1,0:T(8,128)S(1)}, u32[]{:S(2)}, u32[]{:S(2)}) %collective-permute-start.9) | collective-permute-done | bytes 409632 | tf_op jit(solution)/shard_map/ppermute | solution.py:451
  87.5 0.6 row_bands.1
  88.2 5.3 %collective-permute-start.11 = (f32[7,40,512]{2,1,0:T(8,128)S(1)}, f32[7,40,512]{2,1,0:T(8,128)S(1)}, u32[]{:S(2)}, u32[]{:S(2)}) collective-permute-start(f32[7,40,512]{2,1,0:T(8,128)S(1)} %get-tuple-element.51), channel_id=1, source_target_pairs={{8,0},{9,1},{10,2},{11,3},{12,4},{13,5},{14,6},{15,7},{16,8},{17,9... | collective-permute-start | bytes 1720328 | tf_op jit(solution)/shard_map/ppermute | solution.py:451
  93.5 7.7 %collective-permute-done.10.from_n = f32[7,40,512]{2,1,0:T(8,128)S(1)} collective-permute-done((f32[7,40,512]{2,1,0:T(8,128)S(1)}, f32[7,40,512]{2,1,0:T(8,128)S(1)}, u32[]{:S(2)}, u32[]{:S(2)}) %collective-permute-start.10) | collective-permute-done | bytes 573472 | tf_op jit(solution)/shard_map/ppermute | solution.py:451
  101.2 16.6 %biharmonic.1 = f32[64,16,512]{2,1,0:T(8,128)} custom-call(s32[64,16]{1,0:T(8,128)S(1)} %copy.7.nodes, f32[27,3,8,512]{3,2,1,0:T(8,128)S(1)} %get-tuple-element.46.sums, f32[32,512]{1,0:T(8,128)S(1)} %get-tuple-element.47.edge, f32[25,8,512]{2,1,0:T(8,128)S(1)} %collective-permute-done.8.from_e, f32[25,8,512]{2,1,0:T(8,128)S(1)} %collective-permute-done.9.from_w, ...), custom_call_target="tpu_custom_call" | custom-call | tf_op jit(solution)/shard_map/biharmonic/pallas_call | solution.py:540
  (26 shorter events, 1.1 us)
Async XLA Ops:
  1.6 1.0 copy-start.2
  14.0 19.5 %copy-start.1 = (f32[27,3,8,512]{3,2,1,0:T(8,128)}, f32[27,3,8,512]{3,2,1,0:T(8,128)S(1)}, u32[]{:S(2)}) copy-start(f32[27,3,8,512]{3,2,1,0:T(8,128)S(1)} %get-tuple-element.29.sums) | copy-start | bytes 3981316
  14.0 10.5 %collective-permute-start.1 = (f32[48,512]{1,0:T(8,128)S(1)}, f32[48,512]{1,0:T(8,128)S(1)}, u32[]{:S(2)}, u32[]{:S(2)}) collective-permute-start(f32[48,512]{1,0:T(8,128)S(1)} %get-tuple-element.30.edge), channel_id=1, source_target_pairs={{127,0},{0,1},{1,2},{2,3},{3,4},{4,5},{5,6},{6,7},{7,8},{8,9},{9,1... | collective-permute-start | bytes 294920 | tf_op jit(solution)/shard_map/ppermute | solution.py:451
  14.0 10.5 %collective-permute-start = (f32[48,512]{1,0:T(8,128)S(1)}, f32[48,512]{1,0:T(8,128)S(1)}, u32[]{:S(2)}, u32[]{:S(2)}) collective-permute-start(f32[48,512]{1,0:T(8,128)S(1)} %get-tuple-element.31.own), channel_id=1, source_target_pairs={{1,0},{2,1},{3,2},{4,3},{5,4},{6,5},{7,6},{8,7},{9,8},{10,9},{11,1... | collective-permute-start | bytes 294920 | tf_op jit(solution)/shard_map/ppermute | solution.py:451
  24.7 8.0 %collective-permute-start.2 = (f32[48,512]{1,0:T(8,128)S(1)}, f32[48,512]{1,0:T(8,128)S(1)}, u32[]{:S(2)}, u32[]{:S(2)}) collective-permute-start(f32[48,512]{1,0:T(8,128)S(1)} %pad_maximum_fusion), channel_id=1, source_target_pairs={{120,0},{121,1},{122,2},{123,3},{124,4},{125,5},{126,6},{127,7},{0... | collective-permute-start | bytes 294920 | tf_op jit(solution)/shard_map/ppermute | solution.py:451
  24.8 7.9 %collective-permute-start.3 = (f32[48,512]{1,0:T(8,128)S(1)}, f32[48,512]{1,0:T(8,128)S(1)}, u32[]{:S(2)}, u32[]{:S(2)}) collective-permute-start(f32[48,512]{1,0:T(8,128)S(1)} %pad_maximum_fusion.1), channel_id=1, source_target_pairs={{8,0},{9,1},{10,2},{11,3},{12,4},{13,5},{14,6},{15,7},{16,8},{17,9... | collective-permute-start | bytes 294920 | tf_op jit(solution)/shard_map/ppermute | solution.py:451
  38.3 1.1 copy-start
  39.4 8.0 %collective-permute-start.4 = (f32[32,512]{1,0:T(8,128)S(1)}, f32[32,512]{1,0:T(8,128)S(1)}, u32[]{:S(2)}, u32[]{:S(2)}) collective-permute-start(f32[32,512]{1,0:T(8,128)S(1)} %get-tuple-element.43), channel_id=1, source_target_pairs={{1,0},{2,1},{3,2},{4,3},{5,4},{6,5},{7,6},{8,7},{9,8},{10,9},{11,1... | collective-permute-start | bytes 196616 | tf_op jit(solution)/shard_map/ppermute | solution.py:451
  45.5 9.8 %collective-permute-start.5 = (f32[32,512]{1,0:T(8,128)S(1)}, f32[32,512]{1,0:T(8,128)S(1)}, u32[]{:S(2)}, u32[]{:S(2)}) collective-permute-start(f32[32,512]{1,0:T(8,128)S(1)} %get-tuple-element.42.edge), channel_id=1, source_target_pairs={{127,0},{0,1},{1,2},{2,3},{3,4},{4,5},{5,6},{6,7},{7,8},{8,9},{9,1... | collective-permute-start | bytes 196616 | tf_op jit(solution)/shard_map/ppermute | solution.py:451
  55.4 4.3 %collective-permute-start.7 = (f32[32,512]{1,0:T(8,128)S(1)}, f32[32,512]{1,0:T(8,128)S(1)}, u32[]{:S(2)}, u32[]{:S(2)}) collective-permute-start(f32[32,512]{1,0:T(8,128)S(1)} %get-tuple-element.65), channel_id=1, source_target_pairs={{8,0},{9,1},{10,2},{11,3},{12,4},{13,5},{14,6},{15,7},{16,8},{17,9... | collective-permute-start | bytes 196616 | tf_op jit(solution)/shard_map/ppermute | solution.py:451
  55.4 7.7 %collective-permute-start.6 = (f32[32,512]{1,0:T(8,128)S(1)}, f32[32,512]{1,0:T(8,128)S(1)}, u32[]{:S(2)}, u32[]{:S(2)}) collective-permute-start(f32[32,512]{1,0:T(8,128)S(1)} %get-tuple-element.66), channel_id=1, source_target_pairs={{120,0},{121,1},{122,2},{123,3},{124,4},{125,5},{126,6},{127,7},{0... | collective-permute-start | bytes 196616 | tf_op jit(solution)/shard_map/ppermute | solution.py:451
  68.6 5.5 %collective-permute-start.8 = (f32[25,8,512]{2,1,0:T(8,128)S(1)}, f32[25,8,512]{2,1,0:T(8,128)S(1)}, u32[]{:S(2)}, u32[]{:S(2)}) collective-permute-start(f32[25,8,512]{2,1,0:T(8,128)S(1)} %get-tuple-element.48), channel_id=1, source_target_pairs={{1,0},{2,1},{3,2},{4,3},{5,4},{6,5},{7,6},{8,7},{9,8},{10,9},{11,1... | collective-permute-start | bytes 1228808 | tf_op jit(solution)/shard_map/ppermute | solution.py:451
  68.6 18.8 %collective-permute-start.9 = (f32[25,8,512]{2,1,0:T(8,128)S(1)}, f32[25,8,512]{2,1,0:T(8,128)S(1)}, u32[]{:S(2)}, u32[]{:S(2)}) collective-permute-start(f32[25,8,512]{2,1,0:T(8,128)S(1)} %get-tuple-element.49), channel_id=1, source_target_pairs={{127,0},{0,1},{1,2},{2,3},{3,4},{4,5},{5,6},{6,7},{7,8},{8,9},{9,1... | collective-permute-start | bytes 1228808 | tf_op jit(solution)/shard_map/ppermute | solution.py:451
  88.1 13.1 %collective-permute-start.10 = (f32[7,40,512]{2,1,0:T(8,128)S(1)}, f32[7,40,512]{2,1,0:T(8,128)S(1)}, u32[]{:S(2)}, u32[]{:S(2)}) collective-permute-start(f32[7,40,512]{2,1,0:T(8,128)S(1)} %get-tuple-element.50), channel_id=1, source_target_pairs={{120,0},{121,1},{122,2},{123,3},{124,4},{125,5},{126,6},{127,7},{0... | collective-permute-start | bytes 1720328 | tf_op jit(solution)/shard_map/ppermute | solution.py:451
  88.2 13.0 %collective-permute-start.11 = (f32[7,40,512]{2,1,0:T(8,128)S(1)}, f32[7,40,512]{2,1,0:T(8,128)S(1)}, u32[]{:S(2)}, u32[]{:S(2)}) collective-permute-start(f32[7,40,512]{2,1,0:T(8,128)S(1)} %get-tuple-element.51), channel_id=1, source_target_pairs={{8,0},{9,1},{10,2},{11,3},{12,4},{13,5},{14,6},{15,7},{16,8},{17,9... | collective-permute-start | bytes 1720328 | tf_op jit(solution)/shard_map/ppermute | solution.py:451

commit v2 on v1

--- a/solution.py
+++ b/solution.py
@@ -125,37 +125,54 @@
         out[24:32, :] = row8(edge, y)
 
 
-def spot(nodes, e):
-    corner = nodes[e, 0]
-    ey = corner // 75
-    return ey * 8 + (corner - 75 * ey) // 3
+def place(corner):
+    ey = (corner * 874) >> 16
+    return 8 * ey + (((corner - 75 * ey) * 21846) >> 16)
+
+
+def fill_places(nodes, spots):
+    def body(e, _):
+        spots[e] = place(nodes[0, e])
+        return 0
+
+    lax.fori_loop(0, 64, body, 0, unroll=8)
 
 
 def first_kernel(
-    nodes, x, vel, jin, sums, west, east, north, south, t0, u_ref, v_ref, rj_ref, j_ref, rd_ref, gathered, jc
+    nodes, x, vel, jin, sums, west, east, north, south, t0, u_ref, v_ref, rj_ref, j_ref, rd_ref,
+    gathered, winds, jc, node_rows, j_rows, corners, spots, sem,
 ):
     step = pl.program_id(0)
     sub = sublane()
     lane = lax.broadcasted_iota(jnp.int32, (8, 128), 1)
 
-    def gather(src):
-        def body(e, _):
-            gathered[spot(nodes, e)] = src[e]
-            return 0
-
-        lax.fori_loop(0, 64, body, 0, unroll=8)
-
     @pl.when(step == 0)
     def _():
-        gather(vel)
+        copies = [
+            pltpu.make_async_copy(nodes, corners, sem.at[0]),
+            pltpu.make_async_copy(nodes, node_rows, sem.at[1]),
+            pltpu.make_async_copy(jin, j_rows, sem.at[2]),
+            pltpu.make_async_copy(vel, gathered, sem.at[3]),
+        ]
+        for copy in copies:
+            copy.start()
         jc[...] = jnp.zeros_like(jc)
-
-        def jbody(e, _):
-            jc[pl.ds(spot(nodes, e), 1), 0:16] = jin[pl.ds(e, 1), :]
+        for copy in copies[:3]:
+            copy.wait()
+        fill_places(corners, spots)
+        to = place(node_rows[0:1, :])
+        hit = (lax.broadcasted_iota(jnp.int32, (64, 64), 0) == to).astype(F32)
+        jc[:, 0:16] = lax.dot_general(
+            hit, j_rows[...], (((1,), (1,)), ((), ())), precision=lax.Precision.HIGHEST, preferred_element_type=F32
+        )
+        copies[3].wait()
+
+        def order(e, _):
+            winds[spots[e]] = gathered[e]
             return 0
 
-        lax.fori_loop(0, 64, jbody, 0, unroll=8)
-        flat = gathered.reshape(1024, 128)
+        lax.fori_loop(0, 64, order, 0, unroll=8)
+        flat = winds.reshape(1024, 128)
 
         def coef(ey, _):
             comp = jc[pl.ds(pl.multiple_of(8 * ey, 8), 8), :]
@@ -175,7 +192,11 @@
 
         lax.fori_loop(0, 8, coef, 0)
 
-    gather(x)
+    def gather(e, _):
+        gathered[spots[e]] = x[e]
+        return 0
+
+    lax.fori_loop(0, 64, gather, 0, unroll=8)
     flat = gathered.reshape(1024, 128)
     clear_first(sums, east)
 
@@ -190,7 +211,7 @@
         add_nodes(sums, east, ey, c, sub)
         return 0
 
-    lax.fori_loop(0, 8, rows, 0)
+    lax.fori_loop(0, 8, rows, 0, unroll=8)
     thin_messages(sums, east, west, north, south)
     for out in (west, east):
         for half in range(2):
@@ -290,7 +311,7 @@
         add_nodes(out, column, ey, c, sub)
         return 0
 
-    lax.fori_loop(0, 8, rows, 0)
+    lax.fori_loop(0, 8, rows, 0, unroll=8)
     if not wide:
         thin_messages(out, column, west, third, fourth)
         return
@@ -329,66 +350,101 @@
             out[k, 32:40] = jnp.where((sub < 2) | (sub >= 6), b1, roll(b2, 4))
 
 
-def laplace_rows(src, j_ref, inv, dst, first, last, sub):
-    for ii in range(3):
-        dst[3 * first, ii] = jnp.zeros((16, 128), F32)
-
-    def core(f, jac):
-        out = [None] * 16
+def laplace_core(f, jac):
+    out = [None] * 16
+    for j in range(4):
+        d = line(*[f(4 * j + i) for i in range(4)])
+        out[4 * j : 4 * j + 4] = line(*[jac(4 * j + i) * d[i] for i in range(4)])
+    for i in range(4):
+        d = line(*[f(4 * j + i) for j in range(4)])
+        d = line(*[jac(4 * j + i) * d[j] for j in range(4)])
         for j in range(4):
-            d = line(*f[4 * j : 4 * j + 4])
-            out[4 * j : 4 * j + 4] = line(*[jac(4 * j + i) * d[i] for i in range(4)])
-        for i in range(4):
-            d = line(*f[i::4])
-            d = line(*[jac(4 * j + i) * d[j] for j in range(4)])
-            for j in range(4):
-                out[4 * j + i] = out[4 * j + i] + d[j]
-        return out
-
-    def rows(r, _):
-        fa, fb = ([], [])
-        for j in range(4):
-            y = 3 * r + j
-            pa, pb = (src[y, 0, 0:8], src[y, 0, 8:16])
-            ra, rb = (roll(pa, 7), roll(pb, 7))
-            fa += [pa, src[y, 1, 0:8], src[y, 2, 0:8], jnp.where(sub == 7, rb, ra)]
-            fb += [pb, src[y, 1, 8:16], src[y, 2, 8:16], jnp.where(sub == 7, ra, rb)]
-        ca = core(fa, lambda n: j_ref[n, r, 0:8])
-        cb = core(fb, lambda n: j_ref[n, r, 8:16])
-        for j in range(4):
-            y = 3 * r + j
-            ra, rb = (roll(ca[4 * j + 3], 1), roll(cb[4 * j + 3], 1))
-            row = [
-                (ca[4 * j] + jnp.where(sub == 0, rb, ra), cb[4 * j] + jnp.where(sub == 0, ra, rb)),
-                (ca[4 * j + 1], cb[4 * j + 1]),
-                (ca[4 * j + 2], cb[4 * j + 2]),
-            ]
-            for ii in range(3):
-                a, b = row[ii]
-                if j == 0:
-                    a, b = (a + dst[y, ii, 0:8], b + dst[y, ii, 8:16])
-                if j < 3:
-                    a, b = (a * inv[y, ii, 0:8], b * inv[y, ii, 8:16])
-                dst[y, ii, 0:8] = a
-                dst[y, ii, 8:16] = b
-        return 0
-
-    lax.fori_loop(first, last, rows, 0)
-
-
-def last_kernel(
-    nodes, sums, edge, from_e, from_w, from_n, from_s, j_ref, inv, out, field, one, two, spread
-):
-    sub = sublane()
-
-    def own(y, _):
+            out[4 * j + i] = out[4 * j + i] + d[j]
+    return out
+
+
+FIRST, JOIN, SKIP = range(3)
+
+
+def laplace_row(src, j_ref, inv, dst, r, top, bottom, sub):
+    fa, fb = ([], [])
+    for j in range(4):
+        y = 3 * r + j
+        pa, pb = (src[y, 0, 0:8], src[y, 0, 8:16])
+        ra, rb = (roll(pa, 7), roll(pb, 7))
+        fa += [pa, src[y, 1, 0:8], src[y, 2, 0:8], jnp.where(sub == 7, rb, ra)]
+        fb += [pb, src[y, 1, 8:16], src[y, 2, 8:16], jnp.where(sub == 7, ra, rb)]
+    ca = laplace_core(lambda n: fa[n], lambda n: j_ref[n, r, 0:8])
+    cb = laplace_core(lambda n: fb[n], lambda n: j_ref[n, r, 8:16])
+    for j in range(4):
+        what = {0: top, 3: bottom}.get(j)
+        if what == SKIP:
+            continue
+        y = 3 * r + j
+        ra, rb = (roll(ca[4 * j + 3], 1), roll(cb[4 * j + 3], 1))
+        row = [
+            (ca[4 * j] + jnp.where(sub == 0, rb, ra), cb[4 * j] + jnp.where(sub == 0, ra, rb)),
+            (ca[4 * j + 1], cb[4 * j + 1]),
+            (ca[4 * j + 2], cb[4 * j + 2]),
+        ]
+        for ii in range(3):
+            a, b = row[ii]
+            if what == JOIN:
+                a, b = (a + dst[y, ii, 0:8], b + dst[y, ii, 8:16])
+            if what != FIRST:
+                a, b = (a * inv[y, ii, 0:8], b * inv[y, ii, 8:16])
+            dst[y, ii, 0:8] = a
+            dst[y, ii, 8:16] = b
+
+
+def own_rows(sums, edge, from_e, from_w, inv, field, first, last, sub):
+    def body(y, _):
         a0, a1, a2, b0, b1, b2 = joined_row(sums, edge, from_e, from_w, y, sub)
         for ii, (a, b) in enumerate(((a0, b0), (a1, b1), (a2, b2))):
             field[y + 6, ii, 0:8] = a * inv[y + 6, ii, 0:8]
             field[y + 6, ii, 8:16] = b * inv[y + 6, ii, 8:16]
         return 0
 
-    lax.fori_loop(0, 25, own, 0, unroll=5)
+    lax.fori_loop(first, last, body, 0)
+
+
+def inner_kernel(sums, edge, from_e, from_w, j_ref, inv, field, one, two):
+    sub = sublane()
+    own_rows(sums, edge, from_e, from_w, inv, field, 0, 25, sub)
+    laplace_row(field, j_ref, inv, one, 3, FIRST, FIRST, sub)
+
+    def rows_one(r, _):
+        laplace_row(field, j_ref, inv, one, r, JOIN, FIRST, sub)
+        return 0
+
+    lax.fori_loop(4, 9, rows_one, 0, unroll=5)
+    laplace_row(one, j_ref, inv, two, 4, FIRST, FIRST, sub)
+
+    def rows_two(r, _):
+        laplace_row(one, j_ref, inv, two, r, JOIN, FIRST, sub)
+        return 0
+
+    lax.fori_loop(5, 8, rows_two, 0, unroll=3)
+
+
+def last_kernel(
+    nodes, from_n, from_s, j_ref, inv, field_in, one_in, two_in, out, field, one, two, spread, spots
+):
+    sub = sublane()
+
+    @pl.when(pl.program_id(0) == 0)
+    def _():
+        fill_places(nodes, spots)
+
+    def copy_rows(src, dst, first, last):
+        def body(y, _):
+            for ii in range(3):
+                dst[y, ii] = src[y, ii]
+            return 0
+
+        lax.fori_loop(first, last, body, 0)
+
+    copy_rows(field_in, field, 6, 31)
     for msg, first, shared in ((from_n, 0, 6), (from_s, 30, 0)):
         for k in range(7):
             y = first + k
@@ -400,8 +456,20 @@
                     a, b = (a + field[y, ii, 0:8], b + field[y, ii, 8:16])
                 field[y, ii, 0:8] = a
                 field[y, ii, 8:16] = b
-    laplace_rows(field, j_ref, inv, one, 0, 12, sub)
-    laplace_rows(one, j_ref, inv, two, 1, 11, sub)
+    copy_rows(one_in, one, 9, 28)
+    laplace_row(field, j_ref, inv, one, 0, SKIP, FIRST, sub)
+    laplace_row(field, j_ref, inv, one, 1, JOIN, FIRST, sub)
+    laplace_row(field, j_ref, inv, one, 2, JOIN, JOIN, sub)
+    laplace_row(field, j_ref, inv, one, 9, JOIN, FIRST, sub)
+    laplace_row(field, j_ref, inv, one, 10, JOIN, FIRST, sub)
+    laplace_row(field, j_ref, inv, one, 11, JOIN, SKIP, sub)
+    copy_rows(two_in, two, 12, 25)
+    laplace_row(one, j_ref, inv, two, 1, SKIP, FIRST, sub)
+    laplace_row(one, j_ref, inv, two, 2, JOIN, FIRST, sub)
+    laplace_row(one, j_ref, inv, two, 3, JOIN, JOIN, sub)
+    laplace_row(one, j_ref, inv, two, 8, JOIN, FIRST, sub)
+    laplace_row(one, j_ref, inv, two, 9, JOIN, FIRST, sub)
+    laplace_row(one, j_ref, inv, two, 10, JOIN, SKIP, sub)
     flat = spread.reshape(1024, 128)
 
     def finish(ey, _):
@@ -422,7 +490,7 @@
     lax.fori_loop(0, 8, finish, 0)
 
     def scatter(e, _):
-        out[e] = spread[spot(nodes, e)]
+        out[e] = spread[spots[e]]
         return 0
 
     lax.fori_loop(0, 64, scatter, 0, unroll=8)
@@ -444,42 +512,58 @@
 
 PARAMS = pltpu.CompilerParams(vmem_limit_bytes=VMEM_LIMIT, dimension_semantics=("arbitrary",))
 SMEM = pl.BlockSpec(memory_space=pltpu.SMEM)
-
-
-def shifted(value, distance):
+HBM = pl.BlockSpec(memory_space=pltpu.HBM)
+
+
+def swapped(before, after, distance):
     size = lax.axis_size("sfc")
-    return lax.ppermute(value, "sfc", [((i - distance) % size, i) for i in range(size)])
+    even = (lax.axis_index("sfc") // distance) % 2 == 0
+    up = [(i, (i + distance) % size) for i in range(size) if (i // distance) % 2 == 0]
+    over = [(i, (i + distance) % size) for i in range(size) if (i // distance) % 2 == 1]
+    one = lax.ppermute(jnp.where(even, after, before), "sfc", up + [(j, i) for i, j in up])
+    two = lax.ppermute(jnp.where(even, before, after), "sfc", over + [(j, i) for i, j in over])
+    return jnp.where(even, two, one), jnp.where(even, one, two)
 
 
 def per_device(tracers, velocity, jacobian, elem_nodes):
+    nodes = elem_nodes.T
     coef = [sds(16, 8, 8, 128)] * 4 + [sds(8, 8, 128)]
     coef_specs = [fixed(16, 8, 8, 128)] * 4 + [fixed(8, 8, 128)]
     sums_spec = tiled(27, 3, 8, 128)
     first = pl.pallas_call(
         first_kernel,
         grid=(4,),
-        in_specs=[SMEM, tiled(64, 16, 128), fixed(64, 16, 128), fixed(64, 16)],
+        in_specs=[HBM, tiled(64, 16, 128), HBM, HBM],
         out_specs=[sums_spec, tiled(48, 128), tiled(48, 128), tiled(32, 128), tiled(32, 128), tiled(16, 8, 8, 128)]
         + coef_specs,
         out_shape=[sds(27, 3, 8, 512), sds(48, 512), sds(48, 512), sds(32, 512), sds(32, 512), sds(16, 8, 8, 512)]
         + coef,
-        scratch_shapes=[pltpu.VMEM((64, 16, 128), F32), pltpu.VMEM((64, 128), F32)],
+        scratch_shapes=[
+            pltpu.VMEM((64, 16, 128), F32),
+            pltpu.VMEM((64, 16, 128), F32),
+            pltpu.VMEM((64, 128), F32),
+            pltpu.VMEM((16, 64), jnp.int32),
+            pltpu.VMEM((16, 64), F32),
+            pltpu.SMEM((16, 64), jnp.int32),
+            pltpu.SMEM((64,), jnp.int32),
+            pltpu.SemaphoreType.DMA((4,)),
+        ],
         compiler_params=PARAMS,
         name="section_one_sums",
     )
-    sums, west, east, north, south, t0, *coefs = first(elem_nodes, tracers, velocity, jacobian)
+    sums, west, east, north, south, t0, *coefs = first(nodes, tracers, velocity, jacobian.T)
 
     row = lax.broadcasted_iota(jnp.int32, (32, 1), 0)
 
     def corrected(own, from_w, from_e, y):
         return own + jnp.where(row == 0, from_w[y : y + 1], 0.0) + jnp.where(row >= 24, from_e[y : y + 1], 0.0)
 
-    from_e, from_w = (shifted(west, -1), shifted(east, 1))
+    from_w, from_e = swapped(west, east, 1)
     low = lax.broadcasted_iota(jnp.int32, (8, 1), 0) < 4
     beside = [jnp.where(low, from_e[k : k + 8], from_w[k : k + 8]) for k in (32, 40)]
     msg_n = jnp.concatenate([corrected(north, from_w, from_e, 0), west[32:40], beside[0]])
     msg_s = jnp.concatenate([corrected(south, from_w, from_e, 24), west[40:48], beside[1]])
-    from_s, from_n = (shifted(msg_n, -PX), shifted(msg_s, PX))
+    from_n, from_s = swapped(msg_n, msg_s, PX)
 
     whole = pl.BlockSpec(memory_space=pltpu.VMEM)
     jac, inv = pl.pallas_call(
@@ -516,15 +600,15 @@
     sums, west, east, north, south = stage(
         0.75, 0.25, False, sums, east, from_e, from_w, from_n, from_s, 48
     )
-    from_e, from_w = (shifted(west, -1), shifted(east, 1))
+    from_w, from_e = swapped(west, east, 1)
     msg_n = corrected(north, from_w, from_e, 0)
     msg_s = corrected(south, from_w, from_e, 24)
-    from_s, from_n = (shifted(msg_n, -PX), shifted(msg_s, PX))
+    from_n, from_s = swapped(msg_n, msg_s, PX)
 
     sums, west, east, _, edge = stage(
         1.0 / 3.0, 2.0 / 3.0, True, sums, east, from_e, from_w, from_n, from_s, 32
     )
-    from_e, from_w = (shifted(west, -1), shifted(east, 1))
+    from_w, from_e = swapped(west, east, 1)
     message = tiled(25, 8, 128)
     band = tiled(7, 40, 128)
     msg_n, msg_s = pl.pallas_call(
@@ -536,17 +620,30 @@
         compiler_params=PARAMS,
         name="row_bands",
     )(sums, edge, from_e, from_w)
-    from_s, from_n = (shifted(msg_n, -PX), shifted(msg_s, PX))
+    from_n, from_s = swapped(msg_n, msg_s, PX)
+    grown = tiled(37, 3, 16, 128)
+    flops = 64 * 16 * 512 * 60
+    field, one, two = pl.pallas_call(
+        inner_kernel,
+        grid=(4,),
+        in_specs=[sums_spec, tiled(32, 128), message, message, jac_spec, inv_spec],
+        out_specs=[grown] * 3,
+        out_shape=[sds(37, 3, 16, 512)] * 3,
+        compiler_params=PARAMS,
+        cost_estimate=pl.CostEstimate(flops=flops, bytes_accessed=16 * 1024 * 1024, transcendentals=0),
+        name="biharmonic_inner_rows",
+    )(sums, edge, from_e, from_w, jac, inv)
     return pl.pallas_call(
         last_kernel,
         grid=(4,),
-        in_specs=[SMEM, sums_spec, tiled(32, 128), message, message, band, band, jac_spec, inv_spec],
+        in_specs=[SMEM, band, band, jac_spec, inv_spec] + [grown] * 3,
         out_specs=tiled(64, 16, 128),
         out_shape=sds(64, 16, 512),
-        scratch_shapes=[pltpu.VMEM((37, 3, 16, 128), F32)] * 3 + [pltpu.VMEM((64, 16, 128), F32)],
+        scratch_shapes=[pltpu.VMEM((37, 3, 16, 128), F32)] * 3
+        + [pltpu.VMEM((64, 16, 128), F32), pltpu.SMEM((64,), jnp.int32)],
         compiler_params=PARAMS,
-        name="biharmonic",
-    )(elem_nodes, sums, edge, from_e, from_w, from_n, from_s, jac, inv)
+        name="biharmonic_outer_rows",
+    )(nodes, from_n, from_s, jac, inv, field, one, two)
 
 
 def solution(mesh):

time: 118 us -> 98 us (0.83)
  waiting for transfers between devices: 46.2 us -> 34 us
  starting transfers between devices: 27.8 us -> 22.6 us
  Pallas kernels: 39.7 us -> 35.3 us
    ppermute x12, waiting for transfers between devices: 46.2 us -> 34 us  [the longest x6 25 us: swapped(): lax.ppermute(jnp.where(even, before, after), 'sfc', over + [(j, i) for i,...]
    ppermute x12, starting transfers between devices: 27.8 us -> 22.6 us  [the longest x6 22.3 us: swapped(): lax.ppermute(jnp.where(even, before, after), 'sfc', over + [(j, i) for i,...]
    pallas_call x2 -> x3, Pallas kernels: 27.9 us -> 24.4 us  [the longest x1 10.3 us: per_device(): pl.pallas_call(last_kernel, grid=(4,), in_specs=[SMEM, band, band, jac_sp...]
    unnamed x8 -> x12, local copies, waits for them, and re-layouts: 3.68 us -> 4.63 us
  transfers between devices with their start and end apart: 12 -> 12, of which waited for: 9 -> 9; matrix products, arithmetic and copies ran while one was open for 0% -> 0% of each run, Pallas kernels for 0% -> 7%
where the time goes in v2:
time: 98 us; the launch traced here: 97.4 us
  Pallas kernels  35.3 us (36%)
  waiting for transfers between devices  34 us (35%)
  starting transfers between devices  22.6 us (23%)
  local copies, waits for them, and re-layouts  4.65 us (5%)
    ppermute x6, waiting for transfers between devices, swapped(): lax.ppermute(jnp.where(even, before, after), 'sfc', over + [(j, i) for i,...  25 us
    ppermute x6, starting transfers between devices, swapped(): lax.ppermute(jnp.where(even, before, after), 'sfc', over + [(j, i) for i,...  22.3 us
    pallas_call x1, Pallas kernels, per_device(): pl.pallas_call(last_kernel, grid=(4,), in_specs=[SMEM, band, band, jac_sp...  10.3 us
    pallas_call x2, Pallas kernels, stage(): pl.pallas_call(functools.partial(stage_kernel, keep, take, wide), grid=(4...  9.51 us
    ppermute x6, waiting for transfers between devices, swapped(): lax.ppermute(jnp.where(even, after, before), 'sfc', up + [(j, i) for i, j...  9.03 us
    pallas_call x1, Pallas kernels, per_device(): first(nodes, tracers, velocity, jacobian.T)  7.51 us
    pallas_call x1, Pallas kernels, per_device(): pl.pallas_call(inner_kernel, grid=(4,), in_specs=[sums_spec, tiled(32, 12...  6.56 us
    unnamed x12, local copies, waits for them, and re-layouts  4.63 us
  transfers between devices with their start and end apart: 12, of which 9 were waited for; matrix products, arithmetic and copies ran while one was open for 0% of the time, Pallas kernels for 7%

profile of v2, /device:TPU:0, one launch (start us, length us, event | category | flops | bytes accessed | tf_op | source)
XLA Modules:
  0.0 97.4 jit_solution(5087144470824673290)
XLA Ops:
  0.0 1.0 %copy-done.2 = f32[64,16,128]{2,1,0:T(8,128)S(1)} copy-done((f32[64,16,128]{2,1,0:T(8,128)S(1)}, f32[64,16,128]{2,1,0:T(8,128)}, u32[]{:S(2)}) %copy-start.2) | copy-done | bytes 524312
  1.0 0.7 copy-done.3
  1.7 0.7 copy-done.5
  2.4 7.5 %section_one_sums.1 = (f32[27,3,8,512]{3,2,1,0:T(8,128)S(1)}, f32[48,512]{1,0:T(8,128)S(1)}, f32[48,512]{1,0:T(8,128)S(1)}, f32[32,512]{1,0:T(8,128)S(1)}, f32[3...) custom-call(s32[16,64]{1,0:T(8,128)S(1)} %bitcast.10, ...), custom_call_target="tpu_custom_call" | custom-call | tf_op jit(solution)/shard_map/section_one_sums/pallas_call | solution.py:554
  10.0 1.1 %copy-done.1 = f32[27,3,8,512]{3,2,1,0:T(8,128)} copy-done((f32[27,3,8,512]{3,2,1,0:T(8,128)}, f32[27,3,8,512]{3,2,1,0:T(8,128)S(1)}, u32[]{:S(2)}) %copy-start.1) | copy-done | bytes 1327128
  11.1 8.3 %collective-permute-start.1 = (f32[48,512]{1,0:T(8,128)S(1)}, f32[48,512]{1,0:T(8,128)S(1)}, u32[]{:S(2)}, u32[]{:S(2)}) collective-permute-start(f32[48,512]{1,0:T(8,128)S(1)} %get-tuple-element.75), channel_id=1, source_target_pairs={{1,2},{3,4},{5,6},{7,8},{9,10},{11,12},{13,14},{15,16},{17,18},{19... | collective-permute-start | bytes 294920 | tf_op jit(solution)/shard_map/ppermute | solution.py:524
  19.4 2.3 %collective-permute-done.1 = f32[48,512]{1,0:T(8,128)S(1)} collective-permute-done((f32[48,512]{1,0:T(8,128)S(1)}, f32[48,512]{1,0:T(8,128)S(1)}, u32[]{:S(2)}, u32[]{:S(2)}) %collective-permute-start.1) | collective-permute-done | bytes 98336 | tf_op jit(solution)/shard_map/ppermute | solution.py:524
  22.0 2.8 %collective-permute-start.2 = (f32[48,512]{1,0:T(8,128)S(1)}, f32[48,512]{1,0:T(8,128)S(1)}, u32[]{:S(2)}, u32[]{:S(2)}) collective-permute-start(f32[48,512]{1,0:T(8,128)S(1)} %get-tuple-element.72), channel_id=1, source_target_pairs={{8,16},{9,17},{10,18},{11,19},{12,20},{13,21},{14,22},{15,23},{24,... | collective-permute-start | bytes 294920 | tf_op jit(solution)/shard_map/ppermute | solution.py:524
  24.8 1.8 %collective-permute-done.3 = f32[48,512]{1,0:T(8,128)S(1)} collective-permute-done((f32[48,512]{1,0:T(8,128)S(1)}, f32[48,512]{1,0:T(8,128)S(1)}, u32[]{:S(2)}, u32[]{:S(2)}) %collective-permute-start.3) | collective-permute-done | bytes 98336 | tf_op jit(solution)/shard_map/ppermute | solution.py:523
  26.6 3.4 %collective-permute-done.2 = f32[48,512]{1,0:T(8,128)S(1)} collective-permute-done((f32[48,512]{1,0:T(8,128)S(1)}, f32[48,512]{1,0:T(8,128)S(1)}, u32[]{:S(2)}, u32[]{:S(2)}) %collective-permute-start.2) | collective-permute-done | bytes 98336 | tf_op jit(solution)/shard_map/ppermute | solution.py:524
  30.0 0.8 geometry.1
  30.8 4.4 %section_two_sums.1 = (f32[27,3,8,512]{3,2,1,0:T(8,128)S(1)}, f32[32,512]{1,0:T(8,128)S(1)}, f32[32,512]{1,0:T(8,128)S(1)}, f32[32,512]{1,0:T(8,128)S(1)}, f32[32,512]{1,0:T(8,128)S(1)}) custom-call(f32[27,3,8,512]{3,2,1,0:T(8,128)} %copy-done.1, f32[48,512]{1,0:T(8,128)S(1)} %get-tuple-element.33.edge, f32[48,512]{1,0:T(8,128)S(1)} %get-tuple-element.74.from_e, ...), custom_call_target="tpu_custom_call" | custom-call | tf_op jit(solution)/shard_map/section_two_sums/pallas_call | solution.py:586
  35.2 1.1 %copy-done = f32[27,3,8,512]{3,2,1,0:T(8,128)} copy-done((f32[27,3,8,512]{3,2,1,0:T(8,128)}, f32[27,3,8,512]{3,2,1,0:T(8,128)S(1)}, u32[]{:S(2)}) %copy-start) | copy-done | bytes 1327128
  36.3 6.1 %collective-permute-start.5 = (f32[32,512]{1,0:T(8,128)S(1)}, f32[32,512]{1,0:T(8,128)S(1)}, u32[]{:S(2)}, u32[]{:S(2)}) collective-permute-start(f32[32,512]{1,0:T(8,128)S(1)} %get-tuple-element.83), channel_id=1, source_target_pairs={{1,2},{3,4},{5,6},{7,8},{9,10},{11,12},{13,14},{15,16},{17,18},{19... | collective-permute-start | bytes 196616 | tf_op jit(solution)/shard_map/ppermute | solution.py:524
  42.4 3.1 %collective-permute-done.5 = f32[32,512]{1,0:T(8,128)S(1)} collective-permute-done((f32[32,512]{1,0:T(8,128)S(1)}, f32[32,512]{1,0:T(8,128)S(1)}, u32[]{:S(2)}, u32[]{:S(2)}) %collective-permute-start.5) | collective-permute-done | bytes 65568 | tf_op jit(solution)/shard_map/ppermute | solution.py:524
  45.9 4.2 %collective-permute-done.7 = f32[32,512]{1,0:T(8,128)S(1)} collective-permute-done((f32[32,512]{1,0:T(8,128)S(1)}, f32[32,512]{1,0:T(8,128)S(1)}, u32[]{:S(2)}, u32[]{:S(2)}) %collective-permute-start.7) | collective-permute-done | bytes 65568 | tf_op jit(solution)/shard_map/ppermute | solution.py:523
  50.0 3.4 %collective-permute-done.6 = f32[32,512]{1,0:T(8,128)S(1)} collective-permute-done((f32[32,512]{1,0:T(8,128)S(1)}, f32[32,512]{1,0:T(8,128)S(1)}, u32[]{:S(2)}, u32[]{:S(2)}) %collective-permute-start.6) | collective-permute-done | bytes 65568 | tf_op jit(solution)/shard_map/ppermute | solution.py:524
  53.5 5.1 %section_three_sums.1 = (f32[27,3,8,512]{3,2,1,0:T(8,128)S(1)}, f32[25,8,512]{2,1,0:T(8,128)S(1)}, f32[25,8,512]{2,1,0:T(8,128)S(1)}, f32[8,512]{1,0:T(8,128)}, f32[32,512]{1,0:T(8,128)S(1)}) custom-call(f32[27,3,8,512]{3,2,1,0:T(8,128)} %copy-done, f32[32,512]{1,0:T(8,128)S(1)} %get-tuple-element.45.edge, f32[32,512]{1,0:T(8,128)S(1)} %get-tuple-element.82.from_e, ...), custom_call_target="tpu_custom_call" | custom-call | tf_op jit(solution)/shard_map/section_three_sums/pallas_call | solution.py:586
  58.7 5.0 %collective-permute-start.9 = (f32[25,8,512]{2,1,0:T(8,128)S(1)}, f32[25,8,512]{2,1,0:T(8,128)S(1)}, u32[]{:S(2)}, u32[]{:S(2)}) collective-permute-start(f32[25,8,512]{2,1,0:T(8,128)S(1)} %get-tuple-element.65), channel_id=1, source_target_pairs={{1,2},{3,4},{5,6},{7,8},{9,10},{11,12},{13,14},{15,16},{17,18},{19... | collective-permute-start | bytes 1228808 | tf_op jit(solution)/shard_map/ppermute | solution.py:524
  63.6 9.3 %collective-permute-done.9 = f32[25,8,512]{2,1,0:T(8,128)S(1)} collective-permute-done((f32[25,8,512]{2,1,0:T(8,128)S(1)}, f32[25,8,512]{2,1,0:T(8,128)S(1)}, u32[]{:S(2)}, u32[]{:S(2)}) %collective-permute-start.9) | collective-permute-done | bytes 409632 | tf_op jit(solution)/shard_map/ppermute | solution.py:524
  74.0 6.6 %biharmonic_inner_rows.1 = (f32[37,3,16,512]{3,2,1,0:T(8,128)}, f32[37,3,16,512]{3,2,1,0:T(8,128)}, f32[37,3,16,512]{3,2,1,0:T(8,128)}) custom-call(f32[27,3,8,512]{3,2,1,0:T(8,128)S(1)} %get-tuple-element.49.sums, f32[32,512]{1,0:T(8,128)S(1)} %get-tuple-element.50.edge, f32[25,8,512]{2,1,0:T(8,128)S(1)} %get-tuple-element.64.from_e, ...), custom_call_target="tpu_custom_call" | custom-call | flops 31457280 | bytes 16777216 | tf_op jit(solution)/shard_map/biharmonic_inner_rows/pallas_call | solution.py:626
  80.6 3.0 %collective-permute-done.11 = f32[7,40,512]{2,1,0:T(8,128)S(1)} collective-permute-done((f32[7,40,512]{2,1,0:T(8,128)S(1)}, f32[7,40,512]{2,1,0:T(8,128)S(1)}, u32[]{:S(2)}, u32[]{:S(2)}) %collective-permute-start.11) | collective-permute-done | bytes 573472 | tf_op jit(solution)/shard_map/ppermute | solution.py:523
  83.6 3.4 %collective-permute-done.10 = f32[7,40,512]{2,1,0:T(8,128)S(1)} collective-permute-done((f32[7,40,512]{2,1,0:T(8,128)S(1)}, f32[7,40,512]{2,1,0:T(8,128)S(1)}, u32[]{:S(2)}, u32[]{:S(2)}) %collective-permute-start.10) | collective-permute-done | bytes 573472 | tf_op jit(solution)/shard_map/ppermute | solution.py:524
  87.1 10.3 %biharmonic_outer_rows.1 = f32[64,16,512]{2,1,0:T(8,128)} custom-call(s32[16,64]{1,0:T(8,128)S(1)} %bitcast.11, f32[7,40,512]{2,1,0:T(8,128)S(1)} %get-tuple-element.60.from_n, f32[7,40,512]{2,1,0:T(8,128)S(1)} %get-tuple-element.59.from_s, f32[16,12,16,128]{3,2,1,0:T(8,128)S(1)} %get-tuple-element.55.j_ref, f32[37,3,16,128]{3,2,1,0:T(8,128)S(1)} %get-tuple-element.37.inv, ...), custom_call_target="tpu_custom_call" | custom-call | tf_op jit(solution)/shard_map/biharmonic_outer_rows/pallas_call | solution.py:636
  (39 shorter events, 1.8 us)
Async XLA Ops:
  0.0 1.0 %copy-start.2 = (f32[64,16,128]{2,1,0:T(8,128)S(1)}, f32[64,16,128]{2,1,0:T(8,128)}, u32[]{:S(2)}) copy-start(f32[64,16,128]{2,1,0:T(8,128)} %vel.1) | copy-start | bytes 1572868
  1.0 0.7 copy-start.3
  1.7 0.7 copy-start.5
  10.0 1.1 %copy-start.1 = (f32[27,3,8,512]{3,2,1,0:T(8,128)}, f32[27,3,8,512]{3,2,1,0:T(8,128)S(1)}, u32[]{:S(2)}) copy-start(f32[27,3,8,512]{3,2,1,0:T(8,128)S(1)} %get-tuple-element.32.sums) | copy-start | bytes 3981316
  11.1 10.6 %collective-permute-start.1 = (f32[48,512]{1,0:T(8,128)S(1)}, f32[48,512]{1,0:T(8,128)S(1)}, u32[]{:S(2)}, u32[]{:S(2)}) collective-permute-start(f32[48,512]{1,0:T(8,128)S(1)} %get-tuple-element.75), channel_id=1, source_target_pairs={{1,2},{3,4},{5,6},{7,8},{9,10},{11,12},{13,14},{15,16},{17,18},{19... | collective-permute-start | bytes 294920 | tf_op jit(solution)/shard_map/ppermute | solution.py:524
  19.4 2.3 %collective-permute-start = (f32[48,512]{1,0:T(8,128)S(1)}, f32[48,512]{1,0:T(8,128)S(1)}, u32[]{:S(2)}, u32[]{:S(2)}) collective-permute-start(f32[48,512]{1,0:T(8,128)S(1)} %get-tuple-element.76), channel_id=1, source_target_pairs={{0,1},{2,3},{4,5},{6,7},{8,9},{10,11},{12,13},{14,15},{16,17},{18,... | collective-permute-start | bytes 294920 | tf_op jit(solution)/shard_map/ppermute | solution.py:523
  21.9 4.7 %collective-permute-start.3 = (f32[48,512]{1,0:T(8,128)S(1)}, f32[48,512]{1,0:T(8,128)S(1)}, u32[]{:S(2)}, u32[]{:S(2)}) collective-permute-start(f32[48,512]{1,0:T(8,128)S(1)} %get-tuple-element.71), channel_id=1, source_target_pairs={{0,8},{1,9},{2,10},{3,11},{4,12},{5,13},{6,14},{7,15},{16,24},{17,... | collective-permute-start | bytes 294920 | tf_op jit(solution)/shard_map/ppermute | solution.py:523
  22.0 8.0 %collective-permute-start.2 = (f32[48,512]{1,0:T(8,128)S(1)}, f32[48,512]{1,0:T(8,128)S(1)}, u32[]{:S(2)}, u32[]{:S(2)}) collective-permute-start(f32[48,512]{1,0:T(8,128)S(1)} %get-tuple-element.72), channel_id=1, source_target_pairs={{8,16},{9,17},{10,18},{11,19},{12,20},{13,21},{14,22},{15,23},{24,... | collective-permute-start | bytes 294920 | tf_op jit(solution)/shard_map/ppermute | solution.py:524
  35.2 1.1 %copy-start = (f32[27,3,8,512]{3,2,1,0:T(8,128)}, f32[27,3,8,512]{3,2,1,0:T(8,128)S(1)}, u32[]{:S(2)}) copy-start(f32[27,3,8,512]{3,2,1,0:T(8,128)S(1)} %get-tuple-element.44.sums) | copy-start | bytes 3981316
  36.3 9.2 %collective-permute-start.5 = (f32[32,512]{1,0:T(8,128)S(1)}, f32[32,512]{1,0:T(8,128)S(1)}, u32[]{:S(2)}, u32[]{:S(2)}) collective-permute-start(f32[32,512]{1,0:T(8,128)S(1)} %get-tuple-element.83), channel_id=1, source_target_pairs={{1,2},{3,4},{5,6},{7,8},{9,10},{11,12},{13,14},{15,16},{17,18},{19... | collective-permute-start | bytes 196616 | tf_op jit(solution)/shard_map/ppermute | solution.py:524
  42.4 3.1 %collective-permute-start.4 = (f32[32,512]{1,0:T(8,128)S(1)}, f32[32,512]{1,0:T(8,128)S(1)}, u32[]{:S(2)}, u32[]{:S(2)}) collective-permute-start(f32[32,512]{1,0:T(8,128)S(1)} %get-tuple-element.84), channel_id=1, source_target_pairs={{0,1},{2,3},{4,5},{6,7},{8,9},{10,11},{12,13},{14,15},{16,17},{18,... | collective-permute-start | bytes 196616 | tf_op jit(solution)/shard_map/ppermute | solution.py:523
  45.7 4.3 %collective-permute-start.7 = (f32[32,512]{1,0:T(8,128)S(1)}, f32[32,512]{1,0:T(8,128)S(1)}, u32[]{:S(2)}, u32[]{:S(2)}) collective-permute-start(f32[32,512]{1,0:T(8,128)S(1)} %get-tuple-element.77), channel_id=1, source_target_pairs={{0,8},{1,9},{2,10},{3,11},{4,12},{5,13},{6,14},{7,15},{16,24},{17,... | collective-permute-start | bytes 196616 | tf_op jit(solution)/shard_map/ppermute | solution.py:523
  45.8 7.7 %collective-permute-start.6 = (f32[32,512]{1,0:T(8,128)S(1)}, f32[32,512]{1,0:T(8,128)S(1)}, u32[]{:S(2)}, u32[]{:S(2)}) collective-permute-start(f32[32,512]{1,0:T(8,128)S(1)} %get-tuple-element.78), channel_id=1, source_target_pairs={{8,16},{9,17},{10,18},{11,19},{12,20},{13,21},{14,22},{15,23},{24,... | collective-permute-start | bytes 196616 | tf_op jit(solution)/shard_map/ppermute | solution.py:524
  58.7 14.3 %collective-permute-start.9 = (f32[25,8,512]{2,1,0:T(8,128)S(1)}, f32[25,8,512]{2,1,0:T(8,128)S(1)}, u32[]{:S(2)}, u32[]{:S(2)}) collective-permute-start(f32[25,8,512]{2,1,0:T(8,128)S(1)} %get-tuple-element.65), channel_id=1, source_target_pairs={{1,2},{3,4},{5,6},{7,8},{9,10},{11,12},{13,14},{15,16},{17,18},{19... | collective-permute-start | bytes 1228808 | tf_op jit(solution)/shard_map/ppermute | solution.py:524
  63.6 9.4 %collective-permute-start.8 = (f32[25,8,512]{2,1,0:T(8,128)S(1)}, f32[25,8,512]{2,1,0:T(8,128)S(1)}, u32[]{:S(2)}, u32[]{:S(2)}) collective-permute-start(f32[25,8,512]{2,1,0:T(8,128)S(1)} %get-tuple-element.66), channel_id=1, source_target_pairs={{0,1},{2,3},{4,5},{6,7},{8,9},{10,11},{12,13},{14,15},{16,17},{18,... | collective-permute-start | bytes 1228808 | tf_op jit(solution)/shard_map/ppermute | solution.py:523
  73.8 9.8 %collective-permute-start.11 = (f32[7,40,512]{2,1,0:T(8,128)S(1)}, f32[7,40,512]{2,1,0:T(8,128)S(1)}, u32[]{:S(2)}, u32[]{:S(2)}) collective-permute-start(f32[7,40,512]{2,1,0:T(8,128)S(1)} %get-tuple-element.61), channel_id=1, source_target_pairs={{0,8},{1,9},{2,10},{3,11},{4,12},{5,13},{6,14},{7,15},{16,24},{17,... | collective-permute-start | bytes 1720328 | tf_op jit(solution)/shard_map/ppermute | solution.py:523
  73.9 13.1 %collective-permute-start.10 = (f32[7,40,512]{2,1,0:T(8,128)S(1)}, f32[7,40,512]{2,1,0:T(8,128)S(1)}, u32[]{:S(2)}, u32[]{:S(2)}) collective-permute-start(f32[7,40,512]{2,1,0:T(8,128)S(1)} %get-tuple-element.62), channel_id=1, source_target_pairs={{8,16},{9,17},{10,18},{11,19},{12,20},{13,21},{14,22},{15,23},{24,... | collective-permute-start | bytes 1720328 | tf_op jit(solution)/shard_map/ppermute | solution.py:524
  80.6 6.6 %copy-start.4 = (s32[64,16]{0,1:T(8,128)S(1)}, s32[64,16]{0,1:T(8,128)}, u32[]{:S(2)}) copy-start(s32[64,16]{0,1:T(8,128)} %param.7) | copy-start | bytes 12292

commit v3 on v2

--- a/solution.py
+++ b/solution.py
@@ -12,7 +12,8 @@
 STEP_SIZE = 0.04
 DIFFUSION = 0.0001
 F32 = jnp.float32
-VMEM_LIMIT = 48 * 1024 * 1024
+VMEM_LIMIT = 36 * 1024 * 1024
+FIRST_LIMIT = 52 * 1024 * 1024
 
 
 def gll_derivative():
@@ -92,13 +93,13 @@
     return [jac[n] * (mean + scaling * (g[n] - mean)) for n in range(16)]
 
 
-def add_nodes(sums, edge, ey, c, sub):
+def add_nodes(sums, edge, ey, c, sub, joins=(0,)):
     for j in range(4):
         c0, c1, c2, c3 = c[4 * j : 4 * j + 4]
         c0 = c0 + jnp.where(sub == 0, 0.0, roll(c3, 1))
         last = c3[7:8, :]
         y = 3 * ey + j
-        if j == 0:
+        if j in joins:
             c0, c1, c2 = (c0 + sums[y, 0], c1 + sums[y, 1], c2 + sums[y, 2])
             last = last + edge[pl.ds(y, 1), :]
         sums[y, 0] = c0
@@ -107,10 +108,10 @@
         edge[pl.ds(y, 1), :] = last
 
 
-def clear_first(sums, edge):
+def clear_first(sums, edge, y=0):
     for ii in range(3):
-        sums[0, ii] = jnp.zeros((8, 128), F32)
-    edge[0:1, :] = jnp.zeros((1, 128), F32)
+        sums[y, ii] = jnp.zeros((8, 128), F32)
+    edge[y : y + 1, :] = jnp.zeros((1, 128), F32)
 
 
 def thin_messages(sums, edge, west, north, south):
@@ -220,14 +221,22 @@
             ]
 
 
+def own_geometry_kernel(own, from_e, from_w, inv):
+    geometry_rows(own, from_e, from_w, None, None, None, inv, 0, 8)
+
+
 def geometry_kernel(own, from_e, from_w, from_n, from_s, j_ref, inv):
+    geometry_rows(own, from_e, from_w, from_n, from_s, j_ref, inv, -3, 11)
+
+
+def geometry_rows(own, from_e, from_w, from_n, from_s, j_ref, inv, first, last):
     sub = sublane()
 
     def tile(ref, base, t):
         return ref[base : base + 8, 128 * t : 128 * t + 128]
 
     pending = None
-    for r in range(-3, 11):
+    for r in range(first, last):
         if r < 0:
             t = r + 4
             a, b = (tile(from_n, 32, t), tile(from_n, 40, t))
@@ -242,7 +251,7 @@
         for j in range(4):
             ca = [jnp.broadcast_to(a[:, 4 * j + i : 4 * j + i + 1], (8, 128)) for i in range(4)]
             cb = [jnp.broadcast_to(b[:, 4 * j + i : 4 * j + i + 1], (8, 128)) for i in range(4)]
-            if -2 <= r <= 9:
+            if j_ref is not None and -2 <= r <= 9:
                 for i in range(4):
                     j_ref[4 * j + i, r + 2, 0:8] = ca[i]
                     j_ref[4 * j + i, r + 2, 8:16] = cb[i]
@@ -268,7 +277,7 @@
         pending = kept
 
 
-def node_values(sums, edge, from_e, from_w, from_n, from_s, inv, whole, side, sub):
+def node_values(sums, edge, from_e, from_w, inv, whole, side, first, last, sub):
     def body(y, _):
         whole[y, 0] = (sums[y, 0] + jnp.where(sub == 0, row8(from_w, y), 0.0)) * inv[y + 6, 0, 0:8]
         whole[y, 1] = sums[y, 1] * inv[y + 6, 1, 0:8]
@@ -276,11 +285,13 @@
         side[pl.ds(y, 1), :] = (edge[pl.ds(y, 1), :] + from_e[pl.ds(y, 1), :]) * inv[y + 6, 0, 8:9]
         return 0
 
-    lax.fori_loop(0, 25, body, 0, unroll=5)
-    for y, msg in ((0, from_n), (24, from_s)):
-        for ii in range(3):
-            whole[y, ii] = whole[y, ii] + msg[8 * ii : 8 * ii + 8, :] * inv[y + 6, ii, 0:8]
-        side[y : y + 1, :] = side[y : y + 1, :] + msg[24:25, :] * inv[y + 6, 0, 8:9]
+    lax.fori_loop(first, last, body, 0, unroll=4)
+
+
+def add_row(whole, side, msg, inv, y):
+    for ii in range(3):
+        whole[y, ii] = whole[y, ii] + msg[8 * ii : 8 * ii + 8, :] * inv[y + 6, ii, 0:8]
+    side[y : y + 1, :] = side[y : y + 1, :] + msg[24:25, :] * inv[y + 6, 0, 8:9]
 
 
 def element_values(whole, side, ey, sub):
@@ -292,26 +303,49 @@
     return f
 
 
+def stage_row(keep, take, whole, side, t0, u_ref, v_ref, rj_ref, j_ref, rd_ref, ey, sub):
+    f = element_values(whole, side, ey, sub)
+    h = tendency_step(f, lambda n: u_ref[n, ey], lambda n: v_ref[n, ey], lambda n: rj_ref[n, ey])
+    g = [keep * t0[n, ey] + take * h[n] for n in range(16)]
+    return limited(g, [j_ref[n, ey] for n in range(16)], rd_ref[ey])
+
+
+def stage_inner_kernel(
+    keep, take, sums, edge, from_e, from_w, inv, t0, u_ref, v_ref, rj_ref, j_ref, rd_ref, out, column, whole, side
+):
+    sub = sublane()
+    node_values(sums, edge, from_e, from_w, inv, whole, side, 3, 22, sub)
+    clear_first(out, column, 3)
+
+    def rows(ey, _):
+        c = stage_row(keep, take, whole, side, t0, u_ref, v_ref, rj_ref, j_ref, rd_ref, ey, sub)
+        add_nodes(out, column, ey, c, sub)
+        return 0
+
+    lax.fori_loop(1, 7, rows, 0, unroll=6)
+
+
 def stage_kernel(
     keep, take, wide, sums, edge, from_e, from_w, from_n, from_s, inv, t0, u_ref, v_ref, rj_ref, j_ref, rd_ref,
-    out, west, east, third, fourth, whole, side,
+    inner, inner_column, out, west, east, third, fourth, whole, side,
 ):
     sub = sublane()
-    node_values(sums, edge, from_e, from_w, from_n, from_s, inv, whole, side, sub)
+    node_values(sums, edge, from_e, from_w, inv, whole, side, 0, 4, sub)
+    node_values(sums, edge, from_e, from_w, inv, whole, side, 21, 25, sub)
+    add_row(whole, side, from_n, inv, 0)
+    add_row(whole, side, from_s, inv, 24)
     column = fourth if wide else east
-    clear_first(out, column)
-
-    def rows(ey, _):
-        f = element_values(whole, side, ey, sub)
-        h = tendency_step(
-            f, lambda n: u_ref[n, ey], lambda n: v_ref[n, ey], lambda n: rj_ref[n, ey]
-        )
-        g = [keep * t0[n, ey] + take * h[n] for n in range(16)]
-        c = limited(g, [j_ref[n, ey] for n in range(16)], rd_ref[ey])
-        add_nodes(out, column, ey, c, sub)
-        return 0
-
-    lax.fori_loop(0, 8, rows, 0, unroll=8)
+
+    def copy(y, _):
+        for ii in range(3):
+            out[y, ii] = inner[y, ii]
+        column[pl.ds(y, 1), :] = inner_column[pl.ds(y, 1), :]
+        return 0
+
+    lax.fori_loop(3, 22, copy, 0, unroll=19)
+    for ey, joins in ((0, (3,)), (7, (0,))):
+        c = stage_row(keep, take, whole, side, t0, u_ref, v_ref, rj_ref, j_ref, rd_ref, ey, sub)
+        add_nodes(out, column, ey, c, sub, joins)
     if not wide:
         thin_messages(out, column, west, third, fourth)
         return
@@ -366,10 +400,10 @@
 FIRST, JOIN, SKIP = range(3)
 
 
-def laplace_row(src, j_ref, inv, dst, r, top, bottom, sub):
+def laplace_row(src, j_ref, inv, dst, r, top, bottom, sub, at=(0, 0), narrow=False):
     fa, fb = ([], [])
     for j in range(4):
-        y = 3 * r + j
+        y = 3 * r + j - at[0]
         pa, pb = (src[y, 0, 0:8], src[y, 0, 8:16])
         ra, rb = (roll(pa, 7), roll(pb, 7))
         fa += [pa, src[y, 1, 0:8], src[y, 2, 0:8], jnp.where(sub == 7, rb, ra)]
@@ -387,22 +421,24 @@
             (ca[4 * j + 1], cb[4 * j + 1]),
             (ca[4 * j + 2], cb[4 * j + 2]),
         ]
+        z = y - at[1]
         for ii in range(3):
-            a, b = row[ii]
-            if what == JOIN:
-                a, b = (a + dst[y, ii, 0:8], b + dst[y, ii, 8:16])
-            if what != FIRST:
-                a, b = (a * inv[y, ii, 0:8], b * inv[y, ii, 8:16])
-            dst[y, ii, 0:8] = a
-            dst[y, ii, 8:16] = b
+            for part, rows in zip(row[ii], (slice(0, 8), slice(8, 16))):
+                if narrow and ii and rows.start:
+                    continue
+                if what == JOIN:
+                    part = part + dst[z, ii, rows]
+                if what != FIRST:
+                    part = part * inv[y, ii, rows]
+                dst[z, ii, rows] = part
 
 
 def own_rows(sums, edge, from_e, from_w, inv, field, first, last, sub):
     def body(y, _):
         a0, a1, a2, b0, b1, b2 = joined_row(sums, edge, from_e, from_w, y, sub)
         for ii, (a, b) in enumerate(((a0, b0), (a1, b1), (a2, b2))):
-            field[y + 6, ii, 0:8] = a * inv[y + 6, ii, 0:8]
-            field[y + 6, ii, 8:16] = b * inv[y + 6, ii, 8:16]
+            field[y, ii, 0:8] = a * inv[y + 6, ii, 0:8]
+            field[y, ii, 8:16] = b * inv[y + 6, ii, 8:16]
         return 0
 
     lax.fori_loop(first, last, body, 0)
@@ -411,17 +447,17 @@
 def inner_kernel(sums, edge, from_e, from_w, j_ref, inv, field, one, two):
     sub = sublane()
     own_rows(sums, edge, from_e, from_w, inv, field, 0, 25, sub)
-    laplace_row(field, j_ref, inv, one, 3, FIRST, FIRST, sub)
+    laplace_row(field, j_ref, inv, one, 3, FIRST, FIRST, sub, (6, 9))
 
     def rows_one(r, _):
-        laplace_row(field, j_ref, inv, one, r, JOIN, FIRST, sub)
+        laplace_row(field, j_ref, inv, one, r, JOIN, FIRST, sub, (6, 9))
         return 0
 
     lax.fori_loop(4, 9, rows_one, 0, unroll=5)
-    laplace_row(one, j_ref, inv, two, 4, FIRST, FIRST, sub)
+    laplace_row(one, j_ref, inv, two, 4, FIRST, FIRST, sub, (9, 12), True)
 
     def rows_two(r, _):
-        laplace_row(one, j_ref, inv, two, r, JOIN, FIRST, sub)
+        laplace_row(one, j_ref, inv, two, r, JOIN, FIRST, sub, (9, 12), True)
         return 0
 
     lax.fori_loop(5, 8, rows_two, 0, unroll=3)
@@ -439,10 +475,10 @@
     def copy_rows(src, dst, first, last):
         def body(y, _):
             for ii in range(3):
-                dst[y, ii] = src[y, ii]
+                dst[y, ii] = src[y - first, ii]
             return 0
 
-        lax.fori_loop(first, last, body, 0)
+        lax.fori_loop(first, last, body, 0, unroll=4)
 
     copy_rows(field_in, field, 6, 31)
     for msg, first, shared in ((from_n, 0, 6), (from_s, 30, 0)):
@@ -464,12 +500,12 @@
     laplace_row(field, j_ref, inv, one, 10, JOIN, FIRST, sub)
     laplace_row(field, j_ref, inv, one, 11, JOIN, SKIP, sub)
     copy_rows(two_in, two, 12, 25)
-    laplace_row(one, j_ref, inv, two, 1, SKIP, FIRST, sub)
-    laplace_row(one, j_ref, inv, two, 2, JOIN, FIRST, sub)
-    laplace_row(one, j_ref, inv, two, 3, JOIN, JOIN, sub)
-    laplace_row(one, j_ref, inv, two, 8, JOIN, FIRST, sub)
-    laplace_row(one, j_ref, inv, two, 9, JOIN, FIRST, sub)
-    laplace_row(one, j_ref, inv, two, 10, JOIN, SKIP, sub)
+    laplace_row(one, j_ref, inv, two, 1, SKIP, FIRST, sub, narrow=True)
+    laplace_row(one, j_ref, inv, two, 2, JOIN, FIRST, sub, narrow=True)
+    laplace_row(one, j_ref, inv, two, 3, JOIN, JOIN, sub, narrow=True)
+    laplace_row(one, j_ref, inv, two, 8, JOIN, FIRST, sub, narrow=True)
+    laplace_row(one, j_ref, inv, two, 9, JOIN, FIRST, sub, narrow=True)
+    laplace_row(one, j_ref, inv, two, 10, JOIN, SKIP, sub, narrow=True)
     flat = spread.reshape(1024, 128)
 
     def finish(ey, _):
@@ -548,7 +584,7 @@
             pltpu.SMEM((64,), jnp.int32),
             pltpu.SemaphoreType.DMA((4,)),
         ],
-        compiler_params=PARAMS,
+        compiler_params=pltpu.CompilerParams(vmem_limit_bytes=FIRST_LIMIT, dimension_semantics=("arbitrary",)),
         name="section_one_sums",
     )
     sums, west, east, north, south, t0, *coefs = first(nodes, tracers, velocity, jacobian.T)
@@ -566,6 +602,14 @@
     from_n, from_s = swapped(msg_n, msg_s, PX)
 
     whole = pl.BlockSpec(memory_space=pltpu.VMEM)
+    inv_inner = pl.pallas_call(
+        own_geometry_kernel,
+        in_specs=[whole] * 3,
+        out_specs=whole,
+        out_shape=sds(37, 3, 16, 128),
+        compiler_params=pltpu.CompilerParams(vmem_limit_bytes=VMEM_LIMIT),
+        name="inner_geometry",
+    )(west, from_e, from_w)
     jac, inv = pl.pallas_call(
         geometry_kernel,
         in_specs=[whole] * 5,
@@ -576,7 +620,22 @@
     )(west, from_e, from_w, from_n, from_s)
     jac_spec, inv_spec = (fixed(16, 12, 16, 128), fixed(37, 3, 16, 128))
 
-    def stage(keep, take, wide, sums, edge, from_e, from_w, from_n, from_s, rows):
+    def inner_stage(keep, take, sums, edge, from_e, from_w, inv, rows):
+        return pl.pallas_call(
+            functools.partial(stage_inner_kernel, keep, take),
+            grid=(4,),
+            in_specs=[sums_spec] + [tiled(rows, 128)] * 3 + [inv_spec, tiled(16, 8, 8, 128)] + coef_specs,
+            out_specs=[sums_spec, tiled(32, 128)],
+            out_shape=[sds(27, 3, 8, 512), sds(32, 512)],
+            scratch_shapes=[pltpu.VMEM((27, 3, 8, 128), F32), pltpu.VMEM((32, 128), F32)],
+            compiler_params=PARAMS,
+            cost_estimate=pl.CostEstimate(
+                flops=64 * 16 * 512 * 60, bytes_accessed=8 * 1024 * 1024, transcendentals=0
+            ),
+            name="inner_rows",
+        )(sums, edge, from_e, from_w, inv, t0, *coefs)
+
+    def stage(keep, take, wide, sums, edge, from_e, from_w, from_n, from_s, rows, inner):
         if wide:
             outs = [sds(25, 8, 512), sds(25, 8, 512), sds(8, 512), sds(32, 512)]
             specs = [tiled(25, 8, 128), tiled(25, 8, 128), tiled(8, 128), tiled(32, 128)]
@@ -589,24 +648,27 @@
             in_specs=[sums_spec]
             + [tiled(rows, 128)] * 5
             + [inv_spec, tiled(16, 8, 8, 128)]
-            + coef_specs,
+            + coef_specs
+            + [sums_spec, tiled(32, 128)],
             out_specs=[sums_spec] + specs,
             out_shape=[sds(27, 3, 8, 512)] + outs,
             scratch_shapes=[pltpu.VMEM((27, 3, 8, 128), F32), pltpu.VMEM((32, 128), F32)],
             compiler_params=PARAMS,
             name="section_three_sums" if wide else "section_two_sums",
-        )(sums, edge, from_e, from_w, from_n, from_s, inv, t0, *coefs)
-
+        )(sums, edge, from_e, from_w, from_n, from_s, inv, t0, *coefs, *inner)
+
+    inner = inner_stage(0.75, 0.25, sums, east, from_e, from_w, inv_inner, 48)
     sums, west, east, north, south = stage(
-        0.75, 0.25, False, sums, east, from_e, from_w, from_n, from_s, 48
+        0.75, 0.25, False, sums, east, from_e, from_w, from_n, from_s, 48, inner
     )
     from_w, from_e = swapped(west, east, 1)
     msg_n = corrected(north, from_w, from_e, 0)
     msg_s = corrected(south, from_w, from_e, 24)
     from_n, from_s = swapped(msg_n, msg_s, PX)
 
+    inner = inner_stage(1.0 / 3.0, 2.0 / 3.0, sums, east, from_e, from_w, inv, 32)
     sums, west, east, _, edge = stage(
-        1.0 / 3.0, 2.0 / 3.0, True, sums, east, from_e, from_w, from_n, from_s, 32
+        1.0 / 3.0, 2.0 / 3.0, True, sums, east, from_e, from_w, from_n, from_s, 32, inner
     )
     from_w, from_e = swapped(west, east, 1)
     message = tiled(25, 8, 128)
@@ -621,14 +683,14 @@
         name="row_bands",
     )(sums, edge, from_e, from_w)
     from_n, from_s = swapped(msg_n, msg_s, PX)
-    grown = tiled(37, 3, 16, 128)
+    grown = [(25, 3, 16), (19, 3, 16), (13, 3, 16)]
     flops = 64 * 16 * 512 * 60
     field, one, two = pl.pallas_call(
         inner_kernel,
         grid=(4,),
         in_specs=[sums_spec, tiled(32, 128), message, message, jac_spec, inv_spec],
-        out_specs=[grown] * 3,
-        out_shape=[sds(37, 3, 16, 512)] * 3,
+        out_specs=[tiled(*g, 128) for g in grown],
+        out_shape=[sds(*g, 512) for g in grown],
         compiler_params=PARAMS,
         cost_estimate=pl.CostEstimate(flops=flops, bytes_accessed=16 * 1024 * 1024, transcendentals=0),
         name="biharmonic_inner_rows",
@@ -636,7 +698,7 @@
     return pl.pallas_call(
         last_kernel,
         grid=(4,),
-        in_specs=[SMEM, band, band, jac_spec, inv_spec] + [grown] * 3,
+        in_specs=[SMEM, band, band, jac_spec, inv_spec] + [tiled(*g, 128) for g in grown],
         out_specs=tiled(64, 16, 128),
         out_shape=sds(64, 16, 512),
         scratch_shapes=[pltpu.VMEM((37, 3, 16, 128), F32)] * 3

time: 98 us -> 90.8 us (0.927)
  waiting for transfers between devices: 34 us -> 27.2 us
  Pallas kernels: 35.3 us -> 33.2 us
  other arithmetic: 0.71 us -> 2.37 us
    pallas_call x0 -> x3, Pallas kernels: none -> 5.45 us  [the longest x2 4.96 us: inner_stage(): pl.pallas_call(functools.partial(stage_inner_kernel, keep, take), grid=(4...]
    pallas_call x2, Pallas kernels: 9.51 us -> 4.71 us  [stage(): pl.pallas_call(functools.partial(stage_kernel, keep, take, wide), grid=(4...]
    ppermute x6, waiting for transfers between devices: 9.03 us -> 5.22 us  [swapped(): lax.ppermute(jnp.where(even, after, before), 'sfc', up + [(j, i) for i, j...]
    ppermute x6, waiting for transfers between devices: 25 us -> 21.9 us  [swapped(): lax.ppermute(jnp.where(even, before, after), 'sfc', over + [(j, i) for i,...]
    pallas_call x1, Pallas kernels: 10.3 us -> 8.49 us  [per_device(): pl.pallas_call(last_kernel, grid=(4,), in_specs=[SMEM, band, band, jac_sp...]
    pallas_call x1, Pallas kernels: 6.56 us -> 5.44 us  [per_device(): pl.pallas_call(inner_kernel, grid=(4,), in_specs=[sums_spec, tiled(32, 12...]
    unnamed x12 -> x20, local copies, waits for them, and re-layouts: 4.63 us -> 4.57 us
  transfers between devices with their start and end apart: 12 -> 12, of which waited for: 9 -> 7; matrix products, arithmetic and copies ran while one was open for 0% -> 0% of each run, Pallas kernels for 7% -> 12%
where the time goes in v3:
time: 90.8 us; the launch traced here: 90.4 us
  Pallas kernels  33.2 us (37%)
  waiting for transfers between devices  27.2 us (30%)
  starting transfers between devices  22.8 us (25%)
  local copies, waits for them, and re-layouts  4.59 us (5%)
  other arithmetic  2.37 us (3%)
    ppermute x6, starting transfers between devices, swapped(): lax.ppermute(jnp.where(even, before, after), 'sfc', over + [(j, i) for i,...  22.5 us
    ppermute x6, waiting for transfers between devices, swapped(): lax.ppermute(jnp.where(even, before, after), 'sfc', over + [(j, i) for i,...  21.9 us
    pallas_call x1, Pallas kernels, per_device(): pl.pallas_call(last_kernel, grid=(4,), in_specs=[SMEM, band, band, jac_sp...  8.49 us
    pallas_call x1, Pallas kernels, per_device(): first(nodes, tracers, velocity, jacobian.T)  7.73 us
    pallas_call x1, Pallas kernels, per_device(): pl.pallas_call(inner_kernel, grid=(4,), in_specs=[sums_spec, tiled(32, 12...  5.44 us
    ppermute x6, waiting for transfers between devices, swapped(): lax.ppermute(jnp.where(even, after, before), 'sfc', up + [(j, i) for i, j...  5.22 us
    pallas_call x2, Pallas kernels, inner_stage(): pl.pallas_call(functools.partial(stage_inner_kernel, keep, take), grid=(4...  4.96 us
    pallas_call x2, Pallas kernels, stage(): pl.pallas_call(functools.partial(stage_kernel, keep, take, wide), grid=(4...  4.71 us
  transfers between devices with their start and end apart: 12, of which 7 were waited for; matrix products, arithmetic and copies ran while one was open for 0% of the time, Pallas kernels for 12%

profile of v3, /device:TPU:0, one launch (start us, length us, event | category | flops | bytes accessed | tf_op | source)
XLA Modules:
  0.0 90.4 jit_solution(6939148240276864514)
XLA Ops:
  1.4 7.7 %section_one_sums.1 = (f32[27,3,8,512]{3,2,1,0:T(8,128)}, f32[48,512]{1,0:T(8,128)S(1)}, f32[48,512]{1,0:T(8,128)S(1)}, f32[32,512]{1,0:T(8,128)S(1)}, f32[32,51...) custom-call(s32[16,64]{1,0:T(8,128)S(1)} %bitcast.10, ...), custom_call_target="tpu_custom_call" | custom-call | tf_op jit(solution)/shard_map/section_one_sums/pallas_call | solution.py:590
  9.1 0.8 copy-done.1
  9.9 0.7 broadcast_select_fusion.12
  10.6 8.2 %collective-permute-start.1 = (f32[48,512]{1,0:T(8,128)}, f32[48,512]{1,0:T(8,128)}, u32[]{:S(2)}, u32[]{:S(2)}) collective-permute-start(f32[48,512]{1,0:T(8,128)} %get-tuple-element.83), channel_id=1, source_target_pairs={{1,2},{3,4},{5,6},{7,8},{9,10},{11,12},{13,14},{15,16},{17,18},{19... | collective-permute-start | bytes 294920 | tf_op jit(solution)/shard_map/ppermute | solution.py:560
  18.9 2.6 %collective-permute-done.1 = f32[48,512]{1,0:T(8,128)} collective-permute-done((f32[48,512]{1,0:T(8,128)}, f32[48,512]{1,0:T(8,128)}, u32[]{:S(2)}, u32[]{:S(2)}) %collective-permute-start.1) | collective-permute-done | bytes 98336 | tf_op jit(solution)/shard_map/ppermute | solution.py:560
  21.5 1.0 %broadcast_select_fusion.10 = (f32[48,512]{1,0:T(8,128)S(1)}, f32[48,512]{1,0:T(8,128)S(1)}) fusion(f32[48,512]{1,0:T(8,128)} %collective-permute-done.1, f32[48,512]{1,0:T(8,128)} %collective-permute-done, pred[]{:T(512)S(6)} %eq.35), kind=kLoop, calls=%fused_computation.20 | loop fusion | flops 49152 | bytes 393217 | tf_op jit(solution)/shard_map/jit(_where)/select_n | solution.py:561
  22.7 2.8 %collective-permute-start.2 = (f32[48,512]{1,0:T(8,128)S(1)}, f32[48,512]{1,0:T(8,128)S(1)}, u32[]{:S(2)}, u32[]{:S(2)}) collective-permute-start(f32[48,512]{1,0:T(8,128)S(1)} %get-tuple-element.80), channel_id=1, source_target_pairs={{8,16},{9,17},{10,18},{11,19},{12,20},{13,21},{14,22},{15,23},{24,... | collective-permute-start | bytes 294920 | tf_op jit(solution)/shard_map/ppermute | solution.py:560
  26.0 1.0 %copy-done.3 = f32[16,8,8,128]{3,2,1,0:T(8,128)S(1)} copy-done((f32[16,8,8,128]{3,2,1,0:T(8,128)S(1)}, f32[16,8,8,128]{3,2,1,0:T(8,128)}, u32[]{:S(2)}) %copy-start.3) | copy-done | bytes 524312
  27.1 1.3 %copy-done.5 = f32[27,3,8,512]{3,2,1,0:T(8,128)S(1)} copy-done((f32[27,3,8,512]{3,2,1,0:T(8,128)S(1)}, f32[27,3,8,512]{3,2,1,0:T(8,128)}, u32[]{:S(2)}) %copy-start.5) | copy-done | bytes 1327128
  28.4 2.5 %inner_rows.2 = (f32[27,3,8,512]{3,2,1,0:T(8,128)S(1)}, f32[32,512]{1,0:T(8,128)S(1)}) custom-call(f32[27,3,8,512]{3,2,1,0:T(8,128)S(1)} %copy-done.5, f32[48,512]{1,0:T(8,128)S(1)} %get-tuple-element.37.edge, f32[48,512]{1,0:T(8,128)S(1)} %get-tuple-element.82.from_e, f32[48,512]{1,0:T(8,128)S(1)} %get-tuple-element.81.from_w, ...), custom_call_target="tpu_custom_call" | custom-call | flops 31457280 | bytes 8388608 | tf_op jit(solution)/shard_map/inner_rows/pallas_call | solution.py:624
  30.9 0.8 geometry.1
  31.7 1.9 %section_two_sums.1 = (f32[27,3,8,512]{3,2,1,0:T(8,128)S(1)}, f32[32,512]{1,0:T(8,128)S(1)}, f32[32,512]{1,0:T(8,128)S(1)}, f32[32,512]{1,0:T(8,128)S(1)}, f32[32,512]{1,0:T(8,128)S(1)}) custom-call(f32[27,3,8,512]{3,2,1,0:T(8,128)S(1)} %copy-done.6, f32[48,512]{1,0:T(8,128)S(1)} %get-tuple-element.37.edge, f32[48,512]{1,0:T(8,128)S(1)} %get-tuple-element.82.from_e, ...), custom_call_target="tpu_custom_call" | custom-call | tf_op jit(solution)/shard_map/section_two_sums/pallas_call | solution.py:645
  33.7 5.9 %collective-permute-start.5 = (f32[32,512]{1,0:T(8,128)S(1)}, f32[32,512]{1,0:T(8,128)S(1)}, u32[]{:S(2)}, u32[]{:S(2)}) collective-permute-start(f32[32,512]{1,0:T(8,128)S(1)} %get-tuple-element.91), channel_id=1, source_target_pairs={{1,2},{3,4},{5,6},{7,8},{9,10},{11,12},{13,14},{15,16},{17,18},{19... | collective-permute-start | bytes 196616 | tf_op jit(solution)/shard_map/ppermute | solution.py:560
  39.6 3.3 %collective-permute-done.5 = f32[32,512]{1,0:T(8,128)S(1)} collective-permute-done((f32[32,512]{1,0:T(8,128)S(1)}, f32[32,512]{1,0:T(8,128)S(1)}, u32[]{:S(2)}, u32[]{:S(2)}) %collective-permute-start.5) | collective-permute-done | bytes 65568 | tf_op jit(solution)/shard_map/ppermute | solution.py:560
  43.8 2.5 %inner_rows.3 = (f32[27,3,8,512]{3,2,1,0:T(8,128)S(1)}, f32[32,512]{1,0:T(8,128)S(1)}) custom-call(f32[27,3,8,512]{3,2,1,0:T(8,128)S(1)} %get-tuple-element.50.sums, f32[32,512]{1,0:T(8,128)S(1)} %get-tuple-element.51.edge, f32[32,512]{1,0:T(8,128)S(1)} %get-tuple-element.90.from_e, f32[32,512]{1,0:T(8,128)S(1)} %get-tuple-element.89.from_w, ...), custom_call_target="tpu_custom_call" | custom-call | flops 31457280 | bytes 8388608 | tf_op jit(solution)/shard_map/inner_rows/pallas_call | solution.py:624
  46.3 1.1 %collective-permute-done.7 = f32[32,512]{1,0:T(8,128)S(1)} collective-permute-done((f32[32,512]{1,0:T(8,128)S(1)}, f32[32,512]{1,0:T(8,128)S(1)}, u32[]{:S(2)}, u32[]{:S(2)}) %collective-permute-start.7) | collective-permute-done | bytes 65568 | tf_op jit(solution)/shard_map/ppermute | solution.py:559
  47.4 3.4 %collective-permute-done.6 = f32[32,512]{1,0:T(8,128)S(1)} collective-permute-done((f32[32,512]{1,0:T(8,128)S(1)}, f32[32,512]{1,0:T(8,128)S(1)}, u32[]{:S(2)}, u32[]{:S(2)}) %collective-permute-start.6) | collective-permute-done | bytes 65568 | tf_op jit(solution)/shard_map/ppermute | solution.py:560
  50.8 2.8 %section_three_sums.1 = (f32[27,3,8,512]{3,2,1,0:T(8,128)S(1)}, f32[25,8,512]{2,1,0:T(8,128)S(1)}, f32[25,8,512]{2,1,0:T(8,128)S(1)}, f32[8,512]{1,0:T(8,128)}, f32[32,512]{1,0:T(8,128)S(1)}) custom-call(f32[27,3,8,512]{3,2,1,0:T(8,128)S(1)} %get-tuple-element.50.sums, f32[32,512]{1,0:T(8,128)S(1)} %get-tuple-element.51.edge, ...), custom_call_target="tpu_custom_call" | custom-call | tf_op jit(solution)/shard_map/section_three_sums/pallas_call | solution.py:645
  53.7 4.8 %collective-permute-start.9 = (f32[25,8,512]{2,1,0:T(8,128)S(1)}, f32[25,8,512]{2,1,0:T(8,128)S(1)}, u32[]{:S(2)}, u32[]{:S(2)}) collective-permute-start(f32[25,8,512]{2,1,0:T(8,128)S(1)} %get-tuple-element.73), channel_id=1, source_target_pairs={{1,2},{3,4},{5,6},{7,8},{9,10},{11,12},{13,14},{15,16},{17,18},{19... | collective-permute-start | bytes 1228808 | tf_op jit(solution)/shard_map/ppermute | solution.py:560
  58.5 9.3 %collective-permute-done.9 = f32[25,8,512]{2,1,0:T(8,128)S(1)} collective-permute-done((f32[25,8,512]{2,1,0:T(8,128)S(1)}, f32[25,8,512]{2,1,0:T(8,128)S(1)}, u32[]{:S(2)}, u32[]{:S(2)}) %collective-permute-start.9) | collective-permute-done | bytes 409632 | tf_op jit(solution)/shard_map/ppermute | solution.py:560
  68.7 5.4 %biharmonic_inner_rows.1 = (f32[25,3,16,512]{3,2,1,0:T(8,128)S(1)}, f32[19,3,16,512]{3,2,1,0:T(8,128)S(1)}, f32[13,3,16,512]{3,2,1,0:T(8,128)S(1)}) custom-call(f32[27,3,8,512]{3,2,1,0:T(8,128)S(1)} %get-tuple-element.57.sums, f32[32,512]{1,0:T(8,128)S(1)} %get-tuple-element.58.edge, f32[25,8,512]{2,1,0:T(8,128)S(1)} %get-tuple-element.72.from_e, ...), custom_call_target="tpu_custom_call" | custom-call | flops 31457280 | bytes 16777216 | tf_op jit(solution)/shard_map/biharmonic_inner_rows/pallas_call | solution.py:688
  74.2 4.1 %collective-permute-done.11 = f32[7,40,512]{2,1,0:T(8,128)S(1)} collective-permute-done((f32[7,40,512]{2,1,0:T(8,128)S(1)}, f32[7,40,512]{2,1,0:T(8,128)S(1)}, u32[]{:S(2)}, u32[]{:S(2)}) %collective-permute-start.11) | collective-permute-done | bytes 573472 | tf_op jit(solution)/shard_map/ppermute | solution.py:559
  78.3 3.4 %collective-permute-done.10 = f32[7,40,512]{2,1,0:T(8,128)S(1)} collective-permute-done((f32[7,40,512]{2,1,0:T(8,128)S(1)}, f32[7,40,512]{2,1,0:T(8,128)S(1)}, u32[]{:S(2)}, u32[]{:S(2)}) %collective-permute-start.10) | collective-permute-done | bytes 573472 | tf_op jit(solution)/shard_map/ppermute | solution.py:560
  81.9 8.5 %biharmonic_outer_rows.1 = f32[64,16,512]{2,1,0:T(8,128)} custom-call(s32[16,64]{1,0:T(8,128)S(1)} %bitcast.11, f32[7,40,512]{2,1,0:T(8,128)S(1)} %get-tuple-element.68.from_n, f32[7,40,512]{2,1,0:T(8,128)S(1)} %get-tuple-element.67.from_s, f32[16,12,16,128]{3,2,1,0:T(8,128)S(1)} %get-tuple-element.63.j_ref, f32[37,3,16,128]{3,2,1,0:T(8,128)S(1)} %get-tuple-element.41.inv, ...), custom_call_target="tpu_custom_call" | custom-call | tf_op jit(solution)/shard_map/biharmonic_outer_rows/pallas_call | solution.py:698
  (50 shorter events, 4.3 us)
Async XLA Ops:
  0.0 0.7 copy-start.7
  0.7 0.7 copy-start.9
  9.1 0.8 copy-start.1
  9.9 16.1 %copy-start = (f32[16,8,8,512]{3,2,1,0:T(8,128)S(1)}, f32[16,8,8,512]{3,2,1,0:T(8,128)}, u32[]{:S(2)}) copy-start(f32[16,8,8,512]{3,2,1,0:T(8,128)} %get-tuple-element.42.t0) | copy-start | bytes 6291460
  10.6 10.8 %collective-permute-start.1 = (f32[48,512]{1,0:T(8,128)}, f32[48,512]{1,0:T(8,128)}, u32[]{:S(2)}, u32[]{:S(2)}) collective-permute-start(f32[48,512]{1,0:T(8,128)} %get-tuple-element.83), channel_id=1, source_target_pairs={{1,2},{3,4},{5,6},{7,8},{9,10},{11,12},{13,14},{15,16},{17,18},{19... | collective-permute-start | bytes 294920 | tf_op jit(solution)/shard_map/ppermute | solution.py:560
  18.8 2.6 %collective-permute-start = (f32[48,512]{1,0:T(8,128)}, f32[48,512]{1,0:T(8,128)}, u32[]{:S(2)}, u32[]{:S(2)}) collective-permute-start(f32[48,512]{1,0:T(8,128)} %get-tuple-element.84), channel_id=1, source_target_pairs={{0,1},{2,3},{4,5},{6,7},{8,9},{10,11},{12,13},{14,15},{16,17},{18,... | collective-permute-start | bytes 294920 | tf_op jit(solution)/shard_map/ppermute | solution.py:559
  18.9 7.1 %copy-start.2 = (f32[16,8,8,128]{3,2,1,0:T(8,128)S(1)}, f32[16,8,8,128]{3,2,1,0:T(8,128)}, u32[]{:S(2)}) copy-start(f32[16,8,8,128]{3,2,1,0:T(8,128)} %copy-done.1) | copy-start | bytes 1572868
  22.6 8.2 %collective-permute-start.3 = (f32[48,512]{1,0:T(8,128)S(1)}, f32[48,512]{1,0:T(8,128)S(1)}, u32[]{:S(2)}, u32[]{:S(2)}) collective-permute-start(f32[48,512]{1,0:T(8,128)S(1)} %get-tuple-element.79), channel_id=1, source_target_pairs={{0,8},{1,9},{2,10},{3,11},{4,12},{5,13},{6,14},{7,15},{16,24},{17,... | collective-permute-start | bytes 294920 | tf_op jit(solution)/shard_map/ppermute | solution.py:559
  22.7 8.2 %collective-permute-start.2 = (f32[48,512]{1,0:T(8,128)S(1)}, f32[48,512]{1,0:T(8,128)S(1)}, u32[]{:S(2)}, u32[]{:S(2)}) collective-permute-start(f32[48,512]{1,0:T(8,128)S(1)} %get-tuple-element.80), channel_id=1, source_target_pairs={{8,16},{9,17},{10,18},{11,19},{12,20},{13,21},{14,22},{15,23},{24,... | collective-permute-start | bytes 294920 | tf_op jit(solution)/shard_map/ppermute | solution.py:560
  26.0 1.0 %copy-start.3 = (f32[16,8,8,128]{3,2,1,0:T(8,128)S(1)}, f32[16,8,8,128]{3,2,1,0:T(8,128)}, u32[]{:S(2)}) copy-start(f32[16,8,8,128]{3,2,1,0:T(8,128)} %get-tuple-element.46.j_ref) | copy-start | bytes 1572868
  27.1 1.3 %copy-start.5 = (f32[27,3,8,512]{3,2,1,0:T(8,128)S(1)}, f32[27,3,8,512]{3,2,1,0:T(8,128)}, u32[]{:S(2)}) copy-start(f32[27,3,8,512]{3,2,1,0:T(8,128)} %get-tuple-element.36.sums) | copy-start | bytes 3981316
  28.4 3.3 %copy-start.4 = (f32[16,8,8,128]{3,2,1,0:T(8,128)S(1)}, f32[16,8,8,128]{3,2,1,0:T(8,128)}, u32[]{:S(2)}) copy-start(f32[16,8,8,128]{3,2,1,0:T(8,128)} %get-tuple-element.46.j_ref) | copy-start | bytes 1572868
  28.4 3.3 %copy-start.6 = (f32[27,3,8,512]{3,2,1,0:T(8,128)S(1)}, f32[27,3,8,512]{3,2,1,0:T(8,128)}, u32[]{:S(2)}) copy-start(f32[27,3,8,512]{3,2,1,0:T(8,128)} %get-tuple-element.36.sums) | copy-start | bytes 3981316
  33.7 9.2 %collective-permute-start.5 = (f32[32,512]{1,0:T(8,128)S(1)}, f32[32,512]{1,0:T(8,128)S(1)}, u32[]{:S(2)}, u32[]{:S(2)}) collective-permute-start(f32[32,512]{1,0:T(8,128)S(1)} %get-tuple-element.91), channel_id=1, source_target_pairs={{1,2},{3,4},{5,6},{7,8},{9,10},{11,12},{13,14},{15,16},{17,18},{19... | collective-permute-start | bytes 196616 | tf_op jit(solution)/shard_map/ppermute | solution.py:560
  39.6 3.3 %collective-permute-start.4 = (f32[32,512]{1,0:T(8,128)S(1)}, f32[32,512]{1,0:T(8,128)S(1)}, u32[]{:S(2)}, u32[]{:S(2)}) collective-permute-start(f32[32,512]{1,0:T(8,128)S(1)} %get-tuple-element.92), channel_id=1, source_target_pairs={{0,1},{2,3},{4,5},{6,7},{8,9},{10,11},{12,13},{14,15},{16,17},{18,... | collective-permute-start | bytes 196616 | tf_op jit(solution)/shard_map/ppermute | solution.py:559
  43.0 4.3 %collective-permute-start.7 = (f32[32,512]{1,0:T(8,128)S(1)}, f32[32,512]{1,0:T(8,128)S(1)}, u32[]{:S(2)}, u32[]{:S(2)}) collective-permute-start(f32[32,512]{1,0:T(8,128)S(1)} %get-tuple-element.85), channel_id=1, source_target_pairs={{0,8},{1,9},{2,10},{3,11},{4,12},{5,13},{6,14},{7,15},{16,24},{17,... | collective-permute-start | bytes 196616 | tf_op jit(solution)/shard_map/ppermute | solution.py:559
  43.1 7.7 %collective-permute-start.6 = (f32[32,512]{1,0:T(8,128)S(1)}, f32[32,512]{1,0:T(8,128)S(1)}, u32[]{:S(2)}, u32[]{:S(2)}) collective-permute-start(f32[32,512]{1,0:T(8,128)S(1)} %get-tuple-element.86), channel_id=1, source_target_pairs={{8,16},{9,17},{10,18},{11,19},{12,20},{13,21},{14,22},{15,23},{24,... | collective-permute-start | bytes 196616 | tf_op jit(solution)/shard_map/ppermute | solution.py:560
  53.7 14.1 %collective-permute-start.9 = (f32[25,8,512]{2,1,0:T(8,128)S(1)}, f32[25,8,512]{2,1,0:T(8,128)S(1)}, u32[]{:S(2)}, u32[]{:S(2)}) collective-permute-start(f32[25,8,512]{2,1,0:T(8,128)S(1)} %get-tuple-element.73), channel_id=1, source_target_pairs={{1,2},{3,4},{5,6},{7,8},{9,10},{11,12},{13,14},{15,16},{17,18},{19... | collective-permute-start | bytes 1228808 | tf_op jit(solution)/shard_map/ppermute | solution.py:560
  58.5 9.3 %collective-permute-start.8 = (f32[25,8,512]{2,1,0:T(8,128)S(1)}, f32[25,8,512]{2,1,0:T(8,128)S(1)}, u32[]{:S(2)}, u32[]{:S(2)}) collective-permute-start(f32[25,8,512]{2,1,0:T(8,128)S(1)} %get-tuple-element.74), channel_id=1, source_target_pairs={{0,1},{2,3},{4,5},{6,7},{8,9},{10,11},{12,13},{14,15},{16,17},{18,... | collective-permute-start | bytes 1228808 | tf_op jit(solution)/shard_map/ppermute | solution.py:559
  68.6 9.8 %collective-permute-start.11 = (f32[7,40,512]{2,1,0:T(8,128)S(1)}, f32[7,40,512]{2,1,0:T(8,128)S(1)}, u32[]{:S(2)}, u32[]{:S(2)}) collective-permute-start(f32[7,40,512]{2,1,0:T(8,128)S(1)} %get-tuple-element.69), channel_id=1, source_target_pairs={{0,8},{1,9},{2,10},{3,11},{4,12},{5,13},{6,14},{7,15},{16,24},{17,... | collective-permute-start | bytes 1720328 | tf_op jit(solution)/shard_map/ppermute | solution.py:559
  68.7 13.1 %collective-permute-start.10 = (f32[7,40,512]{2,1,0:T(8,128)S(1)}, f32[7,40,512]{2,1,0:T(8,128)S(1)}, u32[]{:S(2)}, u32[]{:S(2)}) collective-permute-start(f32[7,40,512]{2,1,0:T(8,128)S(1)} %get-tuple-element.70), channel_id=1, source_target_pairs={{8,16},{9,17},{10,18},{11,19},{12,20},{13,21},{14,22},{15,23},{24,... | collective-permute-start | bytes 1720328 | tf_op jit(solution)/shard_map/ppermute | solution.py:560
  74.2 7.7 %copy-start.8 = (s32[64,16]{0,1:T(8,128)S(1)}, s32[64,16]{0,1:T(8,128)}, u32[]{:S(2)}) copy-start(s32[64,16]{0,1:T(8,128)} %param.7) | copy-start | bytes 12292

commit v4 on v3

--- a/solution.py
+++ b/solution.py
@@ -140,8 +140,8 @@
 
 
 def first_kernel(
-    nodes, x, vel, jin, sums, west, east, north, south, t0, u_ref, v_ref, rj_ref, j_ref, rd_ref,
-    gathered, winds, jc, node_rows, j_rows, corners, spots, sem,
+    corners, node_rows, x, vel, j_rows, sums, west, east, north, south, t0, u_ref, v_ref, rj_ref, j_ref, rd_ref,
+    gathered, winds, jc, spots,
 ):
     step = pl.program_id(0)
     sub = sublane()
@@ -149,27 +149,16 @@
 
     @pl.when(step == 0)
     def _():
-        copies = [
-            pltpu.make_async_copy(nodes, corners, sem.at[0]),
-            pltpu.make_async_copy(nodes, node_rows, sem.at[1]),
-            pltpu.make_async_copy(jin, j_rows, sem.at[2]),
-            pltpu.make_async_copy(vel, gathered, sem.at[3]),
-        ]
-        for copy in copies:
-            copy.start()
         jc[...] = jnp.zeros_like(jc)
-        for copy in copies[:3]:
-            copy.wait()
         fill_places(corners, spots)
         to = place(node_rows[0:1, :])
         hit = (lax.broadcasted_iota(jnp.int32, (64, 64), 0) == to).astype(F32)
         jc[:, 0:16] = lax.dot_general(
             hit, j_rows[...], (((1,), (1,)), ((), ())), precision=lax.Precision.HIGHEST, preferred_element_type=F32
         )
-        copies[3].wait()
 
         def order(e, _):
-            winds[spots[e]] = gathered[e]
+            winds[spots[e]] = vel[e]
             return 0
 
         lax.fori_loop(0, 64, order, 0, unroll=8)
@@ -400,7 +389,7 @@
 FIRST, JOIN, SKIP = range(3)
 
 
-def laplace_row(src, j_ref, inv, dst, r, top, bottom, sub, at=(0, 0), narrow=False):
+def laplace_row(src, j_ref, inv, dst, r, top, bottom, sub, at=(0, 0), narrow=False, only=range(4)):
     fa, fb = ([], [])
     for j in range(4):
         y = 3 * r + j - at[0]
@@ -412,7 +401,7 @@
     cb = laplace_core(lambda n: fb[n], lambda n: j_ref[n, r, 8:16])
     for j in range(4):
         what = {0: top, 3: bottom}.get(j)
-        if what == SKIP:
+        if what == SKIP or j not in only:
             continue
         y = 3 * r + j
         ra, rb = (roll(ca[4 * j + 3], 1), roll(cb[4 * j + 3], 1))
@@ -493,19 +482,19 @@
                 field[y, ii, 0:8] = a
                 field[y, ii, 8:16] = b
     copy_rows(one_in, one, 9, 28)
-    laplace_row(field, j_ref, inv, one, 0, SKIP, FIRST, sub)
+    laplace_row(field, j_ref, inv, one, 0, SKIP, FIRST, sub, only=(3,))
     laplace_row(field, j_ref, inv, one, 1, JOIN, FIRST, sub)
     laplace_row(field, j_ref, inv, one, 2, JOIN, JOIN, sub)
     laplace_row(field, j_ref, inv, one, 9, JOIN, FIRST, sub)
     laplace_row(field, j_ref, inv, one, 10, JOIN, FIRST, sub)
-    laplace_row(field, j_ref, inv, one, 11, JOIN, SKIP, sub)
+    laplace_row(field, j_ref, inv, one, 11, JOIN, SKIP, sub, only=(0,))
     copy_rows(two_in, two, 12, 25)
-    laplace_row(one, j_ref, inv, two, 1, SKIP, FIRST, sub, narrow=True)
+    laplace_row(one, j_ref, inv, two, 1, SKIP, FIRST, sub, narrow=True, only=(3,))
     laplace_row(one, j_ref, inv, two, 2, JOIN, FIRST, sub, narrow=True)
     laplace_row(one, j_ref, inv, two, 3, JOIN, JOIN, sub, narrow=True)
     laplace_row(one, j_ref, inv, two, 8, JOIN, FIRST, sub, narrow=True)
     laplace_row(one, j_ref, inv, two, 9, JOIN, FIRST, sub, narrow=True)
-    laplace_row(one, j_ref, inv, two, 10, JOIN, SKIP, sub, narrow=True)
+    laplace_row(one, j_ref, inv, two, 10, JOIN, SKIP, sub, narrow=True, only=(0,))
     flat = spread.reshape(1024, 128)
 
     def finish(ey, _):
@@ -548,7 +537,6 @@
 
 PARAMS = pltpu.CompilerParams(vmem_limit_bytes=VMEM_LIMIT, dimension_semantics=("arbitrary",))
 SMEM = pl.BlockSpec(memory_space=pltpu.SMEM)
-HBM = pl.BlockSpec(memory_space=pltpu.HBM)
 
 
 def swapped(before, after, distance):
@@ -569,7 +557,7 @@
     first = pl.pallas_call(
         first_kernel,
         grid=(4,),
-        in_specs=[HBM, tiled(64, 16, 128), HBM, HBM],
+        in_specs=[SMEM, fixed(16, 64), tiled(64, 16, 128), fixed(64, 16, 128), fixed(16, 64)],
         out_specs=[sums_spec, tiled(48, 128), tiled(48, 128), tiled(32, 128), tiled(32, 128), tiled(16, 8, 8, 128)]
         + coef_specs,
         out_shape=[sds(27, 3, 8, 512), sds(48, 512), sds(48, 512), sds(32, 512), sds(32, 512), sds(16, 8, 8, 512)]
@@ -578,16 +566,12 @@
             pltpu.VMEM((64, 16, 128), F32),
             pltpu.VMEM((64, 16, 128), F32),
             pltpu.VMEM((64, 128), F32),
-            pltpu.VMEM((16, 64), jnp.int32),
-            pltpu.VMEM((16, 64), F32),
-            pltpu.SMEM((16, 64), jnp.int32),
             pltpu.SMEM((64,), jnp.int32),
-            pltpu.SemaphoreType.DMA((4,)),
         ],
         compiler_params=pltpu.CompilerParams(vmem_limit_bytes=FIRST_LIMIT, dimension_semantics=("arbitrary",)),
         name="section_one_sums",
     )
-    sums, west, east, north, south, t0, *coefs = first(nodes, tracers, velocity, jacobian.T)
+    sums, west, east, north, south, t0, *coefs = first(nodes, nodes, tracers, velocity, jacobian.T)
 
     row = lax.broadcasted_iota(jnp.int32, (32, 1), 0)
 

time: 90.8 us -> 89.9 us (0.990)
  no operation moved by 1% of the time
where the time goes in v4:
time: 89.9 us; the launch traced here: 89.5 us
  Pallas kernels  32.4 us (36%)
  waiting for transfers between devices  27.2 us (30%)
  starting transfers between devices  22.8 us (25%)
  local copies, waits for them, and re-layouts  4.59 us (5%)
  other arithmetic  2.37 us (3%)
    ppermute x6, starting transfers between devices, swapped(): lax.ppermute(jnp.where(even, before, after), 'sfc', over + [(j, i) for i,...  22.5 us
    ppermute x6, waiting for transfers between devices, swapped(): lax.ppermute(jnp.where(even, before, after), 'sfc', over + [(j, i) for i,...  21.9 us
    pallas_call x1, Pallas kernels, per_device(): pl.pallas_call(last_kernel, grid=(4,), in_specs=[SMEM, band, band, jac_sp...  8.15 us
    pallas_call x1, Pallas kernels, per_device(): first(nodes, nodes, tracers, velocity, jacobian.T)  7.22 us
    pallas_call x1, Pallas kernels, per_device(): pl.pallas_call(inner_kernel, grid=(4,), in_specs=[sums_spec, tiled(32, 12...  5.44 us
    ppermute x6, waiting for transfers between devices, swapped(): lax.ppermute(jnp.where(even, after, before), 'sfc', up + [(j, i) for i, j...  5.22 us
    pallas_call x2, Pallas kernels, inner_stage(): pl.pallas_call(functools.partial(stage_inner_kernel, keep, take), grid=(4...  4.96 us
    pallas_call x2, Pallas kernels, stage(): pl.pallas_call(functools.partial(stage_kernel, keep, take, wide), grid=(4...  4.71 us
  transfers between devices with their start and end apart: 12, of which 7 were waited for; matrix products, arithmetic and copies ran while one was open for 0% of the time, Pallas kernels for 12%

profile of v4, /device:TPU:0, one launch (start us, length us, event | category | flops | bytes accessed | tf_op | source)
XLA Modules:
  0.0 89.5 jit_solution(13477167605420928512)
XLA Ops:
  1.4 7.2 %section_one_sums.1 = (f32[27,3,8,512]{3,2,1,0:T(8,128)}, f32[48,512]{1,0:T(8,128)S(1)}, f32[48,512]{1,0:T(8,128)S(1)}, f32[32,512]{1,0:T(8,128)S(1)}, f32[32,51...) custom-call(s32[16,64]{1,0:T(8,128)S(1)} %bitcast.10, ...), custom_call_target="tpu_custom_call" | custom-call | tf_op jit(solution)/shard_map/section_one_sums/pallas_call | solution.py:574
  8.6 0.8 copy-done.1
  9.4 0.7 broadcast_select_fusion.12
  10.1 8.2 %collective-permute-start.1 = (f32[48,512]{1,0:T(8,128)}, f32[48,512]{1,0:T(8,128)}, u32[]{:S(2)}, u32[]{:S(2)}) collective-permute-start(f32[48,512]{1,0:T(8,128)} %get-tuple-element.83), channel_id=1, source_target_pairs={{1,2},{3,4},{5,6},{7,8},{9,10},{11,12},{13,14},{15,16},{17,18},{19... | collective-permute-start | bytes 294920 | tf_op jit(solution)/shard_map/ppermute | solution.py:548
  18.4 2.6 %collective-permute-done.1 = f32[48,512]{1,0:T(8,128)} collective-permute-done((f32[48,512]{1,0:T(8,128)}, f32[48,512]{1,0:T(8,128)}, u32[]{:S(2)}, u32[]{:S(2)}) %collective-permute-start.1) | collective-permute-done | bytes 98336 | tf_op jit(solution)/shard_map/ppermute | solution.py:548
  21.0 1.0 %broadcast_select_fusion.10 = (f32[48,512]{1,0:T(8,128)S(1)}, f32[48,512]{1,0:T(8,128)S(1)}) fusion(f32[48,512]{1,0:T(8,128)} %collective-permute-done.1, f32[48,512]{1,0:T(8,128)} %collective-permute-done, pred[]{:T(512)S(6)} %eq.35), kind=kLoop, calls=%fused_computation.20 | loop fusion | flops 49152 | bytes 393217 | tf_op jit(solution)/shard_map/jit(_where)/select_n | solution.py:549
  22.2 2.8 %collective-permute-start.2 = (f32[48,512]{1,0:T(8,128)S(1)}, f32[48,512]{1,0:T(8,128)S(1)}, u32[]{:S(2)}, u32[]{:S(2)}) collective-permute-start(f32[48,512]{1,0:T(8,128)S(1)} %get-tuple-element.80), channel_id=1, source_target_pairs={{8,16},{9,17},{10,18},{11,19},{12,20},{13,21},{14,22},{15,23},{24,... | collective-permute-start | bytes 294920 | tf_op jit(solution)/shard_map/ppermute | solution.py:548
  25.5 1.0 %copy-done.3 = f32[16,8,8,128]{3,2,1,0:T(8,128)S(1)} copy-done((f32[16,8,8,128]{3,2,1,0:T(8,128)S(1)}, f32[16,8,8,128]{3,2,1,0:T(8,128)}, u32[]{:S(2)}) %copy-start.3) | copy-done | bytes 524312
  26.6 1.3 %copy-done.5 = f32[27,3,8,512]{3,2,1,0:T(8,128)S(1)} copy-done((f32[27,3,8,512]{3,2,1,0:T(8,128)S(1)}, f32[27,3,8,512]{3,2,1,0:T(8,128)}, u32[]{:S(2)}) %copy-start.5) | copy-done | bytes 1327128
  27.9 2.5 %inner_rows.2 = (f32[27,3,8,512]{3,2,1,0:T(8,128)S(1)}, f32[32,512]{1,0:T(8,128)S(1)}) custom-call(f32[27,3,8,512]{3,2,1,0:T(8,128)S(1)} %copy-done.5, f32[48,512]{1,0:T(8,128)S(1)} %get-tuple-element.37.edge, f32[48,512]{1,0:T(8,128)S(1)} %get-tuple-element.82.from_e, f32[48,512]{1,0:T(8,128)S(1)} %get-tuple-element.81.from_w, ...), custom_call_target="tpu_custom_call" | custom-call | flops 31457280 | bytes 8388608 | tf_op jit(solution)/shard_map/inner_rows/pallas_call | solution.py:608
  30.4 0.8 geometry.1
  31.2 1.9 %section_two_sums.1 = (f32[27,3,8,512]{3,2,1,0:T(8,128)S(1)}, f32[32,512]{1,0:T(8,128)S(1)}, f32[32,512]{1,0:T(8,128)S(1)}, f32[32,512]{1,0:T(8,128)S(1)}, f32[32,512]{1,0:T(8,128)S(1)}) custom-call(f32[27,3,8,512]{3,2,1,0:T(8,128)S(1)} %copy-done.6, f32[48,512]{1,0:T(8,128)S(1)} %get-tuple-element.37.edge, f32[48,512]{1,0:T(8,128)S(1)} %get-tuple-element.82.from_e, ...), custom_call_target="tpu_custom_call" | custom-call | tf_op jit(solution)/shard_map/section_two_sums/pallas_call | solution.py:629
  33.2 5.9 %collective-permute-start.5 = (f32[32,512]{1,0:T(8,128)S(1)}, f32[32,512]{1,0:T(8,128)S(1)}, u32[]{:S(2)}, u32[]{:S(2)}) collective-permute-start(f32[32,512]{1,0:T(8,128)S(1)} %get-tuple-element.91), channel_id=1, source_target_pairs={{1,2},{3,4},{5,6},{7,8},{9,10},{11,12},{13,14},{15,16},{17,18},{19... | collective-permute-start | bytes 196616 | tf_op jit(solution)/shard_map/ppermute | solution.py:548
  39.1 3.3 %collective-permute-done.5 = f32[32,512]{1,0:T(8,128)S(1)} collective-permute-done((f32[32,512]{1,0:T(8,128)S(1)}, f32[32,512]{1,0:T(8,128)S(1)}, u32[]{:S(2)}, u32[]{:S(2)}) %collective-permute-start.5) | collective-permute-done | bytes 65568 | tf_op jit(solution)/shard_map/ppermute | solution.py:548
  43.3 2.5 %inner_rows.3 = (f32[27,3,8,512]{3,2,1,0:T(8,128)S(1)}, f32[32,512]{1,0:T(8,128)S(1)}) custom-call(f32[27,3,8,512]{3,2,1,0:T(8,128)S(1)} %get-tuple-element.50.sums, f32[32,512]{1,0:T(8,128)S(1)} %get-tuple-element.51.edge, f32[32,512]{1,0:T(8,128)S(1)} %get-tuple-element.90.from_e, f32[32,512]{1,0:T(8,128)S(1)} %get-tuple-element.89.from_w, ...), custom_call_target="tpu_custom_call" | custom-call | flops 31457280 | bytes 8388608 | tf_op jit(solution)/shard_map/inner_rows/pallas_call | solution.py:608
  45.8 1.1 %collective-permute-done.7 = f32[32,512]{1,0:T(8,128)S(1)} collective-permute-done((f32[32,512]{1,0:T(8,128)S(1)}, f32[32,512]{1,0:T(8,128)S(1)}, u32[]{:S(2)}, u32[]{:S(2)}) %collective-permute-start.7) | collective-permute-done | bytes 65568 | tf_op jit(solution)/shard_map/ppermute | solution.py:547
  46.9 3.4 %collective-permute-done.6 = f32[32,512]{1,0:T(8,128)S(1)} collective-permute-done((f32[32,512]{1,0:T(8,128)S(1)}, f32[32,512]{1,0:T(8,128)S(1)}, u32[]{:S(2)}, u32[]{:S(2)}) %collective-permute-start.6) | collective-permute-done | bytes 65568 | tf_op jit(solution)/shard_map/ppermute | solution.py:548
  50.3 2.8 %section_three_sums.1 = (f32[27,3,8,512]{3,2,1,0:T(8,128)S(1)}, f32[25,8,512]{2,1,0:T(8,128)S(1)}, f32[25,8,512]{2,1,0:T(8,128)S(1)}, f32[8,512]{1,0:T(8,128)}, f32[32,512]{1,0:T(8,128)S(1)}) custom-call(f32[27,3,8,512]{3,2,1,0:T(8,128)S(1)} %get-tuple-element.50.sums, f32[32,512]{1,0:T(8,128)S(1)} %get-tuple-element.51.edge, ...), custom_call_target="tpu_custom_call" | custom-call | tf_op jit(solution)/shard_map/section_three_sums/pallas_call | solution.py:629
  53.2 4.8 %collective-permute-start.9 = (f32[25,8,512]{2,1,0:T(8,128)S(1)}, f32[25,8,512]{2,1,0:T(8,128)S(1)}, u32[]{:S(2)}, u32[]{:S(2)}) collective-permute-start(f32[25,8,512]{2,1,0:T(8,128)S(1)} %get-tuple-element.73), channel_id=1, source_target_pairs={{1,2},{3,4},{5,6},{7,8},{9,10},{11,12},{13,14},{15,16},{17,18},{19... | collective-permute-start | bytes 1228808 | tf_op jit(solution)/shard_map/ppermute | solution.py:548
  58.0 9.3 %collective-permute-done.9 = f32[25,8,512]{2,1,0:T(8,128)S(1)} collective-permute-done((f32[25,8,512]{2,1,0:T(8,128)S(1)}, f32[25,8,512]{2,1,0:T(8,128)S(1)}, u32[]{:S(2)}, u32[]{:S(2)}) %collective-permute-start.9) | collective-permute-done | bytes 409632 | tf_op jit(solution)/shard_map/ppermute | solution.py:548
  68.2 5.4 %biharmonic_inner_rows.1 = (f32[25,3,16,512]{3,2,1,0:T(8,128)S(1)}, f32[19,3,16,512]{3,2,1,0:T(8,128)S(1)}, f32[13,3,16,512]{3,2,1,0:T(8,128)S(1)}) custom-call(f32[27,3,8,512]{3,2,1,0:T(8,128)S(1)} %get-tuple-element.57.sums, f32[32,512]{1,0:T(8,128)S(1)} %get-tuple-element.58.edge, f32[25,8,512]{2,1,0:T(8,128)S(1)} %get-tuple-element.72.from_e, ...), custom_call_target="tpu_custom_call" | custom-call | flops 31457280 | bytes 16777216 | tf_op jit(solution)/shard_map/biharmonic_inner_rows/pallas_call | solution.py:672
  73.7 4.1 %collective-permute-done.11 = f32[7,40,512]{2,1,0:T(8,128)S(1)} collective-permute-done((f32[7,40,512]{2,1,0:T(8,128)S(1)}, f32[7,40,512]{2,1,0:T(8,128)S(1)}, u32[]{:S(2)}, u32[]{:S(2)}) %collective-permute-start.11) | collective-permute-done | bytes 573472 | tf_op jit(solution)/shard_map/ppermute | solution.py:547
  77.8 3.4 %collective-permute-done.10 = f32[7,40,512]{2,1,0:T(8,128)S(1)} collective-permute-done((f32[7,40,512]{2,1,0:T(8,128)S(1)}, f32[7,40,512]{2,1,0:T(8,128)S(1)}, u32[]{:S(2)}, u32[]{:S(2)}) %collective-permute-start.10) | collective-permute-done | bytes 573472 | tf_op jit(solution)/shard_map/ppermute | solution.py:548
  81.4 8.2 %biharmonic_outer_rows.1 = f32[64,16,512]{2,1,0:T(8,128)} custom-call(s32[16,64]{1,0:T(8,128)S(1)} %bitcast.12, f32[7,40,512]{2,1,0:T(8,128)S(1)} %get-tuple-element.68.from_n, f32[7,40,512]{2,1,0:T(8,128)S(1)} %get-tuple-element.67.from_s, f32[16,12,16,128]{3,2,1,0:T(8,128)S(1)} %get-tuple-element.63.j_ref, f32[37,3,16,128]{3,2,1,0:T(8,128)S(1)} %get-tuple-element.41.inv, ...), custom_call_target="tpu_custom_call" | custom-call | tf_op jit(solution)/shard_map/biharmonic_outer_rows/pallas_call | solution.py:682
  (50 shorter events, 4.3 us)
Async XLA Ops:
  0.0 0.7 copy-start.7
  0.7 0.7 copy-start.9
  8.6 0.8 copy-start.1
  9.4 16.1 %copy-start = (f32[16,8,8,512]{3,2,1,0:T(8,128)S(1)}, f32[16,8,8,512]{3,2,1,0:T(8,128)}, u32[]{:S(2)}) copy-start(f32[16,8,8,512]{3,2,1,0:T(8,128)} %get-tuple-element.42.t0) | copy-start | bytes 6291460
  10.1 10.8 %collective-permute-start.1 = (f32[48,512]{1,0:T(8,128)}, f32[48,512]{1,0:T(8,128)}, u32[]{:S(2)}, u32[]{:S(2)}) collective-permute-start(f32[48,512]{1,0:T(8,128)} %get-tuple-element.83), channel_id=1, source_target_pairs={{1,2},{3,4},{5,6},{7,8},{9,10},{11,12},{13,14},{15,16},{17,18},{19... | collective-permute-start | bytes 294920 | tf_op jit(solution)/shard_map/ppermute | solution.py:548
  18.3 2.6 %collective-permute-start = (f32[48,512]{1,0:T(8,128)}, f32[48,512]{1,0:T(8,128)}, u32[]{:S(2)}, u32[]{:S(2)}) collective-permute-start(f32[48,512]{1,0:T(8,128)} %get-tuple-element.84), channel_id=1, source_target_pairs={{0,1},{2,3},{4,5},{6,7},{8,9},{10,11},{12,13},{14,15},{16,17},{18,... | collective-permute-start | bytes 294920 | tf_op jit(solution)/shard_map/ppermute | solution.py:547
  18.4 7.1 %copy-start.2 = (f32[16,8,8,128]{3,2,1,0:T(8,128)S(1)}, f32[16,8,8,128]{3,2,1,0:T(8,128)}, u32[]{:S(2)}) copy-start(f32[16,8,8,128]{3,2,1,0:T(8,128)} %copy-done.1) | copy-start | bytes 1572868
  22.1 8.2 %collective-permute-start.3 = (f32[48,512]{1,0:T(8,128)S(1)}, f32[48,512]{1,0:T(8,128)S(1)}, u32[]{:S(2)}, u32[]{:S(2)}) collective-permute-start(f32[48,512]{1,0:T(8,128)S(1)} %get-tuple-element.79), channel_id=1, source_target_pairs={{0,8},{1,9},{2,10},{3,11},{4,12},{5,13},{6,14},{7,15},{16,24},{17,... | collective-permute-start | bytes 294920 | tf_op jit(solution)/shard_map/ppermute | solution.py:547
  22.2 8.2 %collective-permute-start.2 = (f32[48,512]{1,0:T(8,128)S(1)}, f32[48,512]{1,0:T(8,128)S(1)}, u32[]{:S(2)}, u32[]{:S(2)}) collective-permute-start(f32[48,512]{1,0:T(8,128)S(1)} %get-tuple-element.80), channel_id=1, source_target_pairs={{8,16},{9,17},{10,18},{11,19},{12,20},{13,21},{14,22},{15,23},{24,... | collective-permute-start | bytes 294920 | tf_op jit(solution)/shard_map/ppermute | solution.py:548
  25.5 1.0 %copy-start.3 = (f32[16,8,8,128]{3,2,1,0:T(8,128)S(1)}, f32[16,8,8,128]{3,2,1,0:T(8,128)}, u32[]{:S(2)}) copy-start(f32[16,8,8,128]{3,2,1,0:T(8,128)} %get-tuple-element.46.j_ref) | copy-start | bytes 1572868
  26.6 1.3 %copy-start.5 = (f32[27,3,8,512]{3,2,1,0:T(8,128)S(1)}, f32[27,3,8,512]{3,2,1,0:T(8,128)}, u32[]{:S(2)}) copy-start(f32[27,3,8,512]{3,2,1,0:T(8,128)} %get-tuple-element.36.sums) | copy-start | bytes 3981316
  27.9 3.3 %copy-start.4 = (f32[16,8,8,128]{3,2,1,0:T(8,128)S(1)}, f32[16,8,8,128]{3,2,1,0:T(8,128)}, u32[]{:S(2)}) copy-start(f32[16,8,8,128]{3,2,1,0:T(8,128)} %get-tuple-element.46.j_ref) | copy-start | bytes 1572868
  27.9 3.3 %copy-start.6 = (f32[27,3,8,512]{3,2,1,0:T(8,128)S(1)}, f32[27,3,8,512]{3,2,1,0:T(8,128)}, u32[]{:S(2)}) copy-start(f32[27,3,8,512]{3,2,1,0:T(8,128)} %get-tuple-element.36.sums) | copy-start | bytes 3981316
  33.2 9.2 %collective-permute-start.5 = (f32[32,512]{1,0:T(8,128)S(1)}, f32[32,512]{1,0:T(8,128)S(1)}, u32[]{:S(2)}, u32[]{:S(2)}) collective-permute-start(f32[32,512]{1,0:T(8,128)S(1)} %get-tuple-element.91), channel_id=1, source_target_pairs={{1,2},{3,4},{5,6},{7,8},{9,10},{11,12},{13,14},{15,16},{17,18},{19... | collective-permute-start | bytes 196616 | tf_op jit(solution)/shard_map/ppermute | solution.py:548
  39.1 3.3 %collective-permute-start.4 = (f32[32,512]{1,0:T(8,128)S(1)}, f32[32,512]{1,0:T(8,128)S(1)}, u32[]{:S(2)}, u32[]{:S(2)}) collective-permute-start(f32[32,512]{1,0:T(8,128)S(1)} %get-tuple-element.92), channel_id=1, source_target_pairs={{0,1},{2,3},{4,5},{6,7},{8,9},{10,11},{12,13},{14,15},{16,17},{18,... | collective-permute-start | bytes 196616 | tf_op jit(solution)/shard_map/ppermute | solution.py:547
  42.5 4.3 %collective-permute-start.7 = (f32[32,512]{1,0:T(8,128)S(1)}, f32[32,512]{1,0:T(8,128)S(1)}, u32[]{:S(2)}, u32[]{:S(2)}) collective-permute-start(f32[32,512]{1,0:T(8,128)S(1)} %get-tuple-element.85), channel_id=1, source_target_pairs={{0,8},{1,9},{2,10},{3,11},{4,12},{5,13},{6,14},{7,15},{16,24},{17,... | collective-permute-start | bytes 196616 | tf_op jit(solution)/shard_map/ppermute | solution.py:547
  42.6 7.7 %collective-permute-start.6 = (f32[32,512]{1,0:T(8,128)S(1)}, f32[32,512]{1,0:T(8,128)S(1)}, u32[]{:S(2)}, u32[]{:S(2)}) collective-permute-start(f32[32,512]{1,0:T(8,128)S(1)} %get-tuple-element.86), channel_id=1, source_target_pairs={{8,16},{9,17},{10,18},{11,19},{12,20},{13,21},{14,22},{15,23},{24,... | collective-permute-start | bytes 196616 | tf_op jit(solution)/shard_map/ppermute | solution.py:548
  53.2 14.1 %collective-permute-start.9 = (f32[25,8,512]{2,1,0:T(8,128)S(1)}, f32[25,8,512]{2,1,0:T(8,128)S(1)}, u32[]{:S(2)}, u32[]{:S(2)}) collective-permute-start(f32[25,8,512]{2,1,0:T(8,128)S(1)} %get-tuple-element.73), channel_id=1, source_target_pairs={{1,2},{3,4},{5,6},{7,8},{9,10},{11,12},{13,14},{15,16},{17,18},{19... | collective-permute-start | bytes 1228808 | tf_op jit(solution)/shard_map/ppermute | solution.py:548
  57.9 9.3 %collective-permute-start.8 = (f32[25,8,512]{2,1,0:T(8,128)S(1)}, f32[25,8,512]{2,1,0:T(8,128)S(1)}, u32[]{:S(2)}, u32[]{:S(2)}) collective-permute-start(f32[25,8,512]{2,1,0:T(8,128)S(1)} %get-tuple-element.74), channel_id=1, source_target_pairs={{0,1},{2,3},{4,5},{6,7},{8,9},{10,11},{12,13},{14,15},{16,17},{18,... | collective-permute-start | bytes 1228808 | tf_op jit(solution)/shard_map/ppermute | solution.py:547
  68.0 9.8 %collective-permute-start.11 = (f32[7,40,512]{2,1,0:T(8,128)S(1)}, f32[7,40,512]{2,1,0:T(8,128)S(1)}, u32[]{:S(2)}, u32[]{:S(2)}) collective-permute-start(f32[7,40,512]{2,1,0:T(8,128)S(1)} %get-tuple-element.69), channel_id=1, source_target_pairs={{0,8},{1,9},{2,10},{3,11},{4,12},{5,13},{6,14},{7,15},{16,24},{17,... | collective-permute-start | bytes 1720328 | tf_op jit(solution)/shard_map/ppermute | solution.py:547
  68.1 13.1 %collective-permute-start.10 = (f32[7,40,512]{2,1,0:T(8,128)S(1)}, f32[7,40,512]{2,1,0:T(8,128)S(1)}, u32[]{:S(2)}, u32[]{:S(2)}) collective-permute-start(f32[7,40,512]{2,1,0:T(8,128)S(1)} %get-tuple-element.70), channel_id=1, source_target_pairs={{8,16},{9,17},{10,18},{11,19},{12,20},{13,21},{14,22},{15,23},{24,... | collective-permute-start | bytes 1720328 | tf_op jit(solution)/shard_map/ppermute | solution.py:548
  73.7 7.7 %copy-start.8 = (s32[64,16]{0,1:T(8,128)S(1)}, s32[64,16]{0,1:T(8,128)}, u32[]{:S(2)}) copy-start(s32[64,16]{0,1:T(8,128)} %param.7) | copy-start | bytes 12292

commit v5 on v4

--- a/solution.py
+++ b/solution.py
@@ -172,10 +172,10 @@
                 w = flat[pl.ds(ey * 128 + n, 8, stride=16), :]
                 wr = pltpu.roll(w, 64, 1)
                 dj = STEP_SIZE * jv
-                u_ref[n, ey] = dj * jnp.where(lane < 64, w, wr)
-                v_ref[n, ey] = dj * jnp.where(lane < 64, wr, w)
-                j_ref[n, ey] = jv
-                rj_ref[n, ey] = 1.0 / jv
+                u_ref[ey, n] = dj * jnp.where(lane < 64, w, wr)
+                v_ref[ey, n] = dj * jnp.where(lane < 64, wr, w)
+                j_ref[ey, n] = jv
+                rj_ref[ey, n] = 1.0 / jv
                 js.append(jv)
             rd_ref[ey] = 1.0 / weighted(js)
             return 0
@@ -193,11 +193,11 @@
     def rows(ey, _):
         f = [flat[pl.ds(ey * 128 + n, 8, stride=16), :] for n in range(16)]
         for n in range(16):
-            t0[n, ey] = f[n]
+            t0[ey, n] = f[n]
         g = tendency_step(
-            f, lambda n: u_ref[n, ey], lambda n: v_ref[n, ey], lambda n: rj_ref[n, ey]
+            f, lambda n: u_ref[ey, n], lambda n: v_ref[ey, n], lambda n: rj_ref[ey, n]
         )
-        c = limited(g, [j_ref[n, ey] for n in range(16)], rd_ref[ey])
+        c = limited(g, [j_ref[ey, n] for n in range(16)], rd_ref[ey])
         add_nodes(sums, east, ey, c, sub)
         return 0
 
@@ -292,11 +292,12 @@
     return f
 
 
-def stage_row(keep, take, whole, side, t0, u_ref, v_ref, rj_ref, j_ref, rd_ref, ey, sub):
+def stage_row(keep, take, whole, side, t0, u_ref, v_ref, rj_ref, j_ref, rd_ref, ey, sub, at=None):
+    at = ey if at is None else at
     f = element_values(whole, side, ey, sub)
-    h = tendency_step(f, lambda n: u_ref[n, ey], lambda n: v_ref[n, ey], lambda n: rj_ref[n, ey])
-    g = [keep * t0[n, ey] + take * h[n] for n in range(16)]
-    return limited(g, [j_ref[n, ey] for n in range(16)], rd_ref[ey])
+    h = tendency_step(f, lambda n: u_ref[at, n], lambda n: v_ref[at, n], lambda n: rj_ref[at, n])
+    g = [keep * t0[at, n] + take * h[n] for n in range(16)]
+    return limited(g, [j_ref[at, n] for n in range(16)], rd_ref[at])
 
 
 def stage_inner_kernel(
@@ -315,7 +316,7 @@
 
 
 def stage_kernel(
-    keep, take, wide, sums, edge, from_e, from_w, from_n, from_s, inv, t0, u_ref, v_ref, rj_ref, j_ref, rd_ref,
+    keep, take, wide, sums, edge, from_e, from_w, from_n, from_s, inv, t0, u0, v0, rj0, j0, rd0, t7, u7, v7, rj7, j7, rd7,
     inner, inner_column, out, west, east, third, fourth, whole, side,
 ):
     sub = sublane()
@@ -332,8 +333,8 @@
         return 0
 
     lax.fori_loop(3, 22, copy, 0, unroll=19)
-    for ey, joins in ((0, (3,)), (7, (0,))):
-        c = stage_row(keep, take, whole, side, t0, u_ref, v_ref, rj_ref, j_ref, rd_ref, ey, sub)
+    for ey, joins, coefs in ((0, (3,), (t0, u0, v0, rj0, j0, rd0)), (7, (0,), (t7, u7, v7, rj7, j7, rd7))):
+        c = stage_row(keep, take, whole, side, *coefs, ey, sub, 0)
         add_nodes(out, column, ey, c, sub, joins)
     if not wide:
         thin_messages(out, column, west, third, fourth)
@@ -551,16 +552,16 @@
 
 def per_device(tracers, velocity, jacobian, elem_nodes):
     nodes = elem_nodes.T
-    coef = [sds(16, 8, 8, 128)] * 4 + [sds(8, 8, 128)]
-    coef_specs = [fixed(16, 8, 8, 128)] * 4 + [fixed(8, 8, 128)]
+    coef = [sds(8, 16, 8, 128)] * 4 + [sds(8, 8, 128)]
+    coef_specs = [fixed(8, 16, 8, 128)] * 4 + [fixed(8, 8, 128)]
     sums_spec = tiled(27, 3, 8, 128)
     first = pl.pallas_call(
         first_kernel,
         grid=(4,),
         in_specs=[SMEM, fixed(16, 64), tiled(64, 16, 128), fixed(64, 16, 128), fixed(16, 64)],
-        out_specs=[sums_spec, tiled(48, 128), tiled(48, 128), tiled(32, 128), tiled(32, 128), tiled(16, 8, 8, 128)]
+        out_specs=[sums_spec, tiled(48, 128), tiled(48, 128), tiled(32, 128), tiled(32, 128), tiled(8, 16, 8, 128)]
         + coef_specs,
-        out_shape=[sds(27, 3, 8, 512), sds(48, 512), sds(48, 512), sds(32, 512), sds(32, 512), sds(16, 8, 8, 512)]
+        out_shape=[sds(27, 3, 8, 512), sds(48, 512), sds(48, 512), sds(32, 512), sds(32, 512), sds(8, 16, 8, 512)]
         + coef,
         scratch_shapes=[
             pltpu.VMEM((64, 16, 128), F32),
@@ -608,7 +609,7 @@
         return pl.pallas_call(
             functools.partial(stage_inner_kernel, keep, take),
             grid=(4,),
-            in_specs=[sums_spec] + [tiled(rows, 128)] * 3 + [inv_spec, tiled(16, 8, 8, 128)] + coef_specs,
+            in_specs=[sums_spec] + [tiled(rows, 128)] * 3 + [inv_spec, tiled(8, 16, 8, 128)] + coef_specs,
             out_specs=[sums_spec, tiled(32, 128)],
             out_shape=[sds(27, 3, 8, 512), sds(32, 512)],
             scratch_shapes=[pltpu.VMEM((27, 3, 8, 128), F32), pltpu.VMEM((32, 128), F32)],
@@ -618,6 +619,13 @@
             ),
             name="inner_rows",
         )(sums, edge, from_e, from_w, inv, t0, *coefs)
+
+    def one_row(ey):
+        return (
+            [pl.BlockSpec((1, 16, 8, 128), lambda t: (ey, 0, 0, t))]
+            + [pl.BlockSpec((1, 16, 8, 128), lambda t: (ey, 0, 0, 0))] * 4
+            + [pl.BlockSpec((1, 8, 128), lambda t: (ey, 0, 0))]
+        )
 
     def stage(keep, take, wide, sums, edge, from_e, from_w, from_n, from_s, rows, inner):
         if wide:
@@ -631,15 +639,16 @@
             grid=(4,),
             in_specs=[sums_spec]
             + [tiled(rows, 128)] * 5
-            + [inv_spec, tiled(16, 8, 8, 128)]
-            + coef_specs
+            + [inv_spec]
+            + one_row(0)
+            + one_row(7)
             + [sums_spec, tiled(32, 128)],
             out_specs=[sums_spec] + specs,
             out_shape=[sds(27, 3, 8, 512)] + outs,
             scratch_shapes=[pltpu.VMEM((27, 3, 8, 128), F32), pltpu.VMEM((32, 128), F32)],
             compiler_params=PARAMS,
             name="section_three_sums" if wide else "section_two_sums",
-        )(sums, edge, from_e, from_w, from_n, from_s, inv, t0, *coefs, *inner)
+        )(sums, edge, from_e, from_w, from_n, from_s, inv, t0, *coefs, t0, *coefs, *inner)
 
     inner = inner_stage(0.75, 0.25, sums, east, from_e, from_w, inv_inner, 48)
     sums, west, east, north, south = stage(

time: 89.9 us -> 89.5 us (level)
  no operation moved by 1% of the time
where the time goes in v5:
time: 89.5 us; the launch traced here: 89.2 us
  Pallas kernels  32 us (36%)
  waiting for transfers between devices  27.2 us (30%)
  starting transfers between devices  22.8 us (25%)
  local copies, waits for them, and re-layouts  4.59 us (5%)
  other arithmetic  2.37 us (3%)
    ppermute x6, starting transfers between devices, swapped(): lax.ppermute(jnp.where(even, before, after), 'sfc', over + [(j, i) for i,...  22.5 us
    ppermute x6, waiting for transfers between devices, swapped(): lax.ppermute(jnp.where(even, before, after), 'sfc', over + [(j, i) for i,...  21.9 us
    pallas_call x1, Pallas kernels, per_device(): pl.pallas_call(last_kernel, grid=(4,), in_specs=[SMEM, band, band, jac_sp...  8.15 us
    pallas_call x1, Pallas kernels, per_device(): first(nodes, nodes, tracers, velocity, jacobian.T)  7.15 us
    pallas_call x1, Pallas kernels, per_device(): pl.pallas_call(inner_kernel, grid=(4,), in_specs=[sums_spec, tiled(32, 12...  5.44 us
    ppermute x6, waiting for transfers between devices, swapped(): lax.ppermute(jnp.where(even, after, before), 'sfc', up + [(j, i) for i, j...  5.25 us
    pallas_call x2, Pallas kernels, inner_stage(): pl.pallas_call(functools.partial(stage_inner_kernel, keep, take), grid=(4...  4.92 us
    unnamed x20, local copies, waits for them, and re-layouts  4.57 us
  transfers between devices with their start and end apart: 12, of which 7 were waited for; matrix products, arithmetic and copies ran while one was open for 0% of the time, Pallas kernels for 12%

profile of v5, /device:TPU:0, one launch (start us, length us, event | category | flops | bytes accessed | tf_op | source)
XLA Modules:
  0.0 89.2 jit_solution(1861232781166646818)
XLA Ops:
  1.4 7.1 %section_one_sums.1 = (f32[27,3,8,512]{3,2,1,0:T(8,128)}, f32[48,512]{1,0:T(8,128)S(1)}, f32[48,512]{1,0:T(8,128)S(1)}, f32[32,512]{1,0:T(8,128)S(1)}, f32[32,51...) custom-call(s32[16,64]{1,0:T(8,128)S(1)} %bitcast.10, ...), custom_call_target="tpu_custom_call" | custom-call | tf_op jit(solution)/shard_map/section_one_sums/pallas_call | solution.py:575
  8.6 0.8 copy-done.1
  9.4 0.7 broadcast_select_fusion.12
  10.1 8.2 %collective-permute-start.1 = (f32[48,512]{1,0:T(8,128)}, f32[48,512]{1,0:T(8,128)}, u32[]{:S(2)}, u32[]{:S(2)}) collective-permute-start(f32[48,512]{1,0:T(8,128)} %get-tuple-element.83), channel_id=1, source_target_pairs={{1,2},{3,4},{5,6},{7,8},{9,10},{11,12},{13,14},{15,16},{17,18},{19... | collective-permute-start | bytes 294920 | tf_op jit(solution)/shard_map/ppermute | solution.py:549
  18.3 2.6 %collective-permute-done.1 = f32[48,512]{1,0:T(8,128)} collective-permute-done((f32[48,512]{1,0:T(8,128)}, f32[48,512]{1,0:T(8,128)}, u32[]{:S(2)}, u32[]{:S(2)}) %collective-permute-start.1) | collective-permute-done | bytes 98336 | tf_op jit(solution)/shard_map/ppermute | solution.py:549
  20.9 1.0 %broadcast_select_fusion.10 = (f32[48,512]{1,0:T(8,128)S(1)}, f32[48,512]{1,0:T(8,128)S(1)}) fusion(f32[48,512]{1,0:T(8,128)} %collective-permute-done.1, f32[48,512]{1,0:T(8,128)} %collective-permute-done, pred[]{:T(512)S(6)} %eq.35), kind=kLoop, calls=%fused_computation.20 | loop fusion | flops 49152 | bytes 393217 | tf_op jit(solution)/shard_map/jit(_where)/select_n | solution.py:550
  22.1 2.8 %collective-permute-start.2 = (f32[48,512]{1,0:T(8,128)S(1)}, f32[48,512]{1,0:T(8,128)S(1)}, u32[]{:S(2)}, u32[]{:S(2)}) collective-permute-start(f32[48,512]{1,0:T(8,128)S(1)} %get-tuple-element.80), channel_id=1, source_target_pairs={{8,16},{9,17},{10,18},{11,19},{12,20},{13,21},{14,22},{15,23},{24,... | collective-permute-start | bytes 294920 | tf_op jit(solution)/shard_map/ppermute | solution.py:549
  25.4 1.0 %copy-done.3 = f32[8,16,8,128]{3,2,1,0:T(8,128)S(1)} copy-done((f32[8,16,8,128]{3,2,1,0:T(8,128)S(1)}, f32[8,16,8,128]{3,2,1,0:T(8,128)}, u32[]{:S(2)}) %copy-start.3) | copy-done | bytes 524312
  26.5 1.3 %copy-done.5 = f32[27,3,8,512]{3,2,1,0:T(8,128)S(1)} copy-done((f32[27,3,8,512]{3,2,1,0:T(8,128)S(1)}, f32[27,3,8,512]{3,2,1,0:T(8,128)}, u32[]{:S(2)}) %copy-start.5) | copy-done | bytes 1327128
  27.8 2.5 %inner_rows.2 = (f32[27,3,8,512]{3,2,1,0:T(8,128)S(1)}, f32[32,512]{1,0:T(8,128)S(1)}) custom-call(f32[27,3,8,512]{3,2,1,0:T(8,128)S(1)} %copy-done.5, f32[48,512]{1,0:T(8,128)S(1)} %get-tuple-element.37.edge, f32[48,512]{1,0:T(8,128)S(1)} %get-tuple-element.82.from_e, f32[48,512]{1,0:T(8,128)S(1)} %get-tuple-element.81.from_w, ...), custom_call_target="tpu_custom_call" | custom-call | flops 31457280 | bytes 8388608 | tf_op jit(solution)/shard_map/inner_rows/pallas_call | solution.py:609
  30.3 0.8 geometry.1
  31.1 1.8 %section_two_sums.1 = (f32[27,3,8,512]{3,2,1,0:T(8,128)S(1)}, f32[32,512]{1,0:T(8,128)S(1)}, f32[32,512]{1,0:T(8,128)S(1)}, f32[32,512]{1,0:T(8,128)S(1)}, f32[32,512]{1,0:T(8,128)S(1)}) custom-call(f32[27,3,8,512]{3,2,1,0:T(8,128)S(1)} %copy-done.6, f32[48,512]{1,0:T(8,128)S(1)} %get-tuple-element.37.edge, f32[48,512]{1,0:T(8,128)S(1)} %get-tuple-element.82.from_e, ...), custom_call_target="tpu_custom_call" | custom-call | tf_op jit(solution)/shard_map/section_two_sums/pallas_call | solution.py:637
  32.9 6.0 %collective-permute-start.5 = (f32[32,512]{1,0:T(8,128)S(1)}, f32[32,512]{1,0:T(8,128)S(1)}, u32[]{:S(2)}, u32[]{:S(2)}) collective-permute-start(f32[32,512]{1,0:T(8,128)S(1)} %get-tuple-element.91), channel_id=1, source_target_pairs={{1,2},{3,4},{5,6},{7,8},{9,10},{11,12},{13,14},{15,16},{17,18},{19... | collective-permute-start | bytes 196616 | tf_op jit(solution)/shard_map/ppermute | solution.py:549
  38.9 3.2 %collective-permute-done.5 = f32[32,512]{1,0:T(8,128)S(1)} collective-permute-done((f32[32,512]{1,0:T(8,128)S(1)}, f32[32,512]{1,0:T(8,128)S(1)}, u32[]{:S(2)}, u32[]{:S(2)}) %collective-permute-start.5) | collective-permute-done | bytes 65568 | tf_op jit(solution)/shard_map/ppermute | solution.py:549
  43.1 2.5 %inner_rows.3 = (f32[27,3,8,512]{3,2,1,0:T(8,128)S(1)}, f32[32,512]{1,0:T(8,128)S(1)}) custom-call(f32[27,3,8,512]{3,2,1,0:T(8,128)S(1)} %get-tuple-element.50.sums, f32[32,512]{1,0:T(8,128)S(1)} %get-tuple-element.51.edge, f32[32,512]{1,0:T(8,128)S(1)} %get-tuple-element.90.from_e, f32[32,512]{1,0:T(8,128)S(1)} %get-tuple-element.89.from_w, ...), custom_call_target="tpu_custom_call" | custom-call | flops 31457280 | bytes 8388608 | tf_op jit(solution)/shard_map/inner_rows/pallas_call | solution.py:609
  45.5 1.1 %collective-permute-done.7 = f32[32,512]{1,0:T(8,128)S(1)} collective-permute-done((f32[32,512]{1,0:T(8,128)S(1)}, f32[32,512]{1,0:T(8,128)S(1)}, u32[]{:S(2)}, u32[]{:S(2)}) %collective-permute-start.7) | collective-permute-done | bytes 65568 | tf_op jit(solution)/shard_map/ppermute | solution.py:548
  46.6 3.4 %collective-permute-done.6 = f32[32,512]{1,0:T(8,128)S(1)} collective-permute-done((f32[32,512]{1,0:T(8,128)S(1)}, f32[32,512]{1,0:T(8,128)S(1)}, u32[]{:S(2)}, u32[]{:S(2)}) %collective-permute-start.6) | collective-permute-done | bytes 65568 | tf_op jit(solution)/shard_map/ppermute | solution.py:549
  50.0 2.6 %section_three_sums.1 = (f32[27,3,8,512]{3,2,1,0:T(8,128)S(1)}, f32[25,8,512]{2,1,0:T(8,128)S(1)}, f32[25,8,512]{2,1,0:T(8,128)S(1)}, f32[8,512]{1,0:T(8,128)}, f32[32,512]{1,0:T(8,128)S(1)}) custom-call(f32[27,3,8,512]{3,2,1,0:T(8,128)S(1)} %get-tuple-element.50.sums, f32[32,512]{1,0:T(8,128)S(1)} %get-tuple-element.51.edge, ...), custom_call_target="tpu_custom_call" | custom-call | tf_op jit(solution)/shard_map/section_three_sums/pallas_call | solution.py:637
  52.8 4.8 %collective-permute-start.9 = (f32[25,8,512]{2,1,0:T(8,128)S(1)}, f32[25,8,512]{2,1,0:T(8,128)S(1)}, u32[]{:S(2)}, u32[]{:S(2)}) collective-permute-start(f32[25,8,512]{2,1,0:T(8,128)S(1)} %get-tuple-element.73), channel_id=1, source_target_pairs={{1,2},{3,4},{5,6},{7,8},{9,10},{11,12},{13,14},{15,16},{17,18},{19... | collective-permute-start | bytes 1228808 | tf_op jit(solution)/shard_map/ppermute | solution.py:549
  57.6 9.3 %collective-permute-done.9 = f32[25,8,512]{2,1,0:T(8,128)S(1)} collective-permute-done((f32[25,8,512]{2,1,0:T(8,128)S(1)}, f32[25,8,512]{2,1,0:T(8,128)S(1)}, u32[]{:S(2)}, u32[]{:S(2)}) %collective-permute-start.9) | collective-permute-done | bytes 409632 | tf_op jit(solution)/shard_map/ppermute | solution.py:549
  67.9 5.4 %biharmonic_inner_rows.1 = (f32[25,3,16,512]{3,2,1,0:T(8,128)S(1)}, f32[19,3,16,512]{3,2,1,0:T(8,128)S(1)}, f32[13,3,16,512]{3,2,1,0:T(8,128)S(1)}) custom-call(f32[27,3,8,512]{3,2,1,0:T(8,128)S(1)} %get-tuple-element.57.sums, f32[32,512]{1,0:T(8,128)S(1)} %get-tuple-element.58.edge, f32[25,8,512]{2,1,0:T(8,128)S(1)} %get-tuple-element.72.from_e, ...), custom_call_target="tpu_custom_call" | custom-call | flops 31457280 | bytes 16777216 | tf_op jit(solution)/shard_map/biharmonic_inner_rows/pallas_call | solution.py:681
  73.3 4.1 %collective-permute-done.11 = f32[7,40,512]{2,1,0:T(8,128)S(1)} collective-permute-done((f32[7,40,512]{2,1,0:T(8,128)S(1)}, f32[7,40,512]{2,1,0:T(8,128)S(1)}, u32[]{:S(2)}, u32[]{:S(2)}) %collective-permute-start.11) | collective-permute-done | bytes 573472 | tf_op jit(solution)/shard_map/ppermute | solution.py:548
  77.5 3.4 %collective-permute-done.10 = f32[7,40,512]{2,1,0:T(8,128)S(1)} collective-permute-done((f32[7,40,512]{2,1,0:T(8,128)S(1)}, f32[7,40,512]{2,1,0:T(8,128)S(1)}, u32[]{:S(2)}, u32[]{:S(2)}) %collective-permute-start.10) | collective-permute-done | bytes 573472 | tf_op jit(solution)/shard_map/ppermute | solution.py:549
  81.0 8.2 %biharmonic_outer_rows.1 = f32[64,16,512]{2,1,0:T(8,128)} custom-call(s32[16,64]{1,0:T(8,128)S(1)} %bitcast.12, f32[7,40,512]{2,1,0:T(8,128)S(1)} %get-tuple-element.68.from_n, f32[7,40,512]{2,1,0:T(8,128)S(1)} %get-tuple-element.67.from_s, f32[16,12,16,128]{3,2,1,0:T(8,128)S(1)} %get-tuple-element.63.j_ref, f32[37,3,16,128]{3,2,1,0:T(8,128)S(1)} %get-tuple-element.41.inv, ...), custom_call_target="tpu_custom_call" | custom-call | tf_op jit(solution)/shard_map/biharmonic_outer_rows/pallas_call | solution.py:691
  (50 shorter events, 4.3 us)
Async XLA Ops:
  0.0 0.7 copy-start.7
  0.7 0.7 copy-start.9
  8.5 0.8 copy-start.1
  9.4 16.1 %copy-start = (f32[8,16,8,512]{3,2,1,0:T(8,128)S(1)}, f32[8,16,8,512]{3,2,1,0:T(8,128)}, u32[]{:S(2)}) copy-start(f32[8,16,8,512]{3,2,1,0:T(8,128)} %get-tuple-element.42.t0.t7) | copy-start | bytes 6291460
  10.1 10.8 %collective-permute-start.1 = (f32[48,512]{1,0:T(8,128)}, f32[48,512]{1,0:T(8,128)}, u32[]{:S(2)}, u32[]{:S(2)}) collective-permute-start(f32[48,512]{1,0:T(8,128)} %get-tuple-element.83), channel_id=1, source_target_pairs={{1,2},{3,4},{5,6},{7,8},{9,10},{11,12},{13,14},{15,16},{17,18},{19... | collective-permute-start | bytes 294920 | tf_op jit(solution)/shard_map/ppermute | solution.py:549
  18.3 2.6 %collective-permute-start = (f32[48,512]{1,0:T(8,128)}, f32[48,512]{1,0:T(8,128)}, u32[]{:S(2)}, u32[]{:S(2)}) collective-permute-start(f32[48,512]{1,0:T(8,128)} %get-tuple-element.84), channel_id=1, source_target_pairs={{0,1},{2,3},{4,5},{6,7},{8,9},{10,11},{12,13},{14,15},{16,17},{18,... | collective-permute-start | bytes 294920 | tf_op jit(solution)/shard_map/ppermute | solution.py:548
  18.3 7.2 %copy-start.2 = (f32[8,16,8,128]{3,2,1,0:T(8,128)S(1)}, f32[8,16,8,128]{3,2,1,0:T(8,128)}, u32[]{:S(2)}) copy-start(f32[8,16,8,128]{3,2,1,0:T(8,128)} %copy-done.1) | copy-start | bytes 1572868
  22.0 8.2 %collective-permute-start.3 = (f32[48,512]{1,0:T(8,128)S(1)}, f32[48,512]{1,0:T(8,128)S(1)}, u32[]{:S(2)}, u32[]{:S(2)}) collective-permute-start(f32[48,512]{1,0:T(8,128)S(1)} %get-tuple-element.79), channel_id=1, source_target_pairs={{0,8},{1,9},{2,10},{3,11},{4,12},{5,13},{6,14},{7,15},{16,24},{17,... | collective-permute-start | bytes 294920 | tf_op jit(solution)/shard_map/ppermute | solution.py:548
  22.1 8.2 %collective-permute-start.2 = (f32[48,512]{1,0:T(8,128)S(1)}, f32[48,512]{1,0:T(8,128)S(1)}, u32[]{:S(2)}, u32[]{:S(2)}) collective-permute-start(f32[48,512]{1,0:T(8,128)S(1)} %get-tuple-element.80), channel_id=1, source_target_pairs={{8,16},{9,17},{10,18},{11,19},{12,20},{13,21},{14,22},{15,23},{24,... | collective-permute-start | bytes 294920 | tf_op jit(solution)/shard_map/ppermute | solution.py:549
  25.4 1.0 %copy-start.3 = (f32[8,16,8,128]{3,2,1,0:T(8,128)S(1)}, f32[8,16,8,128]{3,2,1,0:T(8,128)}, u32[]{:S(2)}) copy-start(f32[8,16,8,128]{3,2,1,0:T(8,128)} %get-tuple-element.46.j_ref.j0.j7) | copy-start | bytes 1572868
  26.5 1.3 %copy-start.5 = (f32[27,3,8,512]{3,2,1,0:T(8,128)S(1)}, f32[27,3,8,512]{3,2,1,0:T(8,128)}, u32[]{:S(2)}) copy-start(f32[27,3,8,512]{3,2,1,0:T(8,128)} %get-tuple-element.36.sums) | copy-start | bytes 3981316
  27.8 3.3 %copy-start.4 = (f32[8,16,8,128]{3,2,1,0:T(8,128)S(1)}, f32[8,16,8,128]{3,2,1,0:T(8,128)}, u32[]{:S(2)}) copy-start(f32[8,16,8,128]{3,2,1,0:T(8,128)} %get-tuple-element.46.j_ref.j0.j7) | copy-start | bytes 1572868
  27.8 3.3 %copy-start.6 = (f32[27,3,8,512]{3,2,1,0:T(8,128)S(1)}, f32[27,3,8,512]{3,2,1,0:T(8,128)}, u32[]{:S(2)}) copy-start(f32[27,3,8,512]{3,2,1,0:T(8,128)} %get-tuple-element.36.sums) | copy-start | bytes 3981316
  32.9 9.2 %collective-permute-start.5 = (f32[32,512]{1,0:T(8,128)S(1)}, f32[32,512]{1,0:T(8,128)S(1)}, u32[]{:S(2)}, u32[]{:S(2)}) collective-permute-start(f32[32,512]{1,0:T(8,128)S(1)} %get-tuple-element.91), channel_id=1, source_target_pairs={{1,2},{3,4},{5,6},{7,8},{9,10},{11,12},{13,14},{15,16},{17,18},{19... | collective-permute-start | bytes 196616 | tf_op jit(solution)/shard_map/ppermute | solution.py:549
  38.9 3.3 %collective-permute-start.4 = (f32[32,512]{1,0:T(8,128)S(1)}, f32[32,512]{1,0:T(8,128)S(1)}, u32[]{:S(2)}, u32[]{:S(2)}) collective-permute-start(f32[32,512]{1,0:T(8,128)S(1)} %get-tuple-element.92), channel_id=1, source_target_pairs={{0,1},{2,3},{4,5},{6,7},{8,9},{10,11},{12,13},{14,15},{16,17},{18,... | collective-permute-start | bytes 196616 | tf_op jit(solution)/shard_map/ppermute | solution.py:548
  42.3 4.3 %collective-permute-start.7 = (f32[32,512]{1,0:T(8,128)S(1)}, f32[32,512]{1,0:T(8,128)S(1)}, u32[]{:S(2)}, u32[]{:S(2)}) collective-permute-start(f32[32,512]{1,0:T(8,128)S(1)} %get-tuple-element.85), channel_id=1, source_target_pairs={{0,8},{1,9},{2,10},{3,11},{4,12},{5,13},{6,14},{7,15},{16,24},{17,... | collective-permute-start | bytes 196616 | tf_op jit(solution)/shard_map/ppermute | solution.py:548
  42.4 7.7 %collective-permute-start.6 = (f32[32,512]{1,0:T(8,128)S(1)}, f32[32,512]{1,0:T(8,128)S(1)}, u32[]{:S(2)}, u32[]{:S(2)}) collective-permute-start(f32[32,512]{1,0:T(8,128)S(1)} %get-tuple-element.86), channel_id=1, source_target_pairs={{8,16},{9,17},{10,18},{11,19},{12,20},{13,21},{14,22},{15,23},{24,... | collective-permute-start | bytes 196616 | tf_op jit(solution)/shard_map/ppermute | solution.py:549
  52.8 14.1 %collective-permute-start.9 = (f32[25,8,512]{2,1,0:T(8,128)S(1)}, f32[25,8,512]{2,1,0:T(8,128)S(1)}, u32[]{:S(2)}, u32[]{:S(2)}) collective-permute-start(f32[25,8,512]{2,1,0:T(8,128)S(1)} %get-tuple-element.73), channel_id=1, source_target_pairs={{1,2},{3,4},{5,6},{7,8},{9,10},{11,12},{13,14},{15,16},{17,18},{19... | collective-permute-start | bytes 1228808 | tf_op jit(solution)/shard_map/ppermute | solution.py:549
  57.6 9.3 %collective-permute-start.8 = (f32[25,8,512]{2,1,0:T(8,128)S(1)}, f32[25,8,512]{2,1,0:T(8,128)S(1)}, u32[]{:S(2)}, u32[]{:S(2)}) collective-permute-start(f32[25,8,512]{2,1,0:T(8,128)S(1)} %get-tuple-element.74), channel_id=1, source_target_pairs={{0,1},{2,3},{4,5},{6,7},{8,9},{10,11},{12,13},{14,15},{16,17},{18,... | collective-permute-start | bytes 1228808 | tf_op jit(solution)/shard_map/ppermute | solution.py:548
  67.7 9.8 %collective-permute-start.11 = (f32[7,40,512]{2,1,0:T(8,128)S(1)}, f32[7,40,512]{2,1,0:T(8,128)S(1)}, u32[]{:S(2)}, u32[]{:S(2)}) collective-permute-start(f32[7,40,512]{2,1,0:T(8,128)S(1)} %get-tuple-element.69), channel_id=1, source_target_pairs={{0,8},{1,9},{2,10},{3,11},{4,12},{5,13},{6,14},{7,15},{16,24},{17,... | collective-permute-start | bytes 1720328 | tf_op jit(solution)/shard_map/ppermute | solution.py:548
  67.8 13.1 %collective-permute-start.10 = (f32[7,40,512]{2,1,0:T(8,128)S(1)}, f32[7,40,512]{2,1,0:T(8,128)S(1)}, u32[]{:S(2)}, u32[]{:S(2)}) collective-permute-start(f32[7,40,512]{2,1,0:T(8,128)S(1)} %get-tuple-element.70), channel_id=1, source_target_pairs={{8,16},{9,17},{10,18},{11,19},{12,20},{13,21},{14,22},{15,23},{24,... | collective-permute-start | bytes 1720328 | tf_op jit(solution)/shard_map/ppermute | solution.py:549
  73.3 7.7 %copy-start.8 = (s32[64,16]{0,1:T(8,128)S(1)}, s32[64,16]{0,1:T(8,128)}, u32[]{:S(2)}) copy-start(s32[64,16]{0,1:T(8,128)} %param.7) | copy-start | bytes 12292

commit v6 on v4

--- a/solution.py
+++ b/solution.py
@@ -373,32 +373,37 @@
             out[k, 32:40] = jnp.where((sub < 2) | (sub >= 6), b1, roll(b2, 4))
 
 
-def laplace_core(f, jac):
+def laplace_core(f, jac, nonzero=range(4)):
     out = [None] * 16
-    for j in range(4):
+    for j in nonzero:
         d = line(*[f(4 * j + i) for i in range(4)])
         out[4 * j : 4 * j + 4] = line(*[jac(4 * j + i) * d[i] for i in range(4)])
     for i in range(4):
-        d = line(*[f(4 * j + i) for j in range(4)])
+        if len(nonzero) == 4:
+            d = line(*[f(4 * j + i) for j in range(4)])
+        else:
+            (k,) = nonzero
+            d = [float(D[j, k]) * f(4 * k + i) for j in range(4)]
         d = line(*[jac(4 * j + i) * d[j] for j in range(4)])
         for j in range(4):
-            out[4 * j + i] = out[4 * j + i] + d[j]
+            n = 4 * j + i
+            out[n] = d[j] if out[n] is None else out[n] + d[j]
     return out
 
 
 FIRST, JOIN, SKIP = range(3)
 
 
-def laplace_row(src, j_ref, inv, dst, r, top, bottom, sub, at=(0, 0), narrow=False, only=range(4)):
-    fa, fb = ([], [])
-    for j in range(4):
+def laplace_row(src, j_ref, inv, dst, r, top, bottom, sub, at=(0, 0), narrow=False, only=range(4), nonzero=range(4)):
+    fa, fb = ([None] * 16, [None] * 16)
+    for j in nonzero:
         y = 3 * r + j - at[0]
         pa, pb = (src[y, 0, 0:8], src[y, 0, 8:16])
         ra, rb = (roll(pa, 7), roll(pb, 7))
-        fa += [pa, src[y, 1, 0:8], src[y, 2, 0:8], jnp.where(sub == 7, rb, ra)]
-        fb += [pb, src[y, 1, 8:16], src[y, 2, 8:16], jnp.where(sub == 7, ra, rb)]
-    ca = laplace_core(lambda n: fa[n], lambda n: j_ref[n, r, 0:8])
-    cb = laplace_core(lambda n: fb[n], lambda n: j_ref[n, r, 8:16])
+        fa[4 * j : 4 * j + 4] = [pa, src[y, 1, 0:8], src[y, 2, 0:8], jnp.where(sub == 7, rb, ra)]
+        fb[4 * j : 4 * j + 4] = [pb, src[y, 1, 8:16], src[y, 2, 8:16], jnp.where(sub == 7, ra, rb)]
+    ca = laplace_core(lambda n: fa[n], lambda n: j_ref[n, r, 0:8], nonzero)
+    cb = laplace_core(lambda n: fb[n], lambda n: j_ref[n, r, 8:16], nonzero)
     for j in range(4):
         what = {0: top, 3: bottom}.get(j)
         if what == SKIP or j not in only:
@@ -433,27 +438,25 @@
     lax.fori_loop(first, last, body, 0)
 
 
-def inner_kernel(sums, edge, from_e, from_w, j_ref, inv, field, one, two):
+def inner_kernel(sums, edge, from_e, from_w, j_ref, inv, field, ends, two, one):
     sub = sublane()
     own_rows(sums, edge, from_e, from_w, inv, field, 0, 25, sub)
-    laplace_row(field, j_ref, inv, one, 3, FIRST, FIRST, sub, (6, 9))
-
-    def rows_one(r, _):
-        laplace_row(field, j_ref, inv, one, r, JOIN, FIRST, sub, (6, 9))
-        return 0
-
-    lax.fori_loop(4, 9, rows_one, 0, unroll=5)
-    laplace_row(one, j_ref, inv, two, 4, FIRST, FIRST, sub, (9, 12), True)
-
-    def rows_two(r, _):
-        laplace_row(one, j_ref, inv, two, r, JOIN, FIRST, sub, (9, 12), True)
-        return 0
-
-    lax.fori_loop(5, 8, rows_two, 0, unroll=3)
+    for src, dst, narrow in ((field, one, False), (one, two, True)):
+
+        def rows(r, _, src=src, dst=dst, narrow=narrow):
+            laplace_row(src, j_ref, inv, dst, r, JOIN, FIRST, sub, (6, 6), narrow)
+            return 0
+
+        laplace_row(src, j_ref, inv, dst, 2, None, FIRST, sub, (6, 6), narrow)
+        lax.fori_loop(3, 9, rows, 0, unroll=3)
+        laplace_row(src, j_ref, inv, dst, 9, JOIN, None, sub, (6, 6), narrow)
+    for ii in range(3):
+        ends[0, ii] = one[0, ii]
+        ends[1, ii] = one[24, ii]
 
 
 def last_kernel(
-    nodes, from_n, from_s, j_ref, inv, field_in, one_in, two_in, out, field, one, two, spread, spots
+    nodes, from_n, from_s, j_ref, inv, field_in, ends, two_in, out, field, one, two, beyond, spread, spots
 ):
     sub = sublane()
 
@@ -478,23 +481,37 @@
             for ii in range(3):
                 a, b = (parts[2 * ii] * inv[y, ii, 0:8], parts[2 * ii + 1] * inv[y, ii, 8:16])
                 if k == shared:
+                    beyond[y // 30, ii, 0:8] = a
+                    beyond[y // 30, ii, 8:16] = b
                     a, b = (a + field[y, ii, 0:8], b + field[y, ii, 8:16])
                 field[y, ii, 0:8] = a
                 field[y, ii, 8:16] = b
-    copy_rows(one_in, one, 9, 28)
-    laplace_row(field, j_ref, inv, one, 0, SKIP, FIRST, sub, only=(3,))
-    laplace_row(field, j_ref, inv, one, 1, JOIN, FIRST, sub)
-    laplace_row(field, j_ref, inv, one, 2, JOIN, JOIN, sub)
-    laplace_row(field, j_ref, inv, one, 9, JOIN, FIRST, sub)
-    laplace_row(field, j_ref, inv, one, 10, JOIN, FIRST, sub)
-    laplace_row(field, j_ref, inv, one, 11, JOIN, SKIP, sub, only=(0,))
-    copy_rows(two_in, two, 12, 25)
-    laplace_row(one, j_ref, inv, two, 1, SKIP, FIRST, sub, narrow=True, only=(3,))
-    laplace_row(one, j_ref, inv, two, 2, JOIN, FIRST, sub, narrow=True)
-    laplace_row(one, j_ref, inv, two, 3, JOIN, JOIN, sub, narrow=True)
-    laplace_row(one, j_ref, inv, two, 8, JOIN, FIRST, sub, narrow=True)
-    laplace_row(one, j_ref, inv, two, 9, JOIN, FIRST, sub, narrow=True)
-    laplace_row(one, j_ref, inv, two, 10, JOIN, SKIP, sub, narrow=True, only=(0,))
+    def row(src, dst, r, top, bottom, **more):
+        laplace_row(src, j_ref, inv, dst, r, top, bottom, sub, **more)
+
+    row(field, one, 0, SKIP, FIRST, only=(3,))
+    row(field, one, 1, JOIN, FIRST)
+    row(beyond, one, 2, JOIN, None, at=(6, 0), nonzero=(0,))
+    row(beyond, one, 9, None, FIRST, at=(29, 0), nonzero=(3,))
+    row(field, one, 10, JOIN, FIRST)
+    row(field, one, 11, JOIN, SKIP, only=(0,))
+    row(one, two, 2, FIRST, FIRST, narrow=True)
+    row(one, two, 3, JOIN, None, narrow=True, nonzero=(0,))
+    row(one, two, 8, None, FIRST, narrow=True, nonzero=(3,))
+    row(one, two, 9, JOIN, FIRST, narrow=True)
+    for ii in range(3):
+        one[6, ii] = one[6, ii] + ends[0, ii]
+        one[30, ii] = one[30, ii] + ends[1, ii]
+    row(one, two, 1, SKIP, JOIN, narrow=True, only=(3,))
+    row(one, two, 10, JOIN, SKIP, narrow=True, only=(0,))
+    for y in (*range(6, 13), *range(24, 31)):
+        two[y, 0] = two[y, 0] + two_in[y - 6, 0]
+        for ii in (1, 2):
+            two[y, ii, 0:8] = two[y, ii, 0:8] + two_in[y - 6, ii, 0:8]
+    for y in range(13, 24):
+        two[y, 0] = two_in[y - 6, 0]
+        for ii in (1, 2):
+            two[y, ii, 0:8] = two_in[y - 6, ii, 0:8]
     flat = spread.reshape(1024, 128)
 
     def finish(ey, _):
@@ -667,14 +684,15 @@
         name="row_bands",
     )(sums, edge, from_e, from_w)
     from_n, from_s = swapped(msg_n, msg_s, PX)
-    grown = [(25, 3, 16), (19, 3, 16), (13, 3, 16)]
+    grown = [(25, 3, 16), (2, 3, 16), (25, 3, 16)]
     flops = 64 * 16 * 512 * 60
-    field, one, two = pl.pallas_call(
+    field, ends, two = pl.pallas_call(
         inner_kernel,
         grid=(4,),
         in_specs=[sums_spec, tiled(32, 128), message, message, jac_spec, inv_spec],
         out_specs=[tiled(*g, 128) for g in grown],
         out_shape=[sds(*g, 512) for g in grown],
+        scratch_shapes=[pltpu.VMEM((25, 3, 16, 128), F32)],
         compiler_params=PARAMS,
         cost_estimate=pl.CostEstimate(flops=flops, bytes_accessed=16 * 1024 * 1024, transcendentals=0),
         name="biharmonic_inner_rows",
@@ -686,10 +704,10 @@
         out_specs=tiled(64, 16, 128),
         out_shape=sds(64, 16, 512),
         scratch_shapes=[pltpu.VMEM((37, 3, 16, 128), F32)] * 3
-        + [pltpu.VMEM((64, 16, 128), F32), pltpu.SMEM((64,), jnp.int32)],
+        + [pltpu.VMEM((2, 3, 16, 128), F32), pltpu.VMEM((64, 16, 128), F32), pltpu.SMEM((64,), jnp.int32)],
         compiler_params=PARAMS,
         name="biharmonic_outer_rows",
-    )(nodes, from_n, from_s, jac, inv, field, one, two)
+    )(nodes, from_n, from_s, jac, inv, field, ends, two)
 
 
 def solution(mesh):

time: 89.9 us -> 88.8 us (0.988)
  waiting for transfers between devices: 27.2 us -> 25.1 us
  Pallas kernels: 32.4 us -> 33.3 us
    pallas_call x1, Pallas kernels: 5.44 us -> 7.53 us  [per_device(): pl.pallas_call(inner_kernel, grid=(4,), in_specs=[sums_spec, tiled(32, 12...]
    ppermute x6, waiting for transfers between devices: 5.22 us -> 3.15 us  [swapped(): lax.ppermute(jnp.where(even, after, before), 'sfc', up + [(j, i) for i, j...]
    pallas_call x1, Pallas kernels: 8.15 us -> 6.95 us  [per_device(): pl.pallas_call(last_kernel, grid=(4,), in_specs=[SMEM, band, band, jac_sp...]
  transfers between devices with their start and end apart: 12 -> 12, of which waited for: 7 -> 7; matrix products, arithmetic and copies ran while one was open for 0% -> 0% of each run, Pallas kernels for 12% -> 15%
where the time goes in v6:
time: 88.8 us; the launch traced here: 88.4 us
  Pallas kernels  33.3 us (37%)
  waiting for transfers between devices  25.1 us (28%)
  starting transfers between devices  22.7 us (26%)
  local copies, waits for them, and re-layouts  4.59 us (5%)
  other arithmetic  2.36 us (3%)
    ppermute x6, starting transfers between devices, swapped(): lax.ppermute(jnp.where(even, before, after), 'sfc', over + [(j, i) for i,...  22.5 us
    ppermute x6, waiting for transfers between devices, swapped(): lax.ppermute(jnp.where(even, before, after), 'sfc', over + [(j, i) for i,...  22 us
    pallas_call x1, Pallas kernels, per_device(): pl.pallas_call(inner_kernel, grid=(4,), in_specs=[sums_spec, tiled(32, 12...  7.53 us
    pallas_call x1, Pallas kernels, per_device(): first(nodes, nodes, tracers, velocity, jacobian.T)  7.23 us
    pallas_call x1, Pallas kernels, per_device(): pl.pallas_call(last_kernel, grid=(4,), in_specs=[SMEM, band, band, jac_sp...  6.95 us
    pallas_call x2, Pallas kernels, inner_stage(): pl.pallas_call(functools.partial(stage_inner_kernel, keep, take), grid=(4...  4.96 us
    pallas_call x2, Pallas kernels, stage(): pl.pallas_call(functools.partial(stage_kernel, keep, take, wide), grid=(4...  4.71 us
    unnamed x20, local copies, waits for them, and re-layouts  4.57 us
  transfers between devices with their start and end apart: 12, of which 7 were waited for; matrix products, arithmetic and copies ran while one was open for 0% of the time, Pallas kernels for 15%

profile of v6, /device:TPU:0, one launch (start us, length us, event | category | flops | bytes accessed | tf_op | source)
XLA Modules:
  0.0 88.4 jit_solution(12372768819540710609)
XLA Ops:
  1.4 7.2 %section_one_sums.1 = (f32[27,3,8,512]{3,2,1,0:T(8,128)}, f32[48,512]{1,0:T(8,128)S(1)}, f32[48,512]{1,0:T(8,128)S(1)}, f32[32,512]{1,0:T(8,128)S(1)}, f32[32,51...) custom-call(s32[16,64]{1,0:T(8,128)S(1)} %bitcast.10, ...), custom_call_target="tpu_custom_call" | custom-call | tf_op jit(solution)/shard_map/section_one_sums/pallas_call | solution.py:591
  8.6 0.8 copy-done.1
  9.4 0.7 broadcast_select_fusion.12
  10.1 8.2 %collective-permute-start.1 = (f32[48,512]{1,0:T(8,128)}, f32[48,512]{1,0:T(8,128)}, u32[]{:S(2)}, u32[]{:S(2)}) collective-permute-start(f32[48,512]{1,0:T(8,128)} %get-tuple-element.83), channel_id=1, source_target_pairs={{1,2},{3,4},{5,6},{7,8},{9,10},{11,12},{13,14},{15,16},{17,18},{19... | collective-permute-start | bytes 294920 | tf_op jit(solution)/shard_map/ppermute | solution.py:565
  18.4 2.6 %collective-permute-done.1 = f32[48,512]{1,0:T(8,128)} collective-permute-done((f32[48,512]{1,0:T(8,128)}, f32[48,512]{1,0:T(8,128)}, u32[]{:S(2)}, u32[]{:S(2)}) %collective-permute-start.1) | collective-permute-done | bytes 98336 | tf_op jit(solution)/shard_map/ppermute | solution.py:565
  21.0 1.0 %broadcast_select_fusion.10 = (f32[48,512]{1,0:T(8,128)S(1)}, f32[48,512]{1,0:T(8,128)S(1)}) fusion(f32[48,512]{1,0:T(8,128)} %collective-permute-done.1, f32[48,512]{1,0:T(8,128)} %collective-permute-done, pred[]{:T(512)S(6)} %eq.35), kind=kLoop, calls=%fused_computation.20 | loop fusion | flops 49152 | bytes 393217 | tf_op jit(solution)/shard_map/jit(_where)/select_n | solution.py:566
  22.2 2.8 %collective-permute-start.2 = (f32[48,512]{1,0:T(8,128)S(1)}, f32[48,512]{1,0:T(8,128)S(1)}, u32[]{:S(2)}, u32[]{:S(2)}) collective-permute-start(f32[48,512]{1,0:T(8,128)S(1)} %get-tuple-element.80), channel_id=1, source_target_pairs={{8,16},{9,17},{10,18},{11,19},{12,20},{13,21},{14,22},{15,23},{24,... | collective-permute-start | bytes 294920 | tf_op jit(solution)/shard_map/ppermute | solution.py:565
  25.5 1.0 %copy-done.3 = f32[16,8,8,128]{3,2,1,0:T(8,128)S(1)} copy-done((f32[16,8,8,128]{3,2,1,0:T(8,128)S(1)}, f32[16,8,8,128]{3,2,1,0:T(8,128)}, u32[]{:S(2)}) %copy-start.3) | copy-done | bytes 524312
  26.6 1.3 %copy-done.5 = f32[27,3,8,512]{3,2,1,0:T(8,128)S(1)} copy-done((f32[27,3,8,512]{3,2,1,0:T(8,128)S(1)}, f32[27,3,8,512]{3,2,1,0:T(8,128)}, u32[]{:S(2)}) %copy-start.5) | copy-done | bytes 1327128
  27.9 2.5 %inner_rows.2 = (f32[27,3,8,512]{3,2,1,0:T(8,128)S(1)}, f32[32,512]{1,0:T(8,128)S(1)}) custom-call(f32[27,3,8,512]{3,2,1,0:T(8,128)S(1)} %copy-done.5, f32[48,512]{1,0:T(8,128)S(1)} %get-tuple-element.37.edge, f32[48,512]{1,0:T(8,128)S(1)} %get-tuple-element.82.from_e, f32[48,512]{1,0:T(8,128)S(1)} %get-tuple-element.81.from_w, ...), custom_call_target="tpu_custom_call" | custom-call | flops 31457280 | bytes 8388608 | tf_op jit(solution)/shard_map/inner_rows/pallas_call | solution.py:625
  30.4 0.8 geometry.1
  31.2 1.9 %section_two_sums.1 = (f32[27,3,8,512]{3,2,1,0:T(8,128)S(1)}, f32[32,512]{1,0:T(8,128)S(1)}, f32[32,512]{1,0:T(8,128)S(1)}, f32[32,512]{1,0:T(8,128)S(1)}, f32[32,512]{1,0:T(8,128)S(1)}) custom-call(f32[27,3,8,512]{3,2,1,0:T(8,128)S(1)} %copy-done.6, f32[48,512]{1,0:T(8,128)S(1)} %get-tuple-element.37.edge, f32[48,512]{1,0:T(8,128)S(1)} %get-tuple-element.82.from_e, ...), custom_call_target="tpu_custom_call" | custom-call | tf_op jit(solution)/shard_map/section_two_sums/pallas_call | solution.py:646
  33.2 5.9 %collective-permute-start.5 = (f32[32,512]{1,0:T(8,128)S(1)}, f32[32,512]{1,0:T(8,128)S(1)}, u32[]{:S(2)}, u32[]{:S(2)}) collective-permute-start(f32[32,512]{1,0:T(8,128)S(1)} %get-tuple-element.91), channel_id=1, source_target_pairs={{1,2},{3,4},{5,6},{7,8},{9,10},{11,12},{13,14},{15,16},{17,18},{19... | collective-permute-start | bytes 196616 | tf_op jit(solution)/shard_map/ppermute | solution.py:565
  39.1 3.3 %collective-permute-done.5 = f32[32,512]{1,0:T(8,128)S(1)} collective-permute-done((f32[32,512]{1,0:T(8,128)S(1)}, f32[32,512]{1,0:T(8,128)S(1)}, u32[]{:S(2)}, u32[]{:S(2)}) %collective-permute-start.5) | collective-permute-done | bytes 65568 | tf_op jit(solution)/shard_map/ppermute | solution.py:565
  43.3 2.5 %inner_rows.3 = (f32[27,3,8,512]{3,2,1,0:T(8,128)S(1)}, f32[32,512]{1,0:T(8,128)S(1)}) custom-call(f32[27,3,8,512]{3,2,1,0:T(8,128)S(1)} %get-tuple-element.50.sums, f32[32,512]{1,0:T(8,128)S(1)} %get-tuple-element.51.edge, f32[32,512]{1,0:T(8,128)S(1)} %get-tuple-element.90.from_e, f32[32,512]{1,0:T(8,128)S(1)} %get-tuple-element.89.from_w, ...), custom_call_target="tpu_custom_call" | custom-call | flops 31457280 | bytes 8388608 | tf_op jit(solution)/shard_map/inner_rows/pallas_call | solution.py:625
  45.8 1.1 %collective-permute-done.7 = f32[32,512]{1,0:T(8,128)S(1)} collective-permute-done((f32[32,512]{1,0:T(8,128)S(1)}, f32[32,512]{1,0:T(8,128)S(1)}, u32[]{:S(2)}, u32[]{:S(2)}) %collective-permute-start.7) | collective-permute-done | bytes 65568 | tf_op jit(solution)/shard_map/ppermute | solution.py:564
  46.9 3.4 %collective-permute-done.6 = f32[32,512]{1,0:T(8,128)S(1)} collective-permute-done((f32[32,512]{1,0:T(8,128)S(1)}, f32[32,512]{1,0:T(8,128)S(1)}, u32[]{:S(2)}, u32[]{:S(2)}) %collective-permute-start.6) | collective-permute-done | bytes 65568 | tf_op jit(solution)/shard_map/ppermute | solution.py:565
  50.3 2.8 %section_three_sums.1 = (f32[27,3,8,512]{3,2,1,0:T(8,128)S(1)}, f32[25,8,512]{2,1,0:T(8,128)S(1)}, f32[25,8,512]{2,1,0:T(8,128)S(1)}, f32[8,512]{1,0:T(8,128)}, f32[32,512]{1,0:T(8,128)S(1)}) custom-call(f32[27,3,8,512]{3,2,1,0:T(8,128)S(1)} %get-tuple-element.50.sums, f32[32,512]{1,0:T(8,128)S(1)} %get-tuple-element.51.edge, ...), custom_call_target="tpu_custom_call" | custom-call | tf_op jit(solution)/shard_map/section_three_sums/pallas_call | solution.py:646
  53.2 4.8 %collective-permute-start.9 = (f32[25,8,512]{2,1,0:T(8,128)S(1)}, f32[25,8,512]{2,1,0:T(8,128)S(1)}, u32[]{:S(2)}, u32[]{:S(2)}) collective-permute-start(f32[25,8,512]{2,1,0:T(8,128)S(1)} %get-tuple-element.73), channel_id=1, source_target_pairs={{1,2},{3,4},{5,6},{7,8},{9,10},{11,12},{13,14},{15,16},{17,18},{19... | collective-permute-start | bytes 1228808 | tf_op jit(solution)/shard_map/ppermute | solution.py:565
  58.0 9.3 %collective-permute-done.9 = f32[25,8,512]{2,1,0:T(8,128)S(1)} collective-permute-done((f32[25,8,512]{2,1,0:T(8,128)S(1)}, f32[25,8,512]{2,1,0:T(8,128)S(1)}, u32[]{:S(2)}, u32[]{:S(2)}) %collective-permute-start.9) | collective-permute-done | bytes 409632 | tf_op jit(solution)/shard_map/ppermute | solution.py:565
  68.3 7.5 %biharmonic_inner_rows.1 = (f32[25,3,16,512]{3,2,1,0:T(8,128)S(1)}, f32[2,3,16,512]{3,2,1,0:T(8,128)S(1)}, f32[25,3,16,512]{3,2,1,0:T(8,128)S(1)}) custom-call(f32[27,3,8,512]{3,2,1,0:T(8,128)S(1)} %get-tuple-element.57.sums, f32[32,512]{1,0:T(8,128)S(1)} %get-tuple-element.58.edge, f32[25,8,512]{2,1,0:T(8,128)S(1)} %get-tuple-element.72.from_e, ...), custom_call_target="tpu_custom_call" | custom-call | flops 31457280 | bytes 16777216 | tf_op jit(solution)/shard_map/biharmonic_inner_rows/pallas_call | solution.py:689
  75.8 2.1 %collective-permute-done.11 = f32[7,40,512]{2,1,0:T(8,128)S(1)} collective-permute-done((f32[7,40,512]{2,1,0:T(8,128)S(1)}, f32[7,40,512]{2,1,0:T(8,128)S(1)}, u32[]{:S(2)}, u32[]{:S(2)}) %collective-permute-start.11) | collective-permute-done | bytes 573472 | tf_op jit(solution)/shard_map/ppermute | solution.py:564
  77.9 3.4 %collective-permute-done.10 = f32[7,40,512]{2,1,0:T(8,128)S(1)} collective-permute-done((f32[7,40,512]{2,1,0:T(8,128)S(1)}, f32[7,40,512]{2,1,0:T(8,128)S(1)}, u32[]{:S(2)}, u32[]{:S(2)}) %collective-permute-start.10) | collective-permute-done | bytes 573472 | tf_op jit(solution)/shard_map/ppermute | solution.py:565
  81.4 7.0 %biharmonic_outer_rows.1 = f32[64,16,512]{2,1,0:T(8,128)} custom-call(s32[16,64]{1,0:T(8,128)S(1)} %bitcast.12, f32[7,40,512]{2,1,0:T(8,128)S(1)} %get-tuple-element.68.from_n, f32[7,40,512]{2,1,0:T(8,128)S(1)} %get-tuple-element.67.from_s, f32[16,12,16,128]{3,2,1,0:T(8,128)S(1)} %get-tuple-element.63.j_ref, f32[37,3,16,128]{3,2,1,0:T(8,128)S(1)} %get-tuple-element.41.inv, ...), custom_call_target="tpu_custom_call" | custom-call | tf_op jit(solution)/shard_map/biharmonic_outer_rows/pallas_call | solution.py:700
  (50 shorter events, 4.3 us)
Async XLA Ops:
  0.0 0.7 copy-start.7
  0.7 0.7 copy-start.9
  8.6 0.8 copy-start.1
  9.4 16.1 %copy-start = (f32[16,8,8,512]{3,2,1,0:T(8,128)S(1)}, f32[16,8,8,512]{3,2,1,0:T(8,128)}, u32[]{:S(2)}) copy-start(f32[16,8,8,512]{3,2,1,0:T(8,128)} %get-tuple-element.42.t0) | copy-start | bytes 6291460
  10.1 10.8 %collective-permute-start.1 = (f32[48,512]{1,0:T(8,128)}, f32[48,512]{1,0:T(8,128)}, u32[]{:S(2)}, u32[]{:S(2)}) collective-permute-start(f32[48,512]{1,0:T(8,128)} %get-tuple-element.83), channel_id=1, source_target_pairs={{1,2},{3,4},{5,6},{7,8},{9,10},{11,12},{13,14},{15,16},{17,18},{19... | collective-permute-start | bytes 294920 | tf_op jit(solution)/shard_map/ppermute | solution.py:565
  18.3 2.6 %collective-permute-start = (f32[48,512]{1,0:T(8,128)}, f32[48,512]{1,0:T(8,128)}, u32[]{:S(2)}, u32[]{:S(2)}) collective-permute-start(f32[48,512]{1,0:T(8,128)} %get-tuple-element.84), channel_id=1, source_target_pairs={{0,1},{2,3},{4,5},{6,7},{8,9},{10,11},{12,13},{14,15},{16,17},{18,... | collective-permute-start | bytes 294920 | tf_op jit(solution)/shard_map/ppermute | solution.py:564
  18.4 7.2 %copy-start.2 = (f32[16,8,8,128]{3,2,1,0:T(8,128)S(1)}, f32[16,8,8,128]{3,2,1,0:T(8,128)}, u32[]{:S(2)}) copy-start(f32[16,8,8,128]{3,2,1,0:T(8,128)} %copy-done.1) | copy-start | bytes 1572868
  22.1 8.3 %collective-permute-start.3 = (f32[48,512]{1,0:T(8,128)S(1)}, f32[48,512]{1,0:T(8,128)S(1)}, u32[]{:S(2)}, u32[]{:S(2)}) collective-permute-start(f32[48,512]{1,0:T(8,128)S(1)} %get-tuple-element.79), channel_id=1, source_target_pairs={{0,8},{1,9},{2,10},{3,11},{4,12},{5,13},{6,14},{7,15},{16,24},{17,... | collective-permute-start | bytes 294920 | tf_op jit(solution)/shard_map/ppermute | solution.py:564
  22.2 8.2 %collective-permute-start.2 = (f32[48,512]{1,0:T(8,128)S(1)}, f32[48,512]{1,0:T(8,128)S(1)}, u32[]{:S(2)}, u32[]{:S(2)}) collective-permute-start(f32[48,512]{1,0:T(8,128)S(1)} %get-tuple-element.80), channel_id=1, source_target_pairs={{8,16},{9,17},{10,18},{11,19},{12,20},{13,21},{14,22},{15,23},{24,... | collective-permute-start | bytes 294920 | tf_op jit(solution)/shard_map/ppermute | solution.py:565
  25.5 1.0 %copy-start.3 = (f32[16,8,8,128]{3,2,1,0:T(8,128)S(1)}, f32[16,8,8,128]{3,2,1,0:T(8,128)}, u32[]{:S(2)}) copy-start(f32[16,8,8,128]{3,2,1,0:T(8,128)} %get-tuple-element.46.j_ref) | copy-start | bytes 1572868
  26.6 1.3 %copy-start.5 = (f32[27,3,8,512]{3,2,1,0:T(8,128)S(1)}, f32[27,3,8,512]{3,2,1,0:T(8,128)}, u32[]{:S(2)}) copy-start(f32[27,3,8,512]{3,2,1,0:T(8,128)} %get-tuple-element.36.sums) | copy-start | bytes 3981316
  27.9 3.3 %copy-start.4 = (f32[16,8,8,128]{3,2,1,0:T(8,128)S(1)}, f32[16,8,8,128]{3,2,1,0:T(8,128)}, u32[]{:S(2)}) copy-start(f32[16,8,8,128]{3,2,1,0:T(8,128)} %get-tuple-element.46.j_ref) | copy-start | bytes 1572868
  27.9 3.3 %copy-start.6 = (f32[27,3,8,512]{3,2,1,0:T(8,128)S(1)}, f32[27,3,8,512]{3,2,1,0:T(8,128)}, u32[]{:S(2)}) copy-start(f32[27,3,8,512]{3,2,1,0:T(8,128)} %get-tuple-element.36.sums) | copy-start | bytes 3981316
  33.2 9.2 %collective-permute-start.5 = (f32[32,512]{1,0:T(8,128)S(1)}, f32[32,512]{1,0:T(8,128)S(1)}, u32[]{:S(2)}, u32[]{:S(2)}) collective-permute-start(f32[32,512]{1,0:T(8,128)S(1)} %get-tuple-element.91), channel_id=1, source_target_pairs={{1,2},{3,4},{5,6},{7,8},{9,10},{11,12},{13,14},{15,16},{17,18},{19... | collective-permute-start | bytes 196616 | tf_op jit(solution)/shard_map/ppermute | solution.py:565
  39.1 3.3 %collective-permute-start.4 = (f32[32,512]{1,0:T(8,128)S(1)}, f32[32,512]{1,0:T(8,128)S(1)}, u32[]{:S(2)}, u32[]{:S(2)}) collective-permute-start(f32[32,512]{1,0:T(8,128)S(1)} %get-tuple-element.92), channel_id=1, source_target_pairs={{0,1},{2,3},{4,5},{6,7},{8,9},{10,11},{12,13},{14,15},{16,17},{18,... | collective-permute-start | bytes 196616 | tf_op jit(solution)/shard_map/ppermute | solution.py:564
  42.5 4.3 %collective-permute-start.7 = (f32[32,512]{1,0:T(8,128)S(1)}, f32[32,512]{1,0:T(8,128)S(1)}, u32[]{:S(2)}, u32[]{:S(2)}) collective-permute-start(f32[32,512]{1,0:T(8,128)S(1)} %get-tuple-element.85), channel_id=1, source_target_pairs={{0,8},{1,9},{2,10},{3,11},{4,12},{5,13},{6,14},{7,15},{16,24},{17,... | collective-permute-start | bytes 196616 | tf_op jit(solution)/shard_map/ppermute | solution.py:564
  42.6 7.7 %collective-permute-start.6 = (f32[32,512]{1,0:T(8,128)S(1)}, f32[32,512]{1,0:T(8,128)S(1)}, u32[]{:S(2)}, u32[]{:S(2)}) collective-permute-start(f32[32,512]{1,0:T(8,128)S(1)} %get-tuple-element.86), channel_id=1, source_target_pairs={{8,16},{9,17},{10,18},{11,19},{12,20},{13,21},{14,22},{15,23},{24,... | collective-permute-start | bytes 196616 | tf_op jit(solution)/shard_map/ppermute | solution.py:565
  53.2 14.1 %collective-permute-start.9 = (f32[25,8,512]{2,1,0:T(8,128)S(1)}, f32[25,8,512]{2,1,0:T(8,128)S(1)}, u32[]{:S(2)}, u32[]{:S(2)}) collective-permute-start(f32[25,8,512]{2,1,0:T(8,128)S(1)} %get-tuple-element.73), channel_id=1, source_target_pairs={{1,2},{3,4},{5,6},{7,8},{9,10},{11,12},{13,14},{15,16},{17,18},{19... | collective-permute-start | bytes 1228808 | tf_op jit(solution)/shard_map/ppermute | solution.py:565
  57.9 9.3 %collective-permute-start.8 = (f32[25,8,512]{2,1,0:T(8,128)S(1)}, f32[25,8,512]{2,1,0:T(8,128)S(1)}, u32[]{:S(2)}, u32[]{:S(2)}) collective-permute-start(f32[25,8,512]{2,1,0:T(8,128)S(1)} %get-tuple-element.74), channel_id=1, source_target_pairs={{0,1},{2,3},{4,5},{6,7},{8,9},{10,11},{12,13},{14,15},{16,17},{18,... | collective-permute-start | bytes 1228808 | tf_op jit(solution)/shard_map/ppermute | solution.py:564
  68.1 9.8 %collective-permute-start.11 = (f32[7,40,512]{2,1,0:T(8,128)S(1)}, f32[7,40,512]{2,1,0:T(8,128)S(1)}, u32[]{:S(2)}, u32[]{:S(2)}) collective-permute-start(f32[7,40,512]{2,1,0:T(8,128)S(1)} %get-tuple-element.69), channel_id=1, source_target_pairs={{0,8},{1,9},{2,10},{3,11},{4,12},{5,13},{6,14},{7,15},{16,24},{17,... | collective-permute-start | bytes 1720328 | tf_op jit(solution)/shard_map/ppermute | solution.py:564
  68.2 13.1 %collective-permute-start.10 = (f32[7,40,512]{2,1,0:T(8,128)S(1)}, f32[7,40,512]{2,1,0:T(8,128)S(1)}, u32[]{:S(2)}, u32[]{:S(2)}) collective-permute-start(f32[7,40,512]{2,1,0:T(8,128)S(1)} %get-tuple-element.70), channel_id=1, source_target_pairs={{8,16},{9,17},{10,18},{11,19},{12,20},{13,21},{14,22},{15,23},{24,... | collective-permute-start | bytes 1720328 | tf_op jit(solution)/shard_map/ppermute | solution.py:565
  75.8 5.6 %copy-start.8 = (s32[64,16]{0,1:T(8,128)S(1)}, s32[64,16]{0,1:T(8,128)}, u32[]{:S(2)}) copy-start(s32[64,16]{0,1:T(8,128)} %param.7) | copy-start | bytes 12292

commit v7 on v6

--- a/solution.py
+++ b/solution.py
@@ -140,7 +140,7 @@
 
 
 def first_kernel(
-    corners, node_rows, x, vel, j_rows, sums, west, east, north, south, t0, u_ref, v_ref, rj_ref, j_ref, rd_ref,
+    corners, node_rows, x, vel, j_rows, sums, west, east, north, south, t0, send_one, send_two, u_ref, v_ref, rj_ref, j_ref, rd_ref,
     gathered, winds, jc, spots,
 ):
     step = pl.program_id(0)
@@ -208,6 +208,9 @@
             out[32 + 8 * half : 40 + 8 * half, :] = jc[
                 pl.ds(pl.multiple_of(8 * (4 * half + step), 8), 8), :
             ]
+    even = lax.axis_index("sfc") % 2 == 0
+    send_one[...] = jnp.where(even, east[...], west[...])
+    send_two[...] = jnp.where(even, west[...], east[...])
 
 
 def own_geometry_kernel(own, from_e, from_w, inv):
@@ -556,13 +559,15 @@
 SMEM = pl.BlockSpec(memory_space=pltpu.SMEM)
 
 
-def swapped(before, after, distance):
+def swapped(before, after, distance, sends=None):
     size = lax.axis_size("sfc")
     even = (lax.axis_index("sfc") // distance) % 2 == 0
     up = [(i, (i + distance) % size) for i in range(size) if (i // distance) % 2 == 0]
     over = [(i, (i + distance) % size) for i in range(size) if (i // distance) % 2 == 1]
-    one = lax.ppermute(jnp.where(even, after, before), "sfc", up + [(j, i) for i, j in up])
-    two = lax.ppermute(jnp.where(even, before, after), "sfc", over + [(j, i) for i, j in over])
+    if sends is None:
+        sends = (jnp.where(even, after, before), jnp.where(even, before, after))
+    one = lax.ppermute(sends[0], "sfc", up + [(j, i) for i, j in up])
+    two = lax.ppermute(sends[1], "sfc", over + [(j, i) for i, j in over])
     return jnp.where(even, two, one), jnp.where(even, one, two)
 
 
@@ -575,9 +580,9 @@
         first_kernel,
         grid=(4,),
         in_specs=[SMEM, fixed(16, 64), tiled(64, 16, 128), fixed(64, 16, 128), fixed(16, 64)],
-        out_specs=[sums_spec, tiled(48, 128), tiled(48, 128), tiled(32, 128), tiled(32, 128), tiled(16, 8, 8, 128)]
+        out_specs=[sums_spec, tiled(48, 128), tiled(48, 128), tiled(32, 128), tiled(32, 128), tiled(16, 8, 8, 128), tiled(48, 128), tiled(48, 128)]
         + coef_specs,
-        out_shape=[sds(27, 3, 8, 512), sds(48, 512), sds(48, 512), sds(32, 512), sds(32, 512), sds(16, 8, 8, 512)]
+        out_shape=[sds(27, 3, 8, 512), sds(48, 512), sds(48, 512), sds(32, 512), sds(32, 512), sds(16, 8, 8, 512), sds(48, 512), sds(48, 512)]
         + coef,
         scratch_shapes=[
             pltpu.VMEM((64, 16, 128), F32),
@@ -588,14 +593,14 @@
         compiler_params=pltpu.CompilerParams(vmem_limit_bytes=FIRST_LIMIT, dimension_semantics=("arbitrary",)),
         name="section_one_sums",
     )
-    sums, west, east, north, south, t0, *coefs = first(nodes, nodes, tracers, velocity, jacobian.T)
+    sums, west, east, north, south, t0, send_one, send_two, *coefs = first(nodes, nodes, tracers, velocity, jacobian.T)
 
     row = lax.broadcasted_iota(jnp.int32, (32, 1), 0)
 
     def corrected(own, from_w, from_e, y):
         return own + jnp.where(row == 0, from_w[y : y + 1], 0.0) + jnp.where(row >= 24, from_e[y : y + 1], 0.0)
 
-    from_w, from_e = swapped(west, east, 1)
+    from_w, from_e = swapped(west, east, 1, (send_one, send_two))
     low = lax.broadcasted_iota(jnp.int32, (8, 1), 0) < 4
     beside = [jnp.where(low, from_e[k : k + 8], from_w[k : k + 8]) for k in (32, 40)]
     msg_n = jnp.concatenate([corrected(north, from_w, from_e, 0), west[32:40], beside[0]])

time: 88.8 us -> 88.1 us (level)
  no operation moved by 1% of the time
where the time goes in v7:
time: 88.1 us; the launch traced here: 87.7 us
  Pallas kernels  33.5 us (38%)
  waiting for transfers between devices  24.8 us (28%)
  starting transfers between devices  22.6 us (26%)
  local copies, waits for them, and re-layouts  4.83 us (5%)
  other arithmetic  1.64 us (2%)
    ppermute x6, starting transfers between devices, swapped(): two = lax.ppermute(sends[1], 'sfc', over + [(j, i) for i, j in over])  22.3 us
    ppermute x6, waiting for transfers between devices, swapped(): two = lax.ppermute(sends[1], 'sfc', over + [(j, i) for i, j in over])  22.2 us
    pallas_call x1, Pallas kernels, per_device(): pl.pallas_call(inner_kernel, grid=(4,), in_specs=[sums_spec, tiled(32, 12...  7.53 us
    pallas_call x1, Pallas kernels, per_device(): first(nodes, nodes, tracers, velocity, jacobian.T)  7.49 us
    pallas_call x1, Pallas kernels, per_device(): pl.pallas_call(last_kernel, grid=(4,), in_specs=[SMEM, band, band, jac_sp...  6.95 us
    pallas_call x2, Pallas kernels, inner_stage(): pl.pallas_call(functools.partial(stage_inner_kernel, keep, take), grid=(4...  4.96 us
    unnamed x20, local copies, waits for them, and re-layouts  4.81 us
    pallas_call x2, Pallas kernels, stage(): pl.pallas_call(functools.partial(stage_kernel, keep, take, wide), grid=(4...  4.71 us
  transfers between devices with their start and end apart: 12, of which 7 were waited for; matrix products, arithmetic and copies ran while one was open for 0% of the time, Pallas kernels for 15%

profile of v7, /device:TPU:0, one launch (start us, length us, event | category | flops | bytes accessed | tf_op | source)
XLA Modules:
  0.0 87.7 jit_solution(14054533729437813991)
XLA Ops:
  0.0 0.7 copy-done.7
  1.4 7.5 %section_one_sums.1 = (f32[27,3,8,512]{3,2,1,0:T(8,128)}, f32[48,512]{1,0:T(8,128)S(1)}, f32[48,512]{1,0:T(8,128)S(1)}, f32[32,512]{1,0:T(8,128)S(1)}, f32[32,51...) custom-call(s32[16,64]{1,0:T(8,128)S(1)} %bitcast.10, ...), custom_call_target="tpu_custom_call" | custom-call | tf_op jit(solution)/shard_map/section_one_sums/pallas_call | solution.py:596
  9.0 8.9 %collective-permute-start.1 = (f32[48,512]{1,0:T(8,128)}, f32[48,512]{1,0:T(8,128)}, u32[]{:S(2)}, u32[]{:S(2)}) collective-permute-start(f32[48,512]{1,0:T(8,128)} %get-tuple-element.41), channel_id=1, source_target_pairs={{1,2},{3,4},{5,6},{7,8},{9,10},{11,12},{13,14},{15,16},{17,18},{19... | collective-permute-start | bytes 294920 | tf_op jit(solution)/shard_map/ppermute | solution.py:570
  17.9 2.6 %collective-permute-done.1 = f32[48,512]{1,0:T(8,128)} collective-permute-done((f32[48,512]{1,0:T(8,128)}, f32[48,512]{1,0:T(8,128)}, u32[]{:S(2)}, u32[]{:S(2)}) %collective-permute-start.1) | collective-permute-done | bytes 98336 | tf_op jit(solution)/shard_map/ppermute | solution.py:570
  20.5 1.0 %broadcast_select_fusion.10 = (f32[48,512]{1,0:T(8,128)S(1)}, f32[48,512]{1,0:T(8,128)S(1)}) fusion(f32[48,512]{1,0:T(8,128)} %collective-permute-done.1, f32[48,512]{1,0:T(8,128)} %collective-permute-done, pred[]{:T(512)S(6)} %eq.35), kind=kLoop, calls=%fused_computation.20 | loop fusion | flops 49152 | bytes 393217 | tf_op jit(solution)/shard_map/jit(_where)/select_n | solution.py:571
  21.7 2.2 %collective-permute-start.2 = (f32[48,512]{1,0:T(8,128)S(1)}, f32[48,512]{1,0:T(8,128)S(1)}, u32[]{:S(2)}, u32[]{:S(2)}) collective-permute-start(f32[48,512]{1,0:T(8,128)S(1)} %get-tuple-element.84), channel_id=1, source_target_pairs={{8,16},{9,17},{10,18},{11,19},{12,20},{13,21},{14,22},{15,23},{24,... | collective-permute-start | bytes 294920 | tf_op jit(solution)/shard_map/ppermute | solution.py:570
  24.5 1.0 %copy-done.1 = f32[16,8,8,128]{3,2,1,0:T(8,128)S(1)} copy-done((f32[16,8,8,128]{3,2,1,0:T(8,128)S(1)}, f32[16,8,8,128]{3,2,1,0:T(8,128)}, u32[]{:S(2)}) %copy-start.1) | copy-done | bytes 524312
  25.5 1.0 %copy-done.3 = f32[16,8,8,128]{3,2,1,0:T(8,128)S(1)} copy-done((f32[16,8,8,128]{3,2,1,0:T(8,128)S(1)}, f32[16,8,8,128]{3,2,1,0:T(8,128)}, u32[]{:S(2)}) %copy-start.3) | copy-done | bytes 524312
  26.5 1.3 %copy-done.5 = f32[27,3,8,512]{3,2,1,0:T(8,128)S(1)} copy-done((f32[27,3,8,512]{3,2,1,0:T(8,128)S(1)}, f32[27,3,8,512]{3,2,1,0:T(8,128)}, u32[]{:S(2)}) %copy-start.5) | copy-done | bytes 1327128
  27.9 2.5 %inner_rows.2 = (f32[27,3,8,512]{3,2,1,0:T(8,128)S(1)}, f32[32,512]{1,0:T(8,128)S(1)}) custom-call(f32[27,3,8,512]{3,2,1,0:T(8,128)S(1)} %copy-done.5, f32[48,512]{1,0:T(8,128)S(1)} %get-tuple-element.39.edge, f32[48,512]{1,0:T(8,128)S(1)} %get-tuple-element.86.from_e, f32[48,512]{1,0:T(8,128)S(1)} %get-tuple-element.85.from_w, ...), custom_call_target="tpu_custom_call" | custom-call | flops 31457280 | bytes 8388608 | tf_op jit(solution)/shard_map/inner_rows/pallas_call | solution.py:630
  30.4 0.8 geometry.1
  31.2 1.9 %section_two_sums.1 = (f32[27,3,8,512]{3,2,1,0:T(8,128)S(1)}, f32[32,512]{1,0:T(8,128)S(1)}, f32[32,512]{1,0:T(8,128)S(1)}, f32[32,512]{1,0:T(8,128)S(1)}, f32[32,512]{1,0:T(8,128)S(1)}) custom-call(f32[27,3,8,512]{3,2,1,0:T(8,128)S(1)} %copy-done.6, f32[48,512]{1,0:T(8,128)S(1)} %get-tuple-element.39.edge, f32[48,512]{1,0:T(8,128)S(1)} %get-tuple-element.86.from_e, ...), custom_call_target="tpu_custom_call" | custom-call | tf_op jit(solution)/shard_map/section_two_sums/pallas_call | solution.py:651
  33.2 5.5 %collective-permute-start.5 = (f32[32,512]{1,0:T(8,128)S(1)}, f32[32,512]{1,0:T(8,128)S(1)}, u32[]{:S(2)}, u32[]{:S(2)}) collective-permute-start(f32[32,512]{1,0:T(8,128)S(1)} %get-tuple-element.93), channel_id=1, source_target_pairs={{1,2},{3,4},{5,6},{7,8},{9,10},{11,12},{13,14},{15,16},{17,18},{19... | collective-permute-start | bytes 196616 | tf_op jit(solution)/shard_map/ppermute | solution.py:570
  38.7 3.7 %collective-permute-done.5 = f32[32,512]{1,0:T(8,128)S(1)} collective-permute-done((f32[32,512]{1,0:T(8,128)S(1)}, f32[32,512]{1,0:T(8,128)S(1)}, u32[]{:S(2)}, u32[]{:S(2)}) %collective-permute-start.5) | collective-permute-done | bytes 65568 | tf_op jit(solution)/shard_map/ppermute | solution.py:570
  42.6 1.3 %collective-permute-start.6 = (f32[32,512]{1,0:T(8,128)S(1)}, f32[32,512]{1,0:T(8,128)S(1)}, u32[]{:S(2)}, u32[]{:S(2)}) collective-permute-start(f32[32,512]{1,0:T(8,128)S(1)} %get-tuple-element.88), channel_id=1, source_target_pairs={{8,16},{9,17},{10,18},{11,19},{12,20},{13,21},{14,22},{15,23},{24,... | collective-permute-start | bytes 196616 | tf_op jit(solution)/shard_map/ppermute | solution.py:570
  43.9 2.5 %inner_rows.3 = (f32[27,3,8,512]{3,2,1,0:T(8,128)S(1)}, f32[32,512]{1,0:T(8,128)S(1)}) custom-call(f32[27,3,8,512]{3,2,1,0:T(8,128)S(1)} %get-tuple-element.54.sums, f32[32,512]{1,0:T(8,128)S(1)} %get-tuple-element.55.edge, f32[32,512]{1,0:T(8,128)S(1)} %get-tuple-element.92.from_e, f32[32,512]{1,0:T(8,128)S(1)} %get-tuple-element.91.from_w, ...), custom_call_target="tpu_custom_call" | custom-call | flops 31457280 | bytes 8388608 | tf_op jit(solution)/shard_map/inner_rows/pallas_call | solution.py:630
  46.8 3.4 %collective-permute-done.6 = f32[32,512]{1,0:T(8,128)S(1)} collective-permute-done((f32[32,512]{1,0:T(8,128)S(1)}, f32[32,512]{1,0:T(8,128)S(1)}, u32[]{:S(2)}, u32[]{:S(2)}) %collective-permute-start.6) | collective-permute-done | bytes 65568 | tf_op jit(solution)/shard_map/ppermute | solution.py:570
  50.3 2.8 %section_three_sums.1 = (f32[27,3,8,512]{3,2,1,0:T(8,128)S(1)}, f32[25,8,512]{2,1,0:T(8,128)S(1)}, f32[25,8,512]{2,1,0:T(8,128)S(1)}, f32[8,512]{1,0:T(8,128)}, f32[32,512]{1,0:T(8,128)S(1)}) custom-call(f32[27,3,8,512]{3,2,1,0:T(8,128)S(1)} %get-tuple-element.54.sums, f32[32,512]{1,0:T(8,128)S(1)} %get-tuple-element.55.edge, ...), custom_call_target="tpu_custom_call" | custom-call | tf_op jit(solution)/shard_map/section_three_sums/pallas_call | solution.py:651
  53.1 4.3 %collective-permute-start.9 = (f32[25,8,512]{2,1,0:T(8,128)S(1)}, f32[25,8,512]{2,1,0:T(8,128)S(1)}, u32[]{:S(2)}, u32[]{:S(2)}) collective-permute-start(f32[25,8,512]{2,1,0:T(8,128)S(1)} %get-tuple-element.77), channel_id=1, source_target_pairs={{1,2},{3,4},{5,6},{7,8},{9,10},{11,12},{13,14},{15,16},{17,18},{19... | collective-permute-start | bytes 1228808 | tf_op jit(solution)/shard_map/ppermute | solution.py:570
  57.5 9.1 %collective-permute-done.9 = f32[25,8,512]{2,1,0:T(8,128)S(1)} collective-permute-done((f32[25,8,512]{2,1,0:T(8,128)S(1)}, f32[25,8,512]{2,1,0:T(8,128)S(1)}, u32[]{:S(2)}, u32[]{:S(2)}) %collective-permute-start.9) | collective-permute-done | bytes 409632 | tf_op jit(solution)/shard_map/ppermute | solution.py:570
  67.6 7.5 %biharmonic_inner_rows.1 = (f32[25,3,16,512]{3,2,1,0:T(8,128)S(1)}, f32[2,3,16,512]{3,2,1,0:T(8,128)S(1)}, f32[25,3,16,512]{3,2,1,0:T(8,128)S(1)}) custom-call(f32[27,3,8,512]{3,2,1,0:T(8,128)S(1)} %get-tuple-element.61.sums, f32[32,512]{1,0:T(8,128)S(1)} %get-tuple-element.62.edge, f32[25,8,512]{2,1,0:T(8,128)S(1)} %get-tuple-element.76.from_e, ...), custom_call_target="tpu_custom_call" | custom-call | flops 31457280 | bytes 16777216 | tf_op jit(solution)/shard_map/biharmonic_inner_rows/pallas_call | solution.py:694
  75.1 2.1 %collective-permute-done.11 = f32[7,40,512]{2,1,0:T(8,128)S(1)} collective-permute-done((f32[7,40,512]{2,1,0:T(8,128)S(1)}, f32[7,40,512]{2,1,0:T(8,128)S(1)}, u32[]{:S(2)}, u32[]{:S(2)}) %collective-permute-start.11) | collective-permute-done | bytes 573472 | tf_op jit(solution)/shard_map/ppermute | solution.py:569
  77.2 3.4 %collective-permute-done.10 = f32[7,40,512]{2,1,0:T(8,128)S(1)} collective-permute-done((f32[7,40,512]{2,1,0:T(8,128)S(1)}, f32[7,40,512]{2,1,0:T(8,128)S(1)}, u32[]{:S(2)}, u32[]{:S(2)}) %collective-permute-start.10) | collective-permute-done | bytes 573472 | tf_op jit(solution)/shard_map/ppermute | solution.py:570
  80.7 7.0 %biharmonic_outer_rows.1 = f32[64,16,512]{2,1,0:T(8,128)} custom-call(s32[16,64]{1,0:T(8,128)S(1)} %bitcast.12, f32[7,40,512]{2,1,0:T(8,128)S(1)} %get-tuple-element.72.from_n, f32[7,40,512]{2,1,0:T(8,128)S(1)} %get-tuple-element.71.from_s, f32[16,12,16,128]{3,2,1,0:T(8,128)S(1)} %get-tuple-element.67.j_ref, f32[37,3,16,128]{3,2,1,0:T(8,128)S(1)} %get-tuple-element.45.inv, ...), custom_call_target="tpu_custom_call" | custom-call | tf_op jit(solution)/shard_map/biharmonic_outer_rows/pallas_call | solution.py:705
  (49 shorter events, 3.5 us)
Async XLA Ops:
  0.0 0.7 copy-start.7
  0.7 0.7 copy-start.9
  8.9 15.6 %copy-start = (f32[16,8,8,512]{3,2,1,0:T(8,128)S(1)}, f32[16,8,8,512]{3,2,1,0:T(8,128)}, u32[]{:S(2)}) copy-start(f32[16,8,8,512]{3,2,1,0:T(8,128)} %get-tuple-element.46.t0) | copy-start | bytes 6291460
  8.9 9.0 %collective-permute-start = (f32[48,512]{1,0:T(8,128)}, f32[48,512]{1,0:T(8,128)}, u32[]{:S(2)}, u32[]{:S(2)}) collective-permute-start(f32[48,512]{1,0:T(8,128)} %get-tuple-element.40), channel_id=1, source_target_pairs={{0,1},{2,3},{4,5},{6,7},{8,9},{10,11},{12,13},{14,15},{16,17},{18,... | collective-permute-start | bytes 294920 | tf_op jit(solution)/shard_map/ppermute | solution.py:569
  9.0 11.5 %collective-permute-start.1 = (f32[48,512]{1,0:T(8,128)}, f32[48,512]{1,0:T(8,128)}, u32[]{:S(2)}, u32[]{:S(2)}) collective-permute-start(f32[48,512]{1,0:T(8,128)} %get-tuple-element.41), channel_id=1, source_target_pairs={{1,2},{3,4},{5,6},{7,8},{9,10},{11,12},{13,14},{15,16},{17,18},{19... | collective-permute-start | bytes 294920 | tf_op jit(solution)/shard_map/ppermute | solution.py:570
  21.6 8.7 %collective-permute-start.3 = (f32[48,512]{1,0:T(8,128)S(1)}, f32[48,512]{1,0:T(8,128)S(1)}, u32[]{:S(2)}, u32[]{:S(2)}) collective-permute-start(f32[48,512]{1,0:T(8,128)S(1)} %get-tuple-element.83), channel_id=1, source_target_pairs={{0,8},{1,9},{2,10},{3,11},{4,12},{5,13},{6,14},{7,15},{16,24},{17,... | collective-permute-start | bytes 294920 | tf_op jit(solution)/shard_map/ppermute | solution.py:569
  21.7 8.6 %collective-permute-start.2 = (f32[48,512]{1,0:T(8,128)S(1)}, f32[48,512]{1,0:T(8,128)S(1)}, u32[]{:S(2)}, u32[]{:S(2)}) collective-permute-start(f32[48,512]{1,0:T(8,128)S(1)} %get-tuple-element.84), channel_id=1, source_target_pairs={{8,16},{9,17},{10,18},{11,19},{12,20},{13,21},{14,22},{15,23},{24,... | collective-permute-start | bytes 294920 | tf_op jit(solution)/shard_map/ppermute | solution.py:570
  24.4 1.0 %copy-start.1 = (f32[16,8,8,128]{3,2,1,0:T(8,128)S(1)}, f32[16,8,8,128]{3,2,1,0:T(8,128)}, u32[]{:S(2)}) copy-start(f32[16,8,8,128]{3,2,1,0:T(8,128)} %get-tuple-element.49.rj_ref) | copy-start | bytes 1572868
  25.5 1.0 %copy-start.3 = (f32[16,8,8,128]{3,2,1,0:T(8,128)S(1)}, f32[16,8,8,128]{3,2,1,0:T(8,128)}, u32[]{:S(2)}) copy-start(f32[16,8,8,128]{3,2,1,0:T(8,128)} %get-tuple-element.50.j_ref) | copy-start | bytes 1572868
  26.5 1.3 %copy-start.5 = (f32[27,3,8,512]{3,2,1,0:T(8,128)S(1)}, f32[27,3,8,512]{3,2,1,0:T(8,128)}, u32[]{:S(2)}) copy-start(f32[27,3,8,512]{3,2,1,0:T(8,128)} %get-tuple-element.38.sums) | copy-start | bytes 3981316
  27.9 3.3 %copy-start.2 = (f32[16,8,8,128]{3,2,1,0:T(8,128)S(1)}, f32[16,8,8,128]{3,2,1,0:T(8,128)}, u32[]{:S(2)}) copy-start(f32[16,8,8,128]{3,2,1,0:T(8,128)} %get-tuple-element.49.rj_ref) | copy-start | bytes 1572868
  27.9 3.3 %copy-start.6 = (f32[27,3,8,512]{3,2,1,0:T(8,128)S(1)}, f32[27,3,8,512]{3,2,1,0:T(8,128)}, u32[]{:S(2)}) copy-start(f32[27,3,8,512]{3,2,1,0:T(8,128)} %get-tuple-element.38.sums) | copy-start | bytes 3981316
  31.2 12.7 %copy-start.4 = (f32[16,8,8,128]{3,2,1,0:T(8,128)S(1)}, f32[16,8,8,128]{3,2,1,0:T(8,128)}, u32[]{:S(2)}) copy-start(f32[16,8,8,128]{3,2,1,0:T(8,128)} %get-tuple-element.50.j_ref) | copy-start | bytes 1572868
  33.2 9.2 %collective-permute-start.5 = (f32[32,512]{1,0:T(8,128)S(1)}, f32[32,512]{1,0:T(8,128)S(1)}, u32[]{:S(2)}, u32[]{:S(2)}) collective-permute-start(f32[32,512]{1,0:T(8,128)S(1)} %get-tuple-element.93), channel_id=1, source_target_pairs={{1,2},{3,4},{5,6},{7,8},{9,10},{11,12},{13,14},{15,16},{17,18},{19... | collective-permute-start | bytes 196616 | tf_op jit(solution)/shard_map/ppermute | solution.py:570
  38.6 3.7 %collective-permute-start.4 = (f32[32,512]{1,0:T(8,128)S(1)}, f32[32,512]{1,0:T(8,128)S(1)}, u32[]{:S(2)}, u32[]{:S(2)}) collective-permute-start(f32[32,512]{1,0:T(8,128)S(1)} %get-tuple-element.94), channel_id=1, source_target_pairs={{0,1},{2,3},{4,5},{6,7},{8,9},{10,11},{12,13},{14,15},{16,17},{18,... | collective-permute-start | bytes 196616 | tf_op jit(solution)/shard_map/ppermute | solution.py:569
  42.5 4.3 %collective-permute-start.7 = (f32[32,512]{1,0:T(8,128)S(1)}, f32[32,512]{1,0:T(8,128)S(1)}, u32[]{:S(2)}, u32[]{:S(2)}) collective-permute-start(f32[32,512]{1,0:T(8,128)S(1)} %get-tuple-element.87), channel_id=1, source_target_pairs={{0,8},{1,9},{2,10},{3,11},{4,12},{5,13},{6,14},{7,15},{16,24},{17,... | collective-permute-start | bytes 196616 | tf_op jit(solution)/shard_map/ppermute | solution.py:569
  42.6 7.7 %collective-permute-start.6 = (f32[32,512]{1,0:T(8,128)S(1)}, f32[32,512]{1,0:T(8,128)S(1)}, u32[]{:S(2)}, u32[]{:S(2)}) collective-permute-start(f32[32,512]{1,0:T(8,128)S(1)} %get-tuple-element.88), channel_id=1, source_target_pairs={{8,16},{9,17},{10,18},{11,19},{12,20},{13,21},{14,22},{15,23},{24,... | collective-permute-start | bytes 196616 | tf_op jit(solution)/shard_map/ppermute | solution.py:570
  53.1 13.4 %collective-permute-start.9 = (f32[25,8,512]{2,1,0:T(8,128)S(1)}, f32[25,8,512]{2,1,0:T(8,128)S(1)}, u32[]{:S(2)}, u32[]{:S(2)}) collective-permute-start(f32[25,8,512]{2,1,0:T(8,128)S(1)} %get-tuple-element.77), channel_id=1, source_target_pairs={{1,2},{3,4},{5,6},{7,8},{9,10},{11,12},{13,14},{15,16},{17,18},{19... | collective-permute-start | bytes 1228808 | tf_op jit(solution)/shard_map/ppermute | solution.py:570
  57.5 9.1 %collective-permute-start.8 = (f32[25,8,512]{2,1,0:T(8,128)S(1)}, f32[25,8,512]{2,1,0:T(8,128)S(1)}, u32[]{:S(2)}, u32[]{:S(2)}) collective-permute-start(f32[25,8,512]{2,1,0:T(8,128)S(1)} %get-tuple-element.78), channel_id=1, source_target_pairs={{0,1},{2,3},{4,5},{6,7},{8,9},{10,11},{12,13},{14,15},{16,17},{18,... | collective-permute-start | bytes 1228808 | tf_op jit(solution)/shard_map/ppermute | solution.py:569
  67.4 9.8 %collective-permute-start.11 = (f32[7,40,512]{2,1,0:T(8,128)S(1)}, f32[7,40,512]{2,1,0:T(8,128)S(1)}, u32[]{:S(2)}, u32[]{:S(2)}) collective-permute-start(f32[7,40,512]{2,1,0:T(8,128)S(1)} %get-tuple-element.73), channel_id=1, source_target_pairs={{0,8},{1,9},{2,10},{3,11},{4,12},{5,13},{6,14},{7,15},{16,24},{17,... | collective-permute-start | bytes 1720328 | tf_op jit(solution)/shard_map/ppermute | solution.py:569
  67.5 13.1 %collective-permute-start.10 = (f32[7,40,512]{2,1,0:T(8,128)S(1)}, f32[7,40,512]{2,1,0:T(8,128)S(1)}, u32[]{:S(2)}, u32[]{:S(2)}) collective-permute-start(f32[7,40,512]{2,1,0:T(8,128)S(1)} %get-tuple-element.74), channel_id=1, source_target_pairs={{8,16},{9,17},{10,18},{11,19},{12,20},{13,21},{14,22},{15,23},{24,... | collective-permute-start | bytes 1720328 | tf_op jit(solution)/shard_map/ppermute | solution.py:570
  75.1 5.6 %copy-start.8 = (s32[64,16]{0,1:T(8,128)S(1)}, s32[64,16]{0,1:T(8,128)}, u32[]{:S(2)}) copy-start(s32[64,16]{0,1:T(8,128)} %param.7) | copy-start | bytes 12292

commit v8 on v7

--- a/solution.py
+++ b/solution.py
@@ -180,13 +180,13 @@
             rd_ref[ey] = 1.0 / weighted(js)
             return 0
 
-        lax.fori_loop(0, 8, coef, 0)
+        lax.fori_loop(0, 8, coef, 0, unroll=4)
 
     def gather(e, _):
         gathered[spots[e]] = x[e]
         return 0
 
-    lax.fori_loop(0, 64, gather, 0, unroll=8)
+    lax.fori_loop(0, 64, gather, 0, unroll=16)
     flat = gathered.reshape(1024, 128)
     clear_first(sums, east)
 
@@ -532,13 +532,13 @@
                 flat[pl.ds(ey * 128 + 4 * j + i, 8, stride=16), :] = vals[i]
         return 0
 
-    lax.fori_loop(0, 8, finish, 0)
+    lax.fori_loop(0, 8, finish, 0, unroll=8)
 
     def scatter(e, _):
         out[e] = spread[spots[e]]
         return 0
 
-    lax.fori_loop(0, 64, scatter, 0, unroll=8)
+    lax.fori_loop(0, 64, scatter, 0, unroll=16)
 
 
 def sds(*shape):

time: 88.1 us -> 87.3 us (level)
  no operation moved by 1% of the time
where the time goes in v8:
time: 87.3 us; the launch traced here: 86.8 us
  Pallas kernels  32.7 us (37%)
  waiting for transfers between devices  24.7 us (28%)
  starting transfers between devices  22.6 us (26%)
  local copies, waits for them, and re-layouts  4.83 us (6%)
  other arithmetic  1.64 us (2%)
    ppermute x6, starting transfers between devices, swapped(): two = lax.ppermute(sends[1], 'sfc', over + [(j, i) for i, j in over])  22.3 us
    ppermute x6, waiting for transfers between devices, swapped(): two = lax.ppermute(sends[1], 'sfc', over + [(j, i) for i, j in over])  22.2 us
    pallas_call x1, Pallas kernels, per_device(): pl.pallas_call(inner_kernel, grid=(4,), in_specs=[sums_spec, tiled(32, 12...  7.53 us
    pallas_call x1, Pallas kernels, per_device(): first(nodes, nodes, tracers, velocity, jacobian.T)  6.98 us
    pallas_call x1, Pallas kernels, per_device(): pl.pallas_call(last_kernel, grid=(4,), in_specs=[SMEM, band, band, jac_sp...  6.64 us
    pallas_call x2, Pallas kernels, inner_stage(): pl.pallas_call(functools.partial(stage_inner_kernel, keep, take), grid=(4...  4.96 us
    unnamed x20, local copies, waits for them, and re-layouts  4.81 us
    pallas_call x2, Pallas kernels, stage(): pl.pallas_call(functools.partial(stage_kernel, keep, take, wide), grid=(4...  4.71 us
  transfers between devices with their start and end apart: 12, of which 7 were waited for; matrix products, arithmetic and copies ran while one was open for 0% of the time, Pallas kernels for 15%

profile of v8, /device:TPU:0, one launch (start us, length us, event | category | flops | bytes accessed | tf_op | source)
XLA Modules:
  0.0 86.8 jit_solution(18262611995538875850)
XLA Ops:
  0.0 0.7 copy-done.7
  1.4 7.0 %section_one_sums.1 = (f32[27,3,8,512]{3,2,1,0:T(8,128)}, f32[48,512]{1,0:T(8,128)S(1)}, f32[48,512]{1,0:T(8,128)S(1)}, f32[32,512]{1,0:T(8,128)S(1)}, f32[32,51...) custom-call(s32[16,64]{1,0:T(8,128)S(1)} %bitcast.10, ...), custom_call_target="tpu_custom_call" | custom-call | tf_op jit(solution)/shard_map/section_one_sums/pallas_call | solution.py:596
  8.5 8.9 %collective-permute-start.1 = (f32[48,512]{1,0:T(8,128)}, f32[48,512]{1,0:T(8,128)}, u32[]{:S(2)}, u32[]{:S(2)}) collective-permute-start(f32[48,512]{1,0:T(8,128)} %get-tuple-element.41), channel_id=1, source_target_pairs={{1,2},{3,4},{5,6},{7,8},{9,10},{11,12},{13,14},{15,16},{17,18},{19... | collective-permute-start | bytes 294920 | tf_op jit(solution)/shard_map/ppermute | solution.py:570
  17.4 2.6 %collective-permute-done.1 = f32[48,512]{1,0:T(8,128)} collective-permute-done((f32[48,512]{1,0:T(8,128)}, f32[48,512]{1,0:T(8,128)}, u32[]{:S(2)}, u32[]{:S(2)}) %collective-permute-start.1) | collective-permute-done | bytes 98336 | tf_op jit(solution)/shard_map/ppermute | solution.py:570
  20.0 1.0 %broadcast_select_fusion.10 = (f32[48,512]{1,0:T(8,128)S(1)}, f32[48,512]{1,0:T(8,128)S(1)}) fusion(f32[48,512]{1,0:T(8,128)} %collective-permute-done.1, f32[48,512]{1,0:T(8,128)} %collective-permute-done, pred[]{:T(512)S(6)} %eq.35), kind=kLoop, calls=%fused_computation.20 | loop fusion | flops 49152 | bytes 393217 | tf_op jit(solution)/shard_map/jit(_where)/select_n | solution.py:571
  21.2 2.2 %collective-permute-start.2 = (f32[48,512]{1,0:T(8,128)S(1)}, f32[48,512]{1,0:T(8,128)S(1)}, u32[]{:S(2)}, u32[]{:S(2)}) collective-permute-start(f32[48,512]{1,0:T(8,128)S(1)} %get-tuple-element.84), channel_id=1, source_target_pairs={{8,16},{9,17},{10,18},{11,19},{12,20},{13,21},{14,22},{15,23},{24,... | collective-permute-start | bytes 294920 | tf_op jit(solution)/shard_map/ppermute | solution.py:570
  24.0 1.0 %copy-done.1 = f32[16,8,8,128]{3,2,1,0:T(8,128)S(1)} copy-done((f32[16,8,8,128]{3,2,1,0:T(8,128)S(1)}, f32[16,8,8,128]{3,2,1,0:T(8,128)}, u32[]{:S(2)}) %copy-start.1) | copy-done | bytes 524312
  25.0 1.0 %copy-done.3 = f32[16,8,8,128]{3,2,1,0:T(8,128)S(1)} copy-done((f32[16,8,8,128]{3,2,1,0:T(8,128)S(1)}, f32[16,8,8,128]{3,2,1,0:T(8,128)}, u32[]{:S(2)}) %copy-start.3) | copy-done | bytes 524312
  26.0 1.3 %copy-done.5 = f32[27,3,8,512]{3,2,1,0:T(8,128)S(1)} copy-done((f32[27,3,8,512]{3,2,1,0:T(8,128)S(1)}, f32[27,3,8,512]{3,2,1,0:T(8,128)}, u32[]{:S(2)}) %copy-start.5) | copy-done | bytes 1327128
  27.4 2.5 %inner_rows.2 = (f32[27,3,8,512]{3,2,1,0:T(8,128)S(1)}, f32[32,512]{1,0:T(8,128)S(1)}) custom-call(f32[27,3,8,512]{3,2,1,0:T(8,128)S(1)} %copy-done.5, f32[48,512]{1,0:T(8,128)S(1)} %get-tuple-element.39.edge, f32[48,512]{1,0:T(8,128)S(1)} %get-tuple-element.86.from_e, f32[48,512]{1,0:T(8,128)S(1)} %get-tuple-element.85.from_w, ...), custom_call_target="tpu_custom_call" | custom-call | flops 31457280 | bytes 8388608 | tf_op jit(solution)/shard_map/inner_rows/pallas_call | solution.py:630
  29.9 0.8 geometry.1
  30.7 1.9 %section_two_sums.1 = (f32[27,3,8,512]{3,2,1,0:T(8,128)S(1)}, f32[32,512]{1,0:T(8,128)S(1)}, f32[32,512]{1,0:T(8,128)S(1)}, f32[32,512]{1,0:T(8,128)S(1)}, f32[32,512]{1,0:T(8,128)S(1)}) custom-call(f32[27,3,8,512]{3,2,1,0:T(8,128)S(1)} %copy-done.6, f32[48,512]{1,0:T(8,128)S(1)} %get-tuple-element.39.edge, f32[48,512]{1,0:T(8,128)S(1)} %get-tuple-element.86.from_e, ...), custom_call_target="tpu_custom_call" | custom-call | tf_op jit(solution)/shard_map/section_two_sums/pallas_call | solution.py:651
  32.7 5.5 %collective-permute-start.5 = (f32[32,512]{1,0:T(8,128)S(1)}, f32[32,512]{1,0:T(8,128)S(1)}, u32[]{:S(2)}, u32[]{:S(2)}) collective-permute-start(f32[32,512]{1,0:T(8,128)S(1)} %get-tuple-element.93), channel_id=1, source_target_pairs={{1,2},{3,4},{5,6},{7,8},{9,10},{11,12},{13,14},{15,16},{17,18},{19... | collective-permute-start | bytes 196616 | tf_op jit(solution)/shard_map/ppermute | solution.py:570
  38.2 3.7 %collective-permute-done.5 = f32[32,512]{1,0:T(8,128)S(1)} collective-permute-done((f32[32,512]{1,0:T(8,128)S(1)}, f32[32,512]{1,0:T(8,128)S(1)}, u32[]{:S(2)}, u32[]{:S(2)}) %collective-permute-start.5) | collective-permute-done | bytes 65568 | tf_op jit(solution)/shard_map/ppermute | solution.py:570
  42.1 1.3 %collective-permute-start.6 = (f32[32,512]{1,0:T(8,128)S(1)}, f32[32,512]{1,0:T(8,128)S(1)}, u32[]{:S(2)}, u32[]{:S(2)}) collective-permute-start(f32[32,512]{1,0:T(8,128)S(1)} %get-tuple-element.88), channel_id=1, source_target_pairs={{8,16},{9,17},{10,18},{11,19},{12,20},{13,21},{14,22},{15,23},{24,... | collective-permute-start | bytes 196616 | tf_op jit(solution)/shard_map/ppermute | solution.py:570
  43.4 2.5 %inner_rows.3 = (f32[27,3,8,512]{3,2,1,0:T(8,128)S(1)}, f32[32,512]{1,0:T(8,128)S(1)}) custom-call(f32[27,3,8,512]{3,2,1,0:T(8,128)S(1)} %get-tuple-element.54.sums, f32[32,512]{1,0:T(8,128)S(1)} %get-tuple-element.55.edge, f32[32,512]{1,0:T(8,128)S(1)} %get-tuple-element.92.from_e, f32[32,512]{1,0:T(8,128)S(1)} %get-tuple-element.91.from_w, ...), custom_call_target="tpu_custom_call" | custom-call | flops 31457280 | bytes 8388608 | tf_op jit(solution)/shard_map/inner_rows/pallas_call | solution.py:630
  46.3 3.4 %collective-permute-done.6 = f32[32,512]{1,0:T(8,128)S(1)} collective-permute-done((f32[32,512]{1,0:T(8,128)S(1)}, f32[32,512]{1,0:T(8,128)S(1)}, u32[]{:S(2)}, u32[]{:S(2)}) %collective-permute-start.6) | collective-permute-done | bytes 65568 | tf_op jit(solution)/shard_map/ppermute | solution.py:570
  49.8 2.8 %section_three_sums.1 = (f32[27,3,8,512]{3,2,1,0:T(8,128)S(1)}, f32[25,8,512]{2,1,0:T(8,128)S(1)}, f32[25,8,512]{2,1,0:T(8,128)S(1)}, f32[8,512]{1,0:T(8,128)}, f32[32,512]{1,0:T(8,128)S(1)}) custom-call(f32[27,3,8,512]{3,2,1,0:T(8,128)S(1)} %get-tuple-element.54.sums, f32[32,512]{1,0:T(8,128)S(1)} %get-tuple-element.55.edge, ...), custom_call_target="tpu_custom_call" | custom-call | tf_op jit(solution)/shard_map/section_three_sums/pallas_call | solution.py:651
  52.6 4.3 %collective-permute-start.9 = (f32[25,8,512]{2,1,0:T(8,128)S(1)}, f32[25,8,512]{2,1,0:T(8,128)S(1)}, u32[]{:S(2)}, u32[]{:S(2)}) collective-permute-start(f32[25,8,512]{2,1,0:T(8,128)S(1)} %get-tuple-element.77), channel_id=1, source_target_pairs={{1,2},{3,4},{5,6},{7,8},{9,10},{11,12},{13,14},{15,16},{17,18},{19... | collective-permute-start | bytes 1228808 | tf_op jit(solution)/shard_map/ppermute | solution.py:570
  57.0 9.1 %collective-permute-done.9 = f32[25,8,512]{2,1,0:T(8,128)S(1)} collective-permute-done((f32[25,8,512]{2,1,0:T(8,128)S(1)}, f32[25,8,512]{2,1,0:T(8,128)S(1)}, u32[]{:S(2)}, u32[]{:S(2)}) %collective-permute-start.9) | collective-permute-done | bytes 409632 | tf_op jit(solution)/shard_map/ppermute | solution.py:570
  67.1 7.5 %biharmonic_inner_rows.1 = (f32[25,3,16,512]{3,2,1,0:T(8,128)S(1)}, f32[2,3,16,512]{3,2,1,0:T(8,128)S(1)}, f32[25,3,16,512]{3,2,1,0:T(8,128)S(1)}) custom-call(f32[27,3,8,512]{3,2,1,0:T(8,128)S(1)} %get-tuple-element.61.sums, f32[32,512]{1,0:T(8,128)S(1)} %get-tuple-element.62.edge, f32[25,8,512]{2,1,0:T(8,128)S(1)} %get-tuple-element.76.from_e, ...), custom_call_target="tpu_custom_call" | custom-call | flops 31457280 | bytes 16777216 | tf_op jit(solution)/shard_map/biharmonic_inner_rows/pallas_call | solution.py:694
  74.6 2.1 %collective-permute-done.11 = f32[7,40,512]{2,1,0:T(8,128)S(1)} collective-permute-done((f32[7,40,512]{2,1,0:T(8,128)S(1)}, f32[7,40,512]{2,1,0:T(8,128)S(1)}, u32[]{:S(2)}, u32[]{:S(2)}) %collective-permute-start.11) | collective-permute-done | bytes 573472 | tf_op jit(solution)/shard_map/ppermute | solution.py:569
  76.7 3.4 %collective-permute-done.10 = f32[7,40,512]{2,1,0:T(8,128)S(1)} collective-permute-done((f32[7,40,512]{2,1,0:T(8,128)S(1)}, f32[7,40,512]{2,1,0:T(8,128)S(1)}, u32[]{:S(2)}, u32[]{:S(2)}) %collective-permute-start.10) | collective-permute-done | bytes 573472 | tf_op jit(solution)/shard_map/ppermute | solution.py:570
  80.2 6.6 %biharmonic_outer_rows.1 = f32[64,16,512]{2,1,0:T(8,128)} custom-call(s32[16,64]{1,0:T(8,128)S(1)} %bitcast.12, f32[7,40,512]{2,1,0:T(8,128)S(1)} %get-tuple-element.72.from_n, f32[7,40,512]{2,1,0:T(8,128)S(1)} %get-tuple-element.71.from_s, f32[16,12,16,128]{3,2,1,0:T(8,128)S(1)} %get-tuple-element.67.j_ref, f32[37,3,16,128]{3,2,1,0:T(8,128)S(1)} %get-tuple-element.45.inv, ...), custom_call_target="tpu_custom_call" | custom-call | tf_op jit(solution)/shard_map/biharmonic_outer_rows/pallas_call | solution.py:705
  (49 shorter events, 3.5 us)
Async XLA Ops:
  0.0 0.7 copy-start.7
  0.7 0.7 copy-start.9
  8.4 15.6 %copy-start = (f32[16,8,8,512]{3,2,1,0:T(8,128)S(1)}, f32[16,8,8,512]{3,2,1,0:T(8,128)}, u32[]{:S(2)}) copy-start(f32[16,8,8,512]{3,2,1,0:T(8,128)} %get-tuple-element.46.t0) | copy-start | bytes 6291460
  8.4 9.0 %collective-permute-start = (f32[48,512]{1,0:T(8,128)}, f32[48,512]{1,0:T(8,128)}, u32[]{:S(2)}, u32[]{:S(2)}) collective-permute-start(f32[48,512]{1,0:T(8,128)} %get-tuple-element.40), channel_id=1, source_target_pairs={{0,1},{2,3},{4,5},{6,7},{8,9},{10,11},{12,13},{14,15},{16,17},{18,... | collective-permute-start | bytes 294920 | tf_op jit(solution)/shard_map/ppermute | solution.py:569
  8.5 11.5 %collective-permute-start.1 = (f32[48,512]{1,0:T(8,128)}, f32[48,512]{1,0:T(8,128)}, u32[]{:S(2)}, u32[]{:S(2)}) collective-permute-start(f32[48,512]{1,0:T(8,128)} %get-tuple-element.41), channel_id=1, source_target_pairs={{1,2},{3,4},{5,6},{7,8},{9,10},{11,12},{13,14},{15,16},{17,18},{19... | collective-permute-start | bytes 294920 | tf_op jit(solution)/shard_map/ppermute | solution.py:570
  21.1 8.7 %collective-permute-start.3 = (f32[48,512]{1,0:T(8,128)S(1)}, f32[48,512]{1,0:T(8,128)S(1)}, u32[]{:S(2)}, u32[]{:S(2)}) collective-permute-start(f32[48,512]{1,0:T(8,128)S(1)} %get-tuple-element.83), channel_id=1, source_target_pairs={{0,8},{1,9},{2,10},{3,11},{4,12},{5,13},{6,14},{7,15},{16,24},{17,... | collective-permute-start | bytes 294920 | tf_op jit(solution)/shard_map/ppermute | solution.py:569
  21.2 8.6 %collective-permute-start.2 = (f32[48,512]{1,0:T(8,128)S(1)}, f32[48,512]{1,0:T(8,128)S(1)}, u32[]{:S(2)}, u32[]{:S(2)}) collective-permute-start(f32[48,512]{1,0:T(8,128)S(1)} %get-tuple-element.84), channel_id=1, source_target_pairs={{8,16},{9,17},{10,18},{11,19},{12,20},{13,21},{14,22},{15,23},{24,... | collective-permute-start | bytes 294920 | tf_op jit(solution)/shard_map/ppermute | solution.py:570
  23.9 1.0 %copy-start.1 = (f32[16,8,8,128]{3,2,1,0:T(8,128)S(1)}, f32[16,8,8,128]{3,2,1,0:T(8,128)}, u32[]{:S(2)}) copy-start(f32[16,8,8,128]{3,2,1,0:T(8,128)} %get-tuple-element.49.rj_ref) | copy-start | bytes 1572868
  25.0 1.0 %copy-start.3 = (f32[16,8,8,128]{3,2,1,0:T(8,128)S(1)}, f32[16,8,8,128]{3,2,1,0:T(8,128)}, u32[]{:S(2)}) copy-start(f32[16,8,8,128]{3,2,1,0:T(8,128)} %get-tuple-element.50.j_ref) | copy-start | bytes 1572868
  26.0 1.3 %copy-start.5 = (f32[27,3,8,512]{3,2,1,0:T(8,128)S(1)}, f32[27,3,8,512]{3,2,1,0:T(8,128)}, u32[]{:S(2)}) copy-start(f32[27,3,8,512]{3,2,1,0:T(8,128)} %get-tuple-element.38.sums) | copy-start | bytes 3981316
  27.4 3.3 %copy-start.2 = (f32[16,8,8,128]{3,2,1,0:T(8,128)S(1)}, f32[16,8,8,128]{3,2,1,0:T(8,128)}, u32[]{:S(2)}) copy-start(f32[16,8,8,128]{3,2,1,0:T(8,128)} %get-tuple-element.49.rj_ref) | copy-start | bytes 1572868
  27.4 3.3 %copy-start.6 = (f32[27,3,8,512]{3,2,1,0:T(8,128)S(1)}, f32[27,3,8,512]{3,2,1,0:T(8,128)}, u32[]{:S(2)}) copy-start(f32[27,3,8,512]{3,2,1,0:T(8,128)} %get-tuple-element.38.sums) | copy-start | bytes 3981316
  30.7 12.7 %copy-start.4 = (f32[16,8,8,128]{3,2,1,0:T(8,128)S(1)}, f32[16,8,8,128]{3,2,1,0:T(8,128)}, u32[]{:S(2)}) copy-start(f32[16,8,8,128]{3,2,1,0:T(8,128)} %get-tuple-element.50.j_ref) | copy-start | bytes 1572868
  32.7 9.2 %collective-permute-start.5 = (f32[32,512]{1,0:T(8,128)S(1)}, f32[32,512]{1,0:T(8,128)S(1)}, u32[]{:S(2)}, u32[]{:S(2)}) collective-permute-start(f32[32,512]{1,0:T(8,128)S(1)} %get-tuple-element.93), channel_id=1, source_target_pairs={{1,2},{3,4},{5,6},{7,8},{9,10},{11,12},{13,14},{15,16},{17,18},{19... | collective-permute-start | bytes 196616 | tf_op jit(solution)/shard_map/ppermute | solution.py:570
  38.1 3.7 %collective-permute-start.4 = (f32[32,512]{1,0:T(8,128)S(1)}, f32[32,512]{1,0:T(8,128)S(1)}, u32[]{:S(2)}, u32[]{:S(2)}) collective-permute-start(f32[32,512]{1,0:T(8,128)S(1)} %get-tuple-element.94), channel_id=1, source_target_pairs={{0,1},{2,3},{4,5},{6,7},{8,9},{10,11},{12,13},{14,15},{16,17},{18,... | collective-permute-start | bytes 196616 | tf_op jit(solution)/shard_map/ppermute | solution.py:569
  42.0 4.3 %collective-permute-start.7 = (f32[32,512]{1,0:T(8,128)S(1)}, f32[32,512]{1,0:T(8,128)S(1)}, u32[]{:S(2)}, u32[]{:S(2)}) collective-permute-start(f32[32,512]{1,0:T(8,128)S(1)} %get-tuple-element.87), channel_id=1, source_target_pairs={{0,8},{1,9},{2,10},{3,11},{4,12},{5,13},{6,14},{7,15},{16,24},{17,... | collective-permute-start | bytes 196616 | tf_op jit(solution)/shard_map/ppermute | solution.py:569
  42.1 7.7 %collective-permute-start.6 = (f32[32,512]{1,0:T(8,128)S(1)}, f32[32,512]{1,0:T(8,128)S(1)}, u32[]{:S(2)}, u32[]{:S(2)}) collective-permute-start(f32[32,512]{1,0:T(8,128)S(1)} %get-tuple-element.88), channel_id=1, source_target_pairs={{8,16},{9,17},{10,18},{11,19},{12,20},{13,21},{14,22},{15,23},{24,... | collective-permute-start | bytes 196616 | tf_op jit(solution)/shard_map/ppermute | solution.py:570
  52.6 13.4 %collective-permute-start.9 = (f32[25,8,512]{2,1,0:T(8,128)S(1)}, f32[25,8,512]{2,1,0:T(8,128)S(1)}, u32[]{:S(2)}, u32[]{:S(2)}) collective-permute-start(f32[25,8,512]{2,1,0:T(8,128)S(1)} %get-tuple-element.77), channel_id=1, source_target_pairs={{1,2},{3,4},{5,6},{7,8},{9,10},{11,12},{13,14},{15,16},{17,18},{19... | collective-permute-start | bytes 1228808 | tf_op jit(solution)/shard_map/ppermute | solution.py:570
  57.0 9.1 %collective-permute-start.8 = (f32[25,8,512]{2,1,0:T(8,128)S(1)}, f32[25,8,512]{2,1,0:T(8,128)S(1)}, u32[]{:S(2)}, u32[]{:S(2)}) collective-permute-start(f32[25,8,512]{2,1,0:T(8,128)S(1)} %get-tuple-element.78), channel_id=1, source_target_pairs={{0,1},{2,3},{4,5},{6,7},{8,9},{10,11},{12,13},{14,15},{16,17},{18,... | collective-permute-start | bytes 1228808 | tf_op jit(solution)/shard_map/ppermute | solution.py:569
  66.9 9.8 %collective-permute-start.11 = (f32[7,40,512]{2,1,0:T(8,128)S(1)}, f32[7,40,512]{2,1,0:T(8,128)S(1)}, u32[]{:S(2)}, u32[]{:S(2)}) collective-permute-start(f32[7,40,512]{2,1,0:T(8,128)S(1)} %get-tuple-element.73), channel_id=1, source_target_pairs={{0,8},{1,9},{2,10},{3,11},{4,12},{5,13},{6,14},{7,15},{16,24},{17,... | collective-permute-start | bytes 1720328 | tf_op jit(solution)/shard_map/ppermute | solution.py:569
  67.0 13.1 %collective-permute-start.10 = (f32[7,40,512]{2,1,0:T(8,128)S(1)}, f32[7,40,512]{2,1,0:T(8,128)S(1)}, u32[]{:S(2)}, u32[]{:S(2)}) collective-permute-start(f32[7,40,512]{2,1,0:T(8,128)S(1)} %get-tuple-element.74), channel_id=1, source_target_pairs={{8,16},{9,17},{10,18},{11,19},{12,20},{13,21},{14,22},{15,23},{24,... | collective-permute-start | bytes 1720328 | tf_op jit(solution)/shard_map/ppermute | solution.py:570
  74.6 5.6 %copy-start.8 = (s32[64,16]{0,1:T(8,128)S(1)}, s32[64,16]{0,1:T(8,128)}, u32[]{:S(2)}) copy-start(s32[64,16]{0,1:T(8,128)} %param.7) | copy-start | bytes 12292
